TPU v7x, 32 devices: a whole 2x2x4 slice. The times are simulated.
32 devices in a mesh: dp: 16 (over z, y, x), tensor: 2 (over core).
Axes of the slice: x: 2, y: 2, z: 4, core: 2. Of those that a mesh axis runs over, the one named last changes fastest.
Arguments:
- source_ids: int32 [16, 512], P('dp', 'tensor'), may hold values from 0 to 50303
- target_ids: int32 [16, 512], P('dp', 'tensor'), may hold values from 0 to 50303
- score_places: int32 [16, 64], P('dp', 'tensor'), may hold values from 0 to 511
- target_labels: int32 [16, 64], P('dp', 'tensor'), may hold values from 0 to 50303
- source_lengths: int32 [16], P('dp'), may hold values from 1 to 512, 4608 in all
- target_lengths: int32 [16], P('dp'), may hold values from 1 to 512, 4608 in all
- pair_order: int32 [16], replicated, may hold values from 0 to 15, each once
- step_count: int32 [1], replicated, may hold values from 1 to 20
- entry_weight: float32 [3, 3, 768, 768], P(None, None, 'dp', 'tensor'), may hold values from -0.21875 to 0.21875
- entry_first: float32 [3, 3, 768, 768], P(None, None, 'dp', 'tensor'), may hold values from -1.9073486e-06 to 1.9073486e-06
- entry_second: float32 [3, 3, 768, 768], P(None, None, 'dp', 'tensor'), may hold values from 8.938092e-16 to 1.4300947e-14
- exit_weight: float32 [3, 768, 768], P(None, 'tensor', 'dp'), may hold values from -0.875 to 0.875
- exit_first: float32 [3, 768, 768], P(None, 'tensor', 'dp'), may hold values from -1.9073486e-06 to 1.9073486e-06
- exit_second: float32 [3, 768, 768], P(None, 'tensor', 'dp'), may hold values from 8.938092e-16 to 1.4300947e-14
- expand_weight: float32 [2, 768, 3072], P(None, 'dp', 'tensor'), may hold values from -0.21875 to 0.21875
- expand_first: float32 [2, 768, 3072], P(None, 'dp', 'tensor'), may hold values from -1.9073486e-06 to 1.9073486e-06
- expand_second: float32 [2, 768, 3072], P(None, 'dp', 'tensor'), may hold values from 8.938092e-16 to 1.4300947e-14
- reduce_weight: float32 [2, 3072, 768], P(None, 'tensor', 'dp'), may hold values from -0.109375 to 0.109375
- reduce_first: float32 [2, 3072, 768], P(None, 'tensor', 'dp'), may hold values from -1.9073486e-06 to 1.9073486e-06
- reduce_second: float32 [2, 3072, 768], P(None, 'tensor', 'dp'), may hold values from 8.938092e-16 to 1.4300947e-14
- norm_gains: float32 [7, 768], replicated, may hold values from 0.5 to 1.5
- gains_first: float32 [7, 768], replicated, may hold values from -2.2888184e-05 to 2.2888184e-05
- gains_second: float32 [7, 768], replicated, may hold values from 8.9380916e-14 to 1.4300946e-12
- token_table: float32 [50304, 768], P(('dp', 'tensor')), may hold values from -1 to 1
- table_first: float32 [50304, 768], P(('dp', 'tensor')), may hold values from -1.9073486e-06 to 1.9073486e-06
- table_second: float32 [50304, 768], P(('dp', 'tensor')), may hold values from 8.938092e-16 to 1.4300947e-14
- place_table: float32 [2, 512, 768], P(None, 'tensor', 'dp'), may hold values from -1 to 1
- place_first: float32 [2, 512, 768], P(None, 'tensor', 'dp'), may hold values from -1.9073486e-06 to 1.9073486e-06
- place_second: float32 [2, 512, 768], P(None, 'tensor', 'dp'), may hold values from 8.938092e-16 to 1.4300947e-14
Outputs:
- mean_loss: float32 [], replicated
- gradient_norm: float32 [], replicated
- pair_losses: float32 [16, 64], P('dp', 'tensor')
- entry_new: float32 [3, 3, 768, 768], P(None, None, 'dp', 'tensor')
- entry_first_new: float32 [3, 3, 768, 768], P(None, None, 'dp', 'tensor')
- entry_second_new: float32 [3, 3, 768, 768], P(None, None, 'dp', 'tensor')
- exit_new: float32 [3, 768, 768], P(None, 'tensor', 'dp')
- exit_first_new: float32 [3, 768, 768], P(None, 'tensor', 'dp')
- exit_second_new: float32 [3, 768, 768], P(None, 'tensor', 'dp')
- expand_new: float32 [2, 768, 3072], P(None, 'dp', 'tensor')
- expand_first_new: float32 [2, 768, 3072], P(None, 'dp', 'tensor')
- expand_second_new: float32 [2, 768, 3072], P(None, 'dp', 'tensor')
- reduce_new: float32 [2, 3072, 768], P(None, 'tensor', 'dp')
- reduce_first_new: float32 [2, 3072, 768], P(None, 'tensor', 'dp')
- reduce_second_new: float32 [2, 3072, 768], P(None, 'tensor', 'dp')
- gains_new: float32 [7, 768], replicated
- gains_first_new: float32 [7, 768], replicated
- gains_second_new: float32 [7, 768], replicated
- table_new: float32 [50304, 768], P(('dp', 'tensor'))
- table_first_new: float32 [50304, 768], P(('dp', 'tensor'))
- table_second_new: float32 [50304, 768], P(('dp', 'tensor'))
- place_new: float32 [2, 512, 768], P(None, 'tensor', 'dp')
- place_first_new: float32 [2, 512, 768], P(None, 'tensor', 'dp')
- place_second_new: float32 [2, 512, 768], P(None, 'tensor', 'dp')
Inputs may be any that keep to these rules, and one draw needn't show every extreme that they name: `score_places`: places may repeat; a place counts only where it is below its pair's target length. `source_lengths`: some pair has exactly 512. `target_lengths`: some pair has exactly 512. `pair_order`: each data group index once.
All inputs are finite; a program needn't handle non-finite values. No bound on the sum of `source_lengths` or of `target_lengths` on one device may be relied on, other than what follows from the above.
Results may differ from a plain program's by a relative error of at most 0.012.
The roundings to bfloat16 on the way count: a program that leaves them out, or rounds other values in their place, can miss the bound.
Values may be sent and summed in bfloat16 or wider, within the bound.
No kernel may reach another device: no remote copies, remote signals or barrier semaphores. Data moves between devices by JAX's collectives and lax.ppermute only.
A program may use at most 384 MiB of HBM per device.

v0:
```python
import jax
import jax.numpy as jnp
from jax import lax
from jax.sharding import PartitionSpec as P

HEAD_DIM = 64


MAX_NORM = 0.01
LEARN_RATE = 0.03
GAIN_RATE = 0.3
FIRST_DECAY = 0.9
SECOND_DECAY = 0.999
ADAM_EPSILON = 1e-08
WEIGHT_DECAY = 0.01
SCORE_FLOOR = -1000000000.0


def merged(part, axis, combine):
    gathered = jax.tree.map(lambda a: lax.all_gather(a, axis), part)

    def take(source):
        return jax.tree.map(lambda a: lax.dynamic_index_in_dim(a, source, 0, False), gathered)

    return lax.fori_loop(
        1, lax.axis_size(axis), lambda source, state: combine(state, take(source)), take(0)
    )


def norm_rows(values, gain):
    centered = values - jnp.mean(values, axis=-1, keepdims=True)
    variance = jnp.mean(centered * centered, axis=-1, keepdims=True)
    return centered * lax.rsqrt(variance + 1e-05) * gain


def spread(rows):
    return lax.all_gather(rows, "tensor", axis=0, tiled=True)


def collect(partial_rows):
    return lax.psum_scatter(partial_rows, "tensor", scatter_dimension=0, tiled=True)


def product(left, right):
    return jnp.dot(left, right, preferred_element_type=jnp.float32)


def product_tn(left, right):
    return lax.dot_general(
        left, right, (((0,), (0,)), ((), ())), preferred_element_type=jnp.float32
    )


def product_nt(left, right):
    return lax.dot_general(
        left, right, (((1,), (1,)), ((), ())), preferred_element_type=jnp.float32
    )


def heads_of(values):
    return values.reshape(values.shape[0], values.shape[1] // HEAD_DIM, HEAD_DIM)


def block_rows(values):
    length = values.shape[0]
    block = min(512, length)
    return values.reshape((length // block, block) + values.shape[1:])


def scores_for(query_block, key_heads, first_row, allowed):
    block = query_block.shape[0]
    raw_scores = jnp.einsum(
        "qhd,khd->hqk", query_block, key_heads, preferred_element_type=jnp.float32
    )
    mask = allowed(first_row + jnp.arange(block), jnp.arange(key_heads.shape[0]))
    return jnp.where(mask[None], raw_scores * HEAD_DIM ** (-0.5), SCORE_FLOOR)


def attend_forward(query, key, value, allowed):
    length = query.shape[0]
    query_blocks = block_rows(heads_of(query))
    key_heads = heads_of(key)
    value_heads = heads_of(value)
    firsts = jnp.arange(query_blocks.shape[0]) * query_blocks.shape[1]

    def one_block(pieces):
        query_block, first_row = pieces
        scores = scores_for(query_block, key_heads, first_row, allowed)
        highest = jnp.max(scores, axis=-1, keepdims=True)
        log_total = highest + jnp.log(jnp.sum(jnp.exp(scores - highest), axis=-1, keepdims=True))
        weights = jnp.exp(scores - log_total).astype(jnp.bfloat16)
        mixed = jnp.einsum("hqk,khd->qhd", weights, value_heads, preferred_element_type=jnp.float32)
        return (mixed.astype(jnp.bfloat16), log_total)

    mixed, log_totals = lax.map(one_block, (query_blocks, firsts))
    return (mixed.reshape(length, -1), log_totals)


def attend_backward(query, key, value, log_totals, grad_mixed, allowed):
    length = query.shape[0]
    query_blocks = block_rows(heads_of(query))
    grad_blocks = block_rows(heads_of(grad_mixed))
    key_heads = heads_of(key)
    value_heads = heads_of(value)
    firsts = jnp.arange(query_blocks.shape[0]) * query_blocks.shape[1]

    def one_block(carry, pieces):
        grad_key, grad_value = carry
        query_block, grad_block, log_total, first_row = pieces
        scores = scores_for(query_block, key_heads, first_row, allowed)
        weights = jnp.exp(scores - log_total)
        grad_value = grad_value + jnp.einsum(
            "hqk,qhd->khd",
            weights.astype(jnp.bfloat16),
            grad_block,
            preferred_element_type=jnp.float32,
        )
        grad_weights = jnp.einsum(
            "qhd,khd->hqk", grad_block, value_heads, preferred_element_type=jnp.float32
        )
        inner = jnp.sum(weights * grad_weights, axis=-1, keepdims=True)
        grad_scores = (weights * (grad_weights - inner) * HEAD_DIM ** (-0.5)).astype(jnp.bfloat16)
        grad_query = jnp.einsum(
            "hqk,khd->qhd", grad_scores, key_heads, preferred_element_type=jnp.float32
        )
        grad_key = grad_key + jnp.einsum(
            "hqk,qhd->khd", grad_scores, query_block, preferred_element_type=jnp.float32
        )
        return ((grad_key, grad_value), grad_query)

    zeros = jnp.zeros(key_heads.shape, jnp.float32)
    (grad_key, grad_value), grad_query = lax.scan(
        one_block, (zeros, zeros), (query_blocks, grad_blocks, log_totals, firsts)
    )
    keys = key.shape[0]
    return (
        grad_query.reshape(length, -1).astype(jnp.bfloat16),
        grad_key.reshape(keys, -1).astype(jnp.bfloat16),
        grad_value.reshape(keys, -1).astype(jnp.bfloat16),
    )


def attention_forward(stream, gain, entry, leave, allowed, memory):
    gathered = spread(norm_rows(stream, gain).astype(jnp.bfloat16))
    source = gathered if memory is None else memory
    query = product(gathered, entry[0]).astype(jnp.bfloat16)
    key = product(source, entry[1]).astype(jnp.bfloat16)
    value = product(source, entry[2]).astype(jnp.bfloat16)
    mixed, log_totals = attend_forward(query, key, value, allowed)
    output = collect(product(mixed, leave))
    return (output, (stream, gathered, query, key, value, mixed, log_totals))


def attention_backward(grad_out, gain, entry, leave, allowed, memory, saved):
    stream, gathered, query, key, value, mixed, log_totals = saved
    grad_rows = spread(grad_out.astype(jnp.bfloat16))
    grad_leave = product_tn(mixed, grad_rows)
    grad_mixed = product_nt(grad_rows, leave).astype(jnp.bfloat16)
    grad_query, grad_key, grad_value = attend_backward(
        query, key, value, log_totals, grad_mixed, allowed
    )
    source = gathered if memory is None else memory
    grad_entry = jnp.stack(
        [
            product_tn(gathered, grad_query),
            product_tn(source, grad_key),
            product_tn(source, grad_value),
        ]
    )
    back_query = product_nt(grad_query, entry[0])
    back_source = product_nt(grad_key, entry[1]) + product_nt(grad_value, entry[2])
    if memory is None:
        grad_normed = collect(back_query + back_source)
        grad_memory = None
    else:
        grad_normed = collect(back_query)
        grad_memory = collect(back_source)
    grad_stream, grad_gain = jax.vjp(norm_rows, stream, gain)[1](grad_normed)
    return (grad_stream + grad_out, grad_gain, grad_entry, grad_leave, grad_memory)


def gelu_exact(values):
    return jax.nn.gelu(values, approximate=False)


def feed_forward(stream, gain, expand, shrink):
    gathered = spread(norm_rows(stream, gain).astype(jnp.bfloat16))
    inner = product(gathered, expand)
    hidden = gelu_exact(inner).astype(jnp.bfloat16)
    output = collect(product(hidden, shrink))
    return (output, (stream, gathered, inner, hidden))


def feed_backward(grad_out, gain, expand, shrink, saved):
    stream, gathered, inner, hidden = saved
    grad_rows = spread(grad_out.astype(jnp.bfloat16))
    grad_shrink = product_tn(hidden, grad_rows)
    grad_hidden = product_nt(grad_rows, shrink).astype(jnp.bfloat16)
    grad_inner = jax.vjp(gelu_exact, inner)[1](grad_hidden.astype(jnp.float32))[0].astype(
        jnp.bfloat16
    )
    grad_expand = product_tn(gathered, grad_inner)
    grad_normed = collect(product_nt(grad_inner, expand))
    grad_stream, grad_gain = jax.vjp(norm_rows, stream, gain)[1](grad_normed)
    return (grad_stream + grad_out, grad_gain, grad_expand, grad_shrink)


def combine(first, second):
    highest = jnp.maximum(first[0], second[0])
    return (
        highest,
        first[1] * jnp.exp(first[0] - highest) + second[1] * jnp.exp(second[0] - highest),
        first[2] + second[2],
    )


def adam_step(master, first, second, grad, clip, fix_one, fix_two, rate):
    grad = grad * clip
    first_new = FIRST_DECAY * first + (1 - FIRST_DECAY) * grad
    second_new = SECOND_DECAY * second + (1 - SECOND_DECAY) * grad * grad
    master_new = master - rate * (
        first_new / fix_one / (jnp.sqrt(second_new / fix_two) + ADAM_EPSILON)
        + WEIGHT_DECAY * master
    )
    return (master_new, first_new, second_new)


def local(
    source_ids,
    target_ids,
    score_places,
    target_labels,
    source_lengths,
    target_lengths,
    pair_order,
    step_count,
    entry_weight,
    entry_first,
    entry_second,
    exit_weight,
    exit_first,
    exit_second,
    expand_weight,
    expand_first,
    expand_second,
    reduce_weight,
    reduce_first,
    reduce_second,
    norm_gains,
    gains_first,
    gains_second,
    token_table,
    table_first,
    table_second,
    place_table,
    place_first,
    place_second,
):
    groups = lax.axis_size("dp")
    parts = lax.axis_size("tensor")
    group = lax.axis_index("dp")
    part = lax.axis_index("tensor")
    every = (
        lax.all_gather(source_ids, ("dp", "tensor"), axis=0, tiled=True),
        lax.all_gather(target_ids, ("dp", "tensor"), axis=0, tiled=True),
        lax.all_gather(score_places, ("dp", "tensor"), axis=0, tiled=True),
        lax.all_gather(target_labels, ("dp", "tensor"), axis=0, tiled=True),
        lax.all_gather(source_lengths, ("dp", "tensor"), axis=0, tiled=True),
        lax.all_gather(target_lengths, ("dp", "tensor"), axis=0, tiled=True),
    )
    source_all = every[0].reshape(groups, -1)
    target_all = every[1].reshape(groups, -1)
    places_all = every[2].reshape(groups, -1)
    labels_all = every[3].reshape(groups, -1)
    source_lens = every[4].reshape(groups, parts)[:, 0]
    target_lens = every[5].reshape(groups, parts)[:, 0]
    chosen = (pair_order == group).astype(jnp.int32)

    def pick(values):
        return jnp.sum(values * chosen.reshape((groups,) + (1,) * (values.ndim - 1)), axis=0)

    source = pick(source_all)
    target = pick(target_all)
    spots = pick(places_all)
    labels = pick(labels_all)
    source_len = pick(source_lens)
    target_len = pick(target_lens)
    length = source.shape[0]
    count = jnp.sum((places_all < target_lens[:, None]).astype(jnp.float32))
    entry, leave, expand, shrink, places = (
        lax.all_gather(entry_weight.astype(jnp.bfloat16), "dp", axis=2, tiled=True),
        lax.all_gather(exit_weight.astype(jnp.bfloat16), "dp", axis=2, tiled=True),
        lax.all_gather(expand_weight.astype(jnp.bfloat16), "dp", axis=1, tiled=True),
        lax.all_gather(reduce_weight.astype(jnp.bfloat16), "dp", axis=2, tiled=True),
        lax.all_gather(place_table.astype(jnp.bfloat16), "dp", axis=2, tiled=True),
    )
    table = lax.all_gather(token_table.astype(jnp.bfloat16), "dp", axis=0, tiled=True)
    rows_owned = token_table.shape[0]
    table_rows_here = table.shape[0]

    def locate(ids):
        block = ids // rows_owned
        return (block // parts * rows_owned + ids % rows_owned, block % parts == part)

    arranged = jnp.stack([source, target]).reshape(2, parts, -1).transpose(1, 0, 2)
    where_row, inside = locate(arranged)
    looked = jnp.take(table, where_row, axis=0).astype(jnp.float32) * inside[..., None].astype(
        jnp.float32
    )
    start = collect(looked)[0] + places.astype(jnp.float32)

    def encoder_mask(query_places, key_places):
        return jnp.broadcast_to(
            key_places[None, :] < source_len, (query_places.shape[0], key_places.shape[0])
        )

    def decoder_mask(query_places, key_places):
        return (key_places[None, :] <= query_places[:, None]) & (key_places[None, :] < target_len)

    stream = start[0]
    output, enc_attend = attention_forward(
        stream, norm_gains[0], entry[0], leave[0], encoder_mask, None
    )
    stream = stream + output
    output, enc_feed = feed_forward(stream, norm_gains[1], expand[0], shrink[0])
    stream = stream + output
    memory = spread(norm_rows(stream, norm_gains[2]).astype(jnp.bfloat16))
    decoded = start[1]
    output, dec_self = attention_forward(
        decoded, norm_gains[3], entry[1], leave[1], decoder_mask, None
    )
    decoded = decoded + output
    output, dec_cross = attention_forward(
        decoded, norm_gains[4], entry[2], leave[2], encoder_mask, memory
    )
    decoded = decoded + output
    output, dec_feed = feed_forward(decoded, norm_gains[5], expand[1], shrink[1])
    decoded = decoded + output
    final = spread(norm_rows(decoded, norm_gains[6]).astype(jnp.bfloat16))
    picked = jnp.take(final, spots, axis=0)
    width = picked.shape[1]
    valid = (spots < target_len).astype(jnp.float32)
    share = picked.shape[0] // parts
    label_row, label_in = locate(labels)
    span = min(128, picked.shape[0])

    def head_part(pieces):
        rows_span, row_span, in_span = pieces
        logits = product_nt(rows_span, table)
        highest = jnp.max(logits, axis=-1)
        totals = jnp.sum(jnp.exp(logits - highest[:, None]), axis=-1)
        golden = jnp.take_along_axis(logits, row_span[:, None], axis=1)[:, 0] * in_span
        return (highest, totals, golden)

    highs, totals, goldens = lax.map(
        head_part,
        (
            picked.reshape(-1, span, width),
            label_row.reshape(-1, span),
            label_in.reshape(-1, span).astype(jnp.float32),
        ),
    )
    highest, total, golden = merged(
        (highs.reshape(-1), totals.reshape(-1), goldens.reshape(-1)), "tensor", combine
    )
    log_total = highest + jnp.log(total)
    losses = (log_total - golden) * valid
    logits = product_nt(picked, table)
    probs = jnp.exp(logits - log_total[:, None])
    onehot = (
        (jnp.arange(logits.shape[1])[None, :] == label_row[:, None]) & label_in[:, None]
    ).astype(jnp.float32)
    grad_logits = ((probs - onehot) * (valid / count)[:, None]).astype(jnp.bfloat16)
    grad_picked = product(grad_logits, table)
    grad_table = product_tn(grad_logits, picked)
    grad_final = collect(jax.ops.segment_sum(grad_picked, spots, num_segments=length))
    pair_losses = lax.dynamic_slice_in_dim(losses, part * share, share)[None]
    grad_decoded, gain_six = jax.vjp(norm_rows, decoded, norm_gains[6])[1](grad_final)
    grad_decoded, gain_five, expand_one, shrink_one = feed_backward(
        grad_decoded, norm_gains[5], expand[1], shrink[1], dec_feed
    )
    grad_decoded, gain_four, entry_two, leave_two, grad_memory = attention_backward(
        grad_decoded, norm_gains[4], entry[2], leave[2], encoder_mask, memory, dec_cross
    )
    grad_decoded, gain_three, entry_one, leave_one, unused_one = attention_backward(
        grad_decoded, norm_gains[3], entry[1], leave[1], decoder_mask, None, dec_self
    )
    grad_stream, gain_two = jax.vjp(norm_rows, stream, norm_gains[2])[1](grad_memory)
    grad_stream, gain_one, expand_zero, shrink_zero = feed_backward(
        grad_stream, norm_gains[1], expand[0], shrink[0], enc_feed
    )
    grad_stream, gain_zero, entry_zero, leave_zero, unused_zero = attention_backward(
        grad_stream, norm_gains[0], entry[0], leave[0], encoder_mask, None, enc_attend
    )
    grad_start = jnp.stack([grad_stream, grad_decoded]).astype(jnp.bfloat16)
    grad_rows_all = spread(grad_start[None])
    segment_ids = jnp.where(inside, where_row, table_rows_here).reshape(-1)
    grad_table = grad_table + jax.ops.segment_sum(
        grad_rows_all.reshape(-1, width).astype(jnp.float32),
        segment_ids,
        num_segments=table_rows_here,
    )
    table_grad = lax.psum_scatter(grad_table, "dp", scatter_dimension=0, tiled=True)
    entry_grad, leave_grad, expand_grad, shrink_grad, place_grad = (
        lax.psum_scatter(
            jnp.stack([entry_zero, entry_one, entry_two]), "dp", scatter_dimension=2, tiled=True
        ),
        lax.psum_scatter(
            jnp.stack([leave_zero, leave_one, leave_two]), "dp", scatter_dimension=2, tiled=True
        ),
        lax.psum_scatter(
            jnp.stack([expand_zero, expand_one]), "dp", scatter_dimension=1, tiled=True
        ),
        lax.psum_scatter(
            jnp.stack([shrink_zero, shrink_one]), "dp", scatter_dimension=2, tiled=True
        ),
        lax.psum_scatter(grad_start.astype(jnp.float32), "dp", scatter_dimension=2, tiled=True),
    )
    gain_partial = jnp.stack(
        [gain_zero, gain_one, gain_two, gain_three, gain_four, gain_five, gain_six]
    )
    owned = (entry_grad, leave_grad, expand_grad, shrink_grad, table_grad, place_grad)
    squares = jnp.zeros((), jnp.float32)
    for grad in owned:
        squares = squares + jnp.sum(grad * grad)
    loss_part = jnp.sum(losses) / count * (part == 0).astype(jnp.float32)
    gain_grad, square_total, mean_loss = lax.psum(
        (gain_partial, squares, loss_part), ("dp", "tensor")
    )
    gradient_norm = jnp.sqrt(square_total + jnp.sum(gain_grad * gain_grad))
    clip = jnp.minimum(1.0, MAX_NORM / (gradient_norm + 1e-06))
    steps = step_count[0].astype(jnp.float32)
    fix_one = 1 - FIRST_DECAY**steps
    fix_two = 1 - SECOND_DECAY**steps
    masters = (
        entry_weight,
        exit_weight,
        expand_weight,
        reduce_weight,
        norm_gains,
        token_table,
        place_table,
    )
    firsts = (
        entry_first,
        exit_first,
        expand_first,
        reduce_first,
        gains_first,
        table_first,
        place_first,
    )
    seconds = (
        entry_second,
        exit_second,
        expand_second,
        reduce_second,
        gains_second,
        table_second,
        place_second,
    )
    grads = (entry_grad, leave_grad, expand_grad, shrink_grad, gain_grad, table_grad, place_grad)
    rates = (LEARN_RATE, LEARN_RATE, LEARN_RATE, LEARN_RATE, GAIN_RATE, LEARN_RATE, LEARN_RATE)
    results = [mean_loss, gradient_norm, pair_losses]
    for master, first, second, grad, rate in zip(masters, firsts, seconds, grads, rates):
        results.extend(adam_step(master, first, second, grad, clip, fix_one, fix_two, rate))
    return tuple(results)


def solution(mesh):
    return jax.shard_map(
        local,
        mesh=mesh,
        in_specs=(
            P("dp", "tensor"),
            P("dp", "tensor"),
            P("dp", "tensor"),
            P("dp", "tensor"),
            P("dp"),
            P("dp"),
            P(),
            P(),
            P(None, None, "dp", "tensor"),
            P(None, None, "dp", "tensor"),
            P(None, None, "dp", "tensor"),
            P(None, "tensor", "dp"),
            P(None, "tensor", "dp"),
            P(None, "tensor", "dp"),
            P(None, "dp", "tensor"),
            P(None, "dp", "tensor"),
            P(None, "dp", "tensor"),
            P(None, "tensor", "dp"),
            P(None, "tensor", "dp"),
            P(None, "tensor", "dp"),
            P(),
            P(),
            P(),
            P(("dp", "tensor"), None),
            P(("dp", "tensor"), None),
            P(("dp", "tensor"), None),
            P(None, "tensor", "dp"),
            P(None, "tensor", "dp"),
            P(None, "tensor", "dp"),
        ),
        out_specs=(
            P(),
            P(),
            P("dp", "tensor"),
            P(None, None, "dp", "tensor"),
            P(None, None, "dp", "tensor"),
            P(None, None, "dp", "tensor"),
            P(None, "tensor", "dp"),
            P(None, "tensor", "dp"),
            P(None, "tensor", "dp"),
            P(None, "dp", "tensor"),
            P(None, "dp", "tensor"),
            P(None, "dp", "tensor"),
            P(None, "tensor", "dp"),
            P(None, "tensor", "dp"),
            P(None, "tensor", "dp"),
            P(),
            P(),
            P(),
            P(("dp", "tensor"), None),
            P(("dp", "tensor"), None),
            P(("dp", "tensor"), None),
            P(None, "tensor", "dp"),
            P(None, "tensor", "dp"),
            P(None, "tensor", "dp"),
        ),
        check_vma=False,
    )
```

profile of v0, /device:TPU:0, one launch (start us, length us, event | category | flops | bytes accessed | tf_op | source)
XLA Modules:
  0.0 3424.4 jit_solution(17820380808416291645)
XLA Ops:
  11.4 43.9 %all-gather.3 = s32[32,1,256]{2,1,0:T(1,128)S(1)} all-gather(s32[1,1,256]{2,1,0:T(1,128)S(1)} %bitcast.451), channel_id=1, replica_groups=mesh['dp'=16,'tensor'=2] {'dp','tensor'}, dimensions={0}, use_global_device_ids=true | all-gather | bytes 33792 | tf_op jit(solution)/shard_map/all_gather | solution.py:264
  55.4 37.1 %all-gather.4 = s32[32,1,256]{2,1,0:T(1,128)S(1)} all-gather(s32[1,1,256]{2,1,0:T(1,128)S(1)} %bitcast.452), channel_id=1, replica_groups=mesh['dp'=16,'tensor'=2] {'dp','tensor'}, dimensions={0}, use_global_device_ids=true | all-gather | bytes 33792 | tf_op jit(solution)/shard_map/all_gather | solution.py:265
  93.8 320.3 %all-gather.25.cloned.1.call-done = bf16[16,1572,768]{2,1,0:T(8,128)(2,1)} async-done(((bf16[1,1572,768]{2,1,0:T(8,128)(2,1)}), bf16[16,1572,768]{2,1,0:T(8,128)(2,1)}) %all-gather.25.cloned.1.call-update) | async-done | bytes 38633488 | tf_op jit(solution)/shard_map/all_gather | solution.py:297
  414.2 44.0 %reshape.986 = bf16[25152,768]{1,0:T(8,128)(2,1)} reshape(bf16[16,1572,768]{2,1,0:T(8,128)(2,1)} %all-gather.25.cloned.1.call-done) | data formatting | bytes 77266944
  458.1 15.4 gather_fusion
  478.9 38.3 %all-reduce.9 = (s32[32]{0:T(128)S(1)}, s32[32]{0:T(128)S(1)}) all-reduce(s32[32]{0:T(128)S(1)} %dynamic-update-slice.1, s32[32]{0:T(128)S(1)} %dynamic-update-slice), channel_id=1, replica_groups=mesh['dp'=16,'tensor'=2] {'dp','tensor'}, use_global_device_ids=true, to_apply=%add.1 | all-reduce | flops 64 | bytes 512
  519.7 49.6 %all_gather.89 = bf16[2,256,768]{1,0,2:T(2,128)(2,1)S(1)} all-gather(bf16[2,256,48]{1,0,2:T(2,128)(2,1)S(1)} %copy.285), channel_id=1, replica_groups=mesh['dp'=16,'tensor'=2] {'dp'}, dimensions={2}, use_global_device_ids=true | all-gather | bytes 835584 | tf_op jit(solution)/shard_map/all_gather | solution.py:295
  574.9 9.5 all-gather.15.cloned.1.call-done
  596.6 48.6 %all-gather.17.cloned.1.call-done = bf16[3,384,768]{1,2,0:T(8,128)(2,1)} async-done(((bf16[3,384,48]{1,2,0:T(8,128)(2,1)}), bf16[3,384,768]{1,2,0:T(8,128)(2,1)}) %all-gather.17.cloned.1.call-update) | async-done | bytes 1769488 | tf_op jit(solution)/shard_map/all_gather | solution.py:292
  650.6 5.4 reduce-scatter.22.cloned.1.call-done
  676.9 64.0 %all-gather.19.cloned.1.call-done = bf16[2,768,1536]{2,1,0:T(8,128)(2,1)} async-done(((bf16[2,48,1536]{2,1,0:T(8,128)(2,1)}), bf16[2,768,1536]{2,1,0:T(8,128)(2,1)}) %all-gather.19.cloned.1.call-update) | async-done | bytes 4718608 | tf_op jit(solution)/shard_map/all_gather | solution.py:293
  740.9 10.8 multiply_convert_fusion.5
  751.7 71.6 %all-gather.21.cloned.1.call-done = bf16[2,1536,768]{1,2,0:T(8,128)(2,1)} async-done(((bf16[2,1536,48]{1,2,0:T(8,128)(2,1)}), bf16[2,1536,768]{1,2,0:T(8,128)(2,1)}) %all-gather.21.cloned.1.call-update) | async-done | bytes 4718608 | tf_op jit(solution)/shard_map/all_gather | solution.py:294
  823.3 4.7 fusion.115
  828.1 5.7 reduce-scatter.20.cloned.1.call-done
  838.6 7.9 reduce-scatter.24.cloned.1.call-done
  866.5 10.4 reduce-scatter.26.cloned.1.call-done
  882.0 10.8 multiply_convert_fusion.4
  899.4 43.6 %all-gather.2 = s32[32,1,32]{2,1,0:T(1,128)} all-gather(s32[1,1,32]{2,1,0:T(1,128)} %bitcast.453), channel_id=1, replica_groups=mesh['dp'=16,'tensor'=2] {'dp','tensor'}, dimensions={0}, use_global_device_ids=true | all-gather | bytes 4224 | tf_op jit(solution)/shard_map/all_gather | solution.py:266
  946.9 37.2 %all-gather.6 = s32[32,1,32]{2,1,0:T(1,128)} all-gather(s32[1,1,32]{2,1,0:T(1,128)} %bitcast.454), channel_id=1, replica_groups=mesh['dp'=16,'tensor'=2] {'dp','tensor'}, dimensions={0}, use_global_device_ids=true | all-gather | bytes 4224 | tf_op jit(solution)/shard_map/all_gather | solution.py:267
  1001.4 21.0 fusion.246
  1022.4 4.4 exponential_reduce_fusion
  1040.4 21.5 fusion.219
  1064.6 6.6 reduce-scatter.30.cloned.1.call-done
  1079.7 4.0 fusion.44
  1087.6 10.4 reduce-scatter.32.cloned.1.call-done
  1113.8 11.9 fusion.122
  1128.8 13.4 fusion.119
  1149.8 10.3 reduce-scatter.34.cloned.1.call-done
  1165.9 4.0 fusion.51
  1185.2 12.3 fusion.131
  1197.5 12.5 fusion.134
  1213.6 4.6 convolution_convert_fusion.2
  1234.0 11.8 fusion.125
  1245.9 12.3 fusion.128
  1266.8 10.1 reduce-scatter.44.cloned.1.call-done
  1286.9 4.6 pad_maximum_fusion.1
  1298.7 4.2 pad_maximum_fusion.2
  1303.0 15.3 copy.214
  1328.0 32.7 fusion.155
  1369.1 4.7 pad_maximum_fusion
  1375.6 138.7 %scatter_fusion = f32[25152,768]{1,0:T(8,128)} fusion(f32[25152,768]{1,0:T(8,128)} %fusion.155, s32[1024]{0:T(1024)S(1)} %bitcast.450, f32[1024,768]{1,0:T(8,128)S(1)} %bitcast_convert_fusion), kind=kCustom, calls=%fused_computation.4 | custom fusion | flops 786432 | bytes 9441280 | tf_op jit(solution)/shard_map/scatter-add | solution.py:398
  1514.3 1792.5 %fusion = f32[1584,768]{1,0:T(8,128)} fusion(f32[25152,768]{1,0:T(8,128)} %scatter_fusion), kind=kCustom, calls=%all-reduce-scatter | all-reduce-scatter fusion | flops 19464192 | bytes 82133504
  3313.6 7.5 collective-permute-done
  3321.0 14.2 concatenate.12
  3335.3 4.3 multiply_reduce_fusion.3
  3353.3 40.3 %all-reduce.10 = (f32[]{:T(128)}, f32[]{:T(128)}, f32[7,768]{1,0:T(8,128)S(1)}) all-reduce(f32[]{:T(128)S(6)} %mul.1058, f32[]{:T(128)S(6)} %add.704, f32[7,768]{1,0:T(8,128)S(1)} %stack.150), channel_id=1, replica_groups=mesh['dp'=16,'tensor'=2] {'dp','tensor'}, use_global_device_ids=true, to_apply=%region_36.37 | all-reduce | flops 5378 | bytes 43024 | tf_op jit(solution)/shard_map/psum | solution.py:427
  3396.3 13.3 multiply_subtract_fusion
  (725 shorter events, 272.0 us)
Async XLA Ops:
  7.2 48.2 %copy-start.199 = (s32[1,256]{1,0:T(1,128)S(1)}, s32[1,256]{1,0:T(1,128)}, u32[]{:S(2)}) copy-start(s32[1,256]{1,0:T(1,128)} %param.30) | copy-start | bytes 3076
  7.2 85.3 %copy-start.200 = (s32[16]{0:T(128)S(1)}, s32[16]{0:T(128)}, u32[]{:S(2)}) copy-start(s32[16]{0:T(128)} %param.35) | copy-start | bytes 196
  7.2 406.9 %all-gather.25.cloned.1.call-start = ((), (), s32[]{:S(2)}) async-start(), calls=%async_computation.35 | async-start | bytes 41152512 | tf_op jit(solution)/shard_map/all_gather | solution.py:297
  11.3 558.6 %reduce-scatter.18.cloned.1.call-start = ((), (), s32[]{:S(2)}) async-start(), calls=%async_computation.15 | async-start | bytes 4718592 | tf_op jit(solution)/shard_map/reduce_scatter | solution.py:41
  475.7 108.6 %all-gather.15.cloned.1.call-start = ((), (), s32[]{:S(2)}) async-start(), calls=%async_computation.16 | async-start | bytes 5640192 | tf_op jit(solution)/shard_map/all_gather | solution.py:291
  476.6 168.6 %all-gather.17.cloned.1.call-start = ((), (), s32[]{:S(2)}) async-start(), calls=%async_computation.17 | async-start | bytes 1880064 | tf_op jit(solution)/shard_map/all_gather | solution.py:292
  478.8 177.2 %reduce-scatter.22.cloned.1.call-start = ((), (), s32[]{:S(2)}) async-start(), calls=%async_computation.19 | async-start | bytes 2359296 | tf_op jit(solution)/shard_map/reduce_scatter | solution.py:41
  518.9 338.5 %copy-start.149 = (pred[512]{0:T(512)(128)(4,1)}, pred[512]{0:T(512)(128)(4,1)S(1)}, u32[]{:S(2)}) copy-start(pred[512]{0:T(512)(128)(4,1)S(1)} %iota_compare_fusion.2) | copy-start | bytes 1540
  519.6 52.4 %copy-start.118 = (f32[768]{0:T(1024)}, f32[768]{0:T(1024)S(1)}, u32[]{:S(2)}) copy-start(f32[768]{0:T(1024)S(1)} %get-tuple-element.322) | copy-start | bytes 9220
  519.6 136.5 %copy-start.127 = (f32[768]{0:T(1024)}, f32[768]{0:T(1024)S(1)}, u32[]{:S(2)}) copy-start(f32[768]{0:T(1024)S(1)} %get-tuple-element.323) | copy-start | bytes 9220
  519.6 154.7 %copy-start.120 = (f32[768]{0:T(1024)}, f32[768]{0:T(1024)S(1)}, u32[]{:S(2)}) copy-start(f32[768]{0:T(1024)S(1)} %get-tuple-element.321) | copy-start | bytes 9220
  571.5 262.3 %copy-start = (f32[2,256,768]{2,1,0:T(8,128)}, f32[2,256,768]{2,1,0:T(8,128)S(1)}, u32[]{:S(2)}) copy-start(f32[2,256,768]{2,1,0:T(8,128)S(1)} %bitcast_add_fusion) | copy-start | bytes 4718596
  571.7 84.4 %copy-start.131 = (f32[256]{0:T(256)}, f32[256]{0:T(256)S(1)}, u32[]{:S(2)}) copy-start(f32[256]{0:T(256)S(1)} %broadcast_multiply_fusion.6) | copy-start | bytes 3076
  572.0 78.6 %copy-start.177 = (f32[256]{0:T(256)}, f32[256]{0:T(256)S(1)}, u32[]{:S(2)}) copy-start(f32[256]{0:T(256)S(1)} %get-tuple-element.314) | copy-start | bytes 3076
  595.9 52.2 %copy-start.59 = (f32[2,48,1536]{2,1,0:T(8,128)S(1)}, f32[2,48,1536]{2,1,0:T(8,128)}, u32[]{:S(2)}) copy-start(f32[2,48,1536]{2,1,0:T(8,128)} %param.43) | copy-start | bytes 1769476
  596.6 53.1 %copy-start.31 = (bf16[6,64,512]{2,1,0:T(8,128)(2,1)}, bf16[6,64,512]{2,1,0:T(8,128)(2,1)S(1)}, u32[]{:S(2)}) copy-start(bf16[6,64,512]{2,1,0:T(8,128)(2,1)S(1)} %convolution_convert_fusion.12) | copy-start | bytes 1179652
  596.6 52.4 %copy-start.57 = (f32[2,1536,48]{1,2,0:T(8,128)S(1)}, f32[2,1536,48]{1,2,0:T(8,128)}, u32[]{:S(2)}) copy-start(f32[2,1536,48]{1,2,0:T(8,128)} %param.46) | copy-start | bytes 1769476
  648.1 92.8 %all-gather.19.cloned.1.call-start = ((), (), s32[]{:S(2)}) async-start(), calls=%async_computation.20 | async-start | bytes 5013504 | tf_op jit(solution)/shard_map/all_gather | solution.py:293
  648.9 174.4 %all-gather.21.cloned.1.call-start = ((), (), s32[]{:S(2)}) async-start(), calls=%async_computation.21 | async-start | bytes 5013504 | tf_op jit(solution)/shard_map/all_gather | solution.py:294
  649.7 184.1 %reduce-scatter.20.cloned.1.call-start = ((), (), s32[]{:S(2)}) async-start(), calls=%async_computation.18 | async-start | bytes 2359296 | tf_op jit(solution)/shard_map/reduce_scatter | solution.py:41
  657.4 189.0 %copy-start.6 = (f32[256,768]{1,0:T(8,128)}, f32[256,768]{1,0:T(8,128)S(1)}, u32[]{:S(2)}) copy-start(f32[256,768]{1,0:T(8,128)S(1)} %get-tuple-element.405) | copy-start | bytes 2359300
  674.2 172.2 %reduce-scatter.24.cloned.1.call-start = ((), (), s32[]{:S(2)}) async-start(), calls=%async_computation.22 | async-start | bytes 2359296 | tf_op jit(solution)/shard_map/reduce_scatter | solution.py:41
  674.3 77.4 %copy-start.167 = (f32[256]{0:T(256)}, f32[256]{0:T(256)S(1)}, u32[]{:S(2)}) copy-start(f32[256]{0:T(256)S(1)} %fusion.173) | copy-start | bytes 3076
  676.9 74.8 %copy-start.39 = (bf16[512,768]{1,0:T(8,128)(2,1)}, bf16[512,768]{1,0:T(8,128)(2,1)S(1)}, u32[]{:S(2)}) copy-start(bf16[512,768]{1,0:T(8,128)(2,1)S(1)} %all_gather.95) | copy-start | bytes 2359300
  828.0 48.9 %reduce-scatter.26.cloned.1.call-start = ((), (), s32[]{:S(2)}) async-start(), calls=%async_computation.23 | async-start | bytes 2359296 | tf_op jit(solution)/shard_map/reduce_scatter | solution.py:41
  866.5 127.0 %reduce-scatter.28.cloned.1.call-start = ((), (), s32[]{:S(2)}) async-start(), calls=%async_computation.24 | async-start | bytes 2359296 | tf_op jit(solution)/shard_map/reduce_scatter | solution.py:41
  896.6 174.6 %reduce-scatter.30.cloned.1.call-start = ((), (), s32[]{:S(2)}) async-start(), calls=%async_computation.25 | async-start | bytes 2359296 | tf_op jit(solution)/shard_map/reduce_scatter | solution.py:41
  1064.6 33.4 reduce-scatter.32.cloned.1.call-start
  1087.5 62.3 %reduce-scatter.38.cloned.1.call-start = ((), (), s32[]{:S(2)}) async-start(), calls=%async_computation.29 | async-start | bytes 2359296 | tf_op jit(solution)/shard_map/reduce_scatter | solution.py:41
  1128.8 31.3 reduce-scatter.34.cloned.1.call-start
  1149.7 71.7 %reduce-scatter.36.cloned.1.call-start = ((), (), s32[]{:S(2)}) async-start(), calls=%async_computation.28 | async-start | bytes 2359296 | tf_op jit(solution)/shard_map/reduce_scatter | solution.py:41
  1163.2 61.7 %copy-start.170 = (f32[256]{0:T(256)}, f32[256]{0:T(256)S(1)}, u32[]{:S(2)}) copy-start(f32[256]{0:T(256)S(1)} %negate_multiply_fusion.6) | copy-start | bytes 3076
  1173.7 93.1 %reduce-scatter.46.cloned.1.call-start = ((), (), s32[]{:S(2)}) async-start(), calls=%async_computation.33 | async-start | bytes 2359296 | tf_op jit(solution)/shard_map/reduce_scatter | solution.py:41
  1221.3 55.7 %reduce-scatter.44.cloned.1.call-start = ((), (), s32[]{:S(2)}) async-start(), calls=%async_computation.32 | async-start | bytes 2359296 | tf_op jit(solution)/shard_map/reduce_scatter | solution.py:41
  1266.5 107.3 %all-gather.23.cloned.1.call-start = ((), (), s32[]{:S(2)}) async-start(), calls=%async_computation.34 | async-start | bytes 2359296 | tf_op jit(solution)/shard_map/all_gather | solution.py:37
  1282.5 2057.0 %reduce-scatter.42.cloned.1.call-start = ((), (), s32[]{:S(2)}) async-start(), calls=%async_computation.31 | async-start | bytes 10027008 | tf_op jit(solution)/shard_map/reduce_scatter | solution.py:411
  1291.6 2049.8 %all-reduce.15.cloned.1.call-start = ((), (), s32[]{:S(2)}) async-start(), calls=%async_computation.36 | async-start | bytes 31457280
  1327.1 2019.9 %reduce-scatter.40.cloned.1.call-start = ((), (), s32[]{:S(2)}) async-start(), calls=%async_computation.30 | async-start | bytes 11280384 | tf_op jit(solution)/shard_map/reduce_scatter | solution.py:405
  1514.3 1795.9 %copy-start.196 = (u32[32]{0:T(128)S(1)}, u32[32]{0:T(128)}, u32[]{:S(2)}) copy-start(u32[32]{0:T(128)} %constant.490) | copy-start | bytes 388
  1514.3 1799.1 %copy-start.159 = (f32[768]{0:T(1024)S(1)}, f32[768]{0:T(1024)}, u32[]{:S(2)}) copy-start(f32[768]{0:T(1024)} %get-tuple-element.301) | copy-start | bytes 9220
  1514.3 1799.2 %copy-start.160 = (f32[768]{0:T(1024)S(1)}, f32[768]{0:T(1024)}, u32[]{:S(2)}) copy-start(f32[768]{0:T(1024)} %get-tuple-element.303) | copy-start | bytes 9220
  1514.3 1799.2 %copy-start.162 = (f32[768]{0:T(1024)S(1)}, f32[768]{0:T(1024)}, u32[]{:S(2)}) copy-start(f32[768]{0:T(1024)} %get-tuple-element.305) | copy-start | bytes 9220
  1514.3 1799.2 %copy-start.161 = (f32[768]{0:T(1024)S(1)}, f32[768]{0:T(1024)}, u32[]{:S(2)}) copy-start(f32[768]{0:T(1024)} %get-tuple-element.430) | copy-start | bytes 9220
  1514.3 1799.2 %copy-start.163 = (f32[768]{0:T(1024)S(1)}, f32[768]{0:T(1024)}, u32[]{:S(2)}) copy-start(f32[768]{0:T(1024)} %get-tuple-element.309) | copy-start | bytes 9220
  3307.9 13.2 collective-permute-start
  3335.2 60.4 %copy-start.117 = (f32[7,768]{1,0:T(8,128)S(1)}, f32[7,768]{1,0:T(8,128)}, u32[]{:S(2)}) copy-start(f32[7,768]{1,0:T(8,128)} %param.49) | copy-start | bytes 64516
  3335.2 60.4 %copy-start.146 = (f32[7,768]{1,0:T(8,128)S(1)}, f32[7,768]{1,0:T(8,128)}, u32[]{:S(2)}) copy-start(f32[7,768]{1,0:T(8,128)} %param.51) | copy-start | bytes 64516
  3335.2 60.4 %copy-start.147 = (f32[7,768]{1,0:T(8,128)S(1)}, f32[7,768]{1,0:T(8,128)}, u32[]{:S(2)}) copy-start(f32[7,768]{1,0:T(8,128)} %param.50) | copy-start | bytes 64516
  (189 other events, 1311.2 us)
Sparse Core Ops, SparseCore 0:
  11.4 402.6 all-gather.24
  475.8 8.4 reduce-scatter.17
  487.9 96.3 all-gather.14
  587.8 57.3 all-gather.16
  648.2 7.8 reduce-scatter.21
  659.2 81.6 all-gather.18
  744.1 79.0 all-gather.20
  826.1 7.6 reduce-scatter.19
  836.1 10.2 reduce-scatter.23
  866.6 10.2 reduce-scatter.25
  896.8 10.2 reduce-scatter.27
  1064.7 6.5 reduce-scatter.29
  1087.6 10.2 reduce-scatter.31
  1128.9 10.2 reduce-scatter.37
  1149.8 10.2 reduce-scatter.33
  1173.8 10.2 reduce-scatter.35
  1221.4 10.2 reduce-scatter.45
  1266.7 10.2 reduce-scatter.43
  1282.6 11.0 all-gather.22
  1300.1 172.0 reduce-scatter.41
  1479.2 733.3 all-reduce.14
  2218.4 370.7 reduce-scatter.39
where the time goes:
time: 3430 us; the launch traced here: 3420 us
  blocking collectives  2120 us (62%)
  waiting for transfers between devices  589 us (17%)
  matrix products  284 us (8%)
  other arithmetic  264 us (8%)
  local copies, waits for them, and re-layouts  136 us (4%)
    unnamed x3, blocking collectives  1830 us
    all_gather x1, waiting for transfers between devices, local(): lax.all_gather(token_table.astype(jnp.bfloat16), 'dp', axis=0, tiled=True)  320 us
    scatter-add x1, other arithmetic, local(): jax.ops.segment_sum(grad_rows_all.reshape(-1, width).astype(jnp.float32),...  139 us
    unnamed x445, local copies, waits for them, and re-layouts  87.9 us
    dot_general x17, matrix products, product(): return jnp.dot(left, right, preferred_element_type=jnp.float32)  75.1 us
    all_gather x1, waiting for transfers between devices, local(): lax.all_gather(reduce_weight.astype(jnp.bfloat16), 'dp', axis=2, tiled=True)  71.6 us
  transfers between devices with their start and end apart: 23, of which 14 were waited for; matrix products, arithmetic and copies ran while one was open for 65% of the time, Pallas kernels for 0%

commit v1 on v0

v1 whole, which is shorter than its diff:
```python
import jax
import jax.numpy as jnp
from jax import lax
from jax.sharding import PartitionSpec as P

HEAD_DIM = 64
MAX_NORM = 0.01
LEARN_RATE = 0.03
GAIN_RATE = 0.3
FIRST_DECAY = 0.9
SECOND_DECAY = 0.999
ADAM_EPSILON = 1e-08
WEIGHT_DECAY = 0.01
SCORE_FLOOR = -1000000000.0
EVERY = ("dp", "tensor")
CORE_SWAP = ((0, 1), (1, 0))
SLOTS = 32


def norm_rows(values, gain):
    centered = values - jnp.mean(values, axis=-1, keepdims=True)
    variance = jnp.mean(centered * centered, axis=-1, keepdims=True)
    return centered * lax.rsqrt(variance + 1e-05) * gain


def swap(values):
    return lax.ppermute(values, "tensor", CORE_SWAP)


def spread(rows):
    return jnp.concatenate([rows, swap(rows)], axis=0)


def collect(partial_rows):
    half = partial_rows.shape[0] // 2
    return partial_rows[:half] + swap(partial_rows[half:])


def to_all(values, axis=EVERY):
    size = lax.axis_size(axis)
    return lax.all_to_all(
        jnp.broadcast_to(values[None], (size,) + values.shape), axis, 0, 0, tiled=True
    )


def product(left, right):
    return jnp.dot(left, right, preferred_element_type=jnp.float32)


def product_tn(left, right):
    return lax.dot_general(
        left, right, (((0,), (0,)), ((), ())), preferred_element_type=jnp.float32
    )


def product_nt(left, right):
    return lax.dot_general(
        left, right, (((1,), (1,)), ((), ())), preferred_element_type=jnp.float32
    )


def heads_of(values):
    return values.reshape(values.shape[0], values.shape[1] // HEAD_DIM, HEAD_DIM)


def scores_for(query, key, allowed):
    raw = jnp.einsum(
        "qhd,khd->hqk", heads_of(query), heads_of(key), preferred_element_type=jnp.float32
    )
    return jnp.where(allowed[None], raw * HEAD_DIM ** (-0.5), SCORE_FLOOR)


def attend_forward(query, key, value, allowed):
    scores = scores_for(query, key, allowed)
    highest = jnp.max(scores, axis=-1, keepdims=True)
    log_total = highest + jnp.log(jnp.sum(jnp.exp(scores - highest), axis=-1, keepdims=True))
    weights = jnp.exp(scores - log_total).astype(jnp.bfloat16)
    mixed = jnp.einsum(
        "hqk,khd->qhd", weights, heads_of(value), preferred_element_type=jnp.float32
    )
    return mixed.astype(jnp.bfloat16).reshape(query.shape), log_total


def attend_backward(query, key, value, log_total, grad_mixed, allowed):
    grad_heads = heads_of(grad_mixed)
    weights = jnp.exp(scores_for(query, key, allowed) - log_total)
    grad_value = jnp.einsum(
        "hqk,qhd->khd",
        weights.astype(jnp.bfloat16),
        grad_heads,
        preferred_element_type=jnp.float32,
    )
    grad_weights = jnp.einsum(
        "qhd,khd->hqk", grad_heads, heads_of(value), preferred_element_type=jnp.float32
    )
    inner = jnp.sum(weights * grad_weights, axis=-1, keepdims=True)
    grad_scores = (weights * (grad_weights - inner) * HEAD_DIM ** (-0.5)).astype(jnp.bfloat16)
    grad_query = jnp.einsum(
        "hqk,khd->qhd", grad_scores, heads_of(key), preferred_element_type=jnp.float32
    )
    grad_key = jnp.einsum(
        "hqk,qhd->khd", grad_scores, heads_of(query), preferred_element_type=jnp.float32
    )
    return tuple(
        grad.astype(jnp.bfloat16).reshape(query.shape)
        for grad in (grad_query, grad_key, grad_value)
    )


def attention_forward(stream, gain, weights, allowed, memory):
    gathered = spread(norm_rows(stream, gain).astype(jnp.bfloat16))
    source = gathered if memory is None else memory
    query = product(gathered, weights[0]).astype(jnp.bfloat16)
    key = product(source, weights[1]).astype(jnp.bfloat16)
    value = product(source, weights[2]).astype(jnp.bfloat16)
    mixed, log_total = attend_forward(query, key, value, allowed)
    output = collect(product_nt(mixed, weights[3]))
    return (output, (stream, gathered, query, key, value, mixed, log_total))


def attention_backward(grad_out, gain, weights, allowed, memory, saved):
    stream, gathered, query, key, value, mixed, log_total = saved
    grad_rows = spread(grad_out.astype(jnp.bfloat16))
    grad_leave = product_tn(grad_rows, mixed)
    grad_mixed = product(grad_rows, weights[3]).astype(jnp.bfloat16)
    grad_query, grad_key, grad_value = attend_backward(
        query, key, value, log_total, grad_mixed, allowed
    )
    source = gathered if memory is None else memory
    grads = (
        product_tn(gathered, grad_query),
        product_tn(source, grad_key),
        product_tn(source, grad_value),
        grad_leave,
    )
    back_query = product_nt(grad_query, weights[0])
    back_source = product_nt(grad_key, weights[1]) + product_nt(grad_value, weights[2])
    if memory is None:
        grad_normed = collect(back_query + back_source)
        grad_memory = None
    else:
        grad_normed = collect(back_query)
        grad_memory = collect(back_source)
    grad_stream, grad_gain = jax.vjp(norm_rows, stream, gain)[1](grad_normed)
    return (grad_stream + grad_out, grad_gain, grads, grad_memory)


def gelu_exact(values):
    return jax.nn.gelu(values, approximate=False)


def feed_forward(stream, gain, weights):
    gathered = spread(norm_rows(stream, gain).astype(jnp.bfloat16))
    inner = product(gathered, weights[0])
    hidden = gelu_exact(inner).astype(jnp.bfloat16)
    output = collect(product_nt(hidden, weights[1]))
    return (output, (stream, gathered, inner, hidden))


def feed_backward(grad_out, gain, weights, saved):
    stream, gathered, inner, hidden = saved
    grad_rows = spread(grad_out.astype(jnp.bfloat16))
    grad_shrink = product_tn(grad_rows, hidden)
    grad_hidden = product(grad_rows, weights[1]).astype(jnp.bfloat16)
    grad_inner = jax.vjp(gelu_exact, inner)[1](grad_hidden.astype(jnp.float32))[0].astype(
        jnp.bfloat16
    )
    grad_expand = product_tn(gathered, grad_inner)
    grad_normed = collect(product_nt(grad_inner, weights[0]))
    grad_stream, grad_gain = jax.vjp(norm_rows, stream, gain)[1](grad_normed)
    return (grad_stream + grad_out, grad_gain, (grad_expand, grad_shrink))


def adam_step(master, first, second, grad, clip, fix_one, fix_two, rate):
    grad = grad * clip
    first_new = FIRST_DECAY * first + (1 - FIRST_DECAY) * grad
    second_new = SECOND_DECAY * second + (1 - SECOND_DECAY) * grad * grad
    master_new = master - rate * (
        first_new / fix_one / (jnp.sqrt(second_new / fix_two) + ADAM_EPSILON)
        + WEIGHT_DECAY * master
    )
    return (master_new, first_new, second_new)


def gather_weights(shards):
    return lax.all_gather(shards, "dp", axis=1, tiled=True)


def scatter_grads(grads):
    stacked = jnp.stack([grad.astype(jnp.bfloat16) for grad in grads])
    return lax.psum_scatter(stacked, "dp", scatter_dimension=1, tiled=True).astype(jnp.float32)


def flipped(values):
    return jnp.swapaxes(values, -1, -2)


def request_slots(ids, rows_owned):
    owner = ids // rows_owned
    here = jnp.arange(ids.shape[0])
    earlier = here[None, :] < here[:, None]
    same = ids[:, None] == ids[None, :]
    leads = jnp.sum((same & earlier).astype(jnp.int32), axis=1) == 0
    leader = jnp.min(jnp.where(same, here[None, :], ids.shape[0]), axis=1)
    rank = jnp.sum(
        (
            (here[None, :] < leader[:, None])
            & leads[None, :]
            & (owner[:, None] == owner[None, :])
        ).astype(jnp.int32),
        axis=1,
    )
    return owner, rank, leads


def chosen_rows(index, count, dtype=jnp.bfloat16):
    return (index[:, None] == jnp.arange(count)[None, :]).astype(dtype)


def local(
    source_ids,
    target_ids,
    score_places,
    target_labels,
    source_lengths,
    target_lengths,
    pair_order,
    step_count,
    entry_weight,
    entry_first,
    entry_second,
    exit_weight,
    exit_first,
    exit_second,
    expand_weight,
    expand_first,
    expand_second,
    reduce_weight,
    reduce_first,
    reduce_second,
    norm_gains,
    gains_first,
    gains_second,
    token_table,
    table_first,
    table_second,
    place_table,
    place_first,
    place_second,
):
    groups = lax.axis_size("dp")
    parts = lax.axis_size("tensor")
    devices = groups * parts
    group = lax.axis_index("dp")
    part = lax.axis_index("tensor")
    low = jnp.bfloat16
    rows_owned, width = token_table.shape
    half = source_ids.shape[1]
    spot_share = score_places.shape[1]

    blocks = entry_weight.shape[3]
    entry_low = entry_weight.astype(low)
    leave_low = flipped(exit_weight.astype(low))
    place_low = flipped(place_table.astype(low))
    place_low = jnp.pad(place_low, ((0, 0), (0, 0), (0, blocks - half)))
    expand_low = expand_weight.astype(low)
    shrink_low = flipped(reduce_weight.astype(low))
    narrow = gather_weights(
        jnp.concatenate(
            [
                entry_low[0],
                leave_low[:1],
                entry_low[1],
                leave_low[1:2],
                entry_low[2],
                leave_low[2:],
                place_low,
            ]
        )
    )
    attend_weights = [[narrow[4 * a + b] for b in range(4)] for a in range(3)]
    places = flipped(narrow[12:14, :, :half])
    feed_weights = [
        gather_weights(jnp.stack([expand_low[b], shrink_low[b]])) for b in range(2)
    ]

    ids = jnp.concatenate([source_ids[0], target_ids[0]])
    owner, rank, leads = request_slots(ids, rows_owned)
    rounds = jnp.max(rank) // SLOTS + 1
    slots_all = devices * SLOTS
    slot_names = jnp.arange(slots_all)

    def slot_in(turn):
        return jnp.where(rank // SLOTS == turn, owner * SLOTS + rank % SLOTS, -1)

    def requests_in(turn):
        asked = (slot_names[:, None] == slot_in(turn)[None, :]) & leads[None, :]
        return jnp.sum(
            jnp.where(asked, ids[None, :] % rows_owned + 1, 0), axis=1
        ).reshape(devices, SLOTS)

    spots = score_places[0]
    extras = jnp.concatenate(
        [
            spots,
            target_labels[0],
            (spots < target_lengths[0]).astype(jnp.int32),
            rounds[None],
        ]
    )
    message = jnp.concatenate(
        [
            requests_in(0),
            jnp.broadcast_to(extras[None], (devices, extras.shape[0])),
        ],
        axis=1,
    )
    heard = lax.all_to_all(message, EVERY, 0, 0, tiled=True)
    asked_first = heard[:, :SLOTS].reshape(-1) - 1
    spots_all = heard[:, SLOTS : SLOTS + spot_share]
    labels_all = heard[:, SLOTS + spot_share : SLOTS + 2 * spot_share]
    valid_all = heard[:, SLOTS + 2 * spot_share : SLOTS + 3 * spot_share]
    rounds_all = jnp.max(heard[:, -1])
    own_table = token_table.astype(low)

    def looked_up(asked, slot):
        sent = product(chosen_rows(asked, rows_owned), own_table).astype(low)
        got = lax.all_to_all(
            sent.reshape(devices, SLOTS, width), EVERY, 0, 0, tiled=True
        ).reshape(slots_all, width)
        return product(chosen_rows(slot, slots_all), got)

    def ask_again(turn):
        return (
            lax.all_to_all(requests_in(turn), EVERY, 0, 0, tiled=True).reshape(-1) - 1
        )

    start = looked_up(asked_first, slot_in(0))
    start = lax.while_loop(
        lambda state: state[0] < rounds_all,
        lambda state: (
            state[0] + 1,
            state[1] + looked_up(ask_again(state[0]), slot_in(state[0])),
        ),
        (jnp.int32(1), start),
    )[1]
    start = start.reshape(2, half, width) + places.astype(jnp.float32)

    row_places = jnp.concatenate(
        [part * half + jnp.arange(half), (1 - part) * half + jnp.arange(half)]
    )
    length = row_places.shape[0]
    encoder_mask = jnp.broadcast_to(row_places[None, :] < source_lengths[0], (length, length))
    decoder_mask = (row_places[None, :] <= row_places[:, None]) & (
        row_places[None, :] < target_lengths[0]
    )
    stream = start[0]
    output, enc_attend = attention_forward(
        stream, norm_gains[0], attend_weights[0], encoder_mask, None
    )
    stream = stream + output
    decoded = start[1]
    output, dec_self = attention_forward(
        decoded, norm_gains[3], attend_weights[1], decoder_mask, None
    )
    decoded = decoded + output
    output, enc_feed = feed_forward(stream, norm_gains[1], feed_weights[0])
    stream = stream + output
    memory = spread(norm_rows(stream, norm_gains[2]).astype(low))
    output, dec_cross = attention_forward(
        decoded, norm_gains[4], attend_weights[2], encoder_mask, memory
    )
    decoded = decoded + output
    output, dec_feed = feed_forward(decoded, norm_gains[5], feed_weights[1])
    decoded = decoded + output
    final = spread(norm_rows(decoded, norm_gains[6]).astype(low))

    picked_own = product(
        (spots[:, None] == row_places[None, :]).astype(low), final
    ).astype(low)
    picked_group = to_all(picked_own, "dp")
    picked = jnp.concatenate([picked_group, swap(picked_group)]).reshape(-1, width)
    scored = picked.shape[0]

    def own_first(values):
        values = values.reshape(groups, parts, spot_share)
        mine = jnp.where(part == 0, values[:, 0], values[:, 1])
        theirs = jnp.where(part == 0, values[:, 1], values[:, 0])
        return jnp.stack([mine, theirs]).reshape(-1)

    def own_second(values):
        values = values.reshape(parts, groups, spot_share)
        zero = jnp.where(part == 0, values[0], values[1])
        one = jnp.where(part == 0, values[1], values[0])
        return jnp.stack([zero, one], axis=1).reshape(-1)

    label_row = own_first(labels_all) - (group * parts + part) * rows_owned
    valid = own_first(valid_all).astype(jnp.float32)
    count = jnp.sum(valid_all.astype(jnp.float32))
    logits = product_nt(picked, own_table)
    onehot = chosen_rows(label_row, rows_owned, jnp.bool_)
    highest = jnp.max(logits, axis=-1)
    log_here = highest + jnp.log(jnp.sum(jnp.exp(logits - highest[:, None]), axis=-1))
    golden_here = jnp.sum(jnp.where(onehot, logits, 0.0), axis=-1)
    stats = to_all(jnp.stack([own_second(log_here), own_second(golden_here)]))
    top = jnp.max(stats[:, 0], axis=0)
    log_total = top + jnp.log(jnp.sum(jnp.exp(stats[:, 0] - top[None]), axis=0))
    golden = jnp.sum(stats[:, 1], axis=0)
    losses = (log_total - golden) * valid_all.reshape(-1).astype(jnp.float32)
    mean_loss = jnp.sum(losses) / count
    of_group = (pair_order == group).astype(jnp.float32)
    pair_rows = jnp.sum(
        losses.reshape(groups, parts, spot_share) * of_group[:, None, None], axis=0
    )
    pair_losses = jnp.where(part == 0, pair_rows[0], pair_rows[1])[None]
    probs = jnp.exp(logits - own_first(log_total)[:, None])
    grad_logits = (
        (probs - onehot.astype(jnp.float32)) * (valid / count)[:, None]
    ).astype(low)
    grad_picked = collect(product(grad_logits, own_table))
    grad_picked = lax.all_to_all(
        grad_picked.astype(low).reshape(groups, spot_share, width), "dp", 0, 0, tiled=True
    )
    grad_picked = spread(jnp.sum(grad_picked.astype(jnp.float32), axis=0))
    spots_group = own_first(spots_all).reshape(parts, groups, spot_share)
    spots_group = lax.dynamic_index_in_dim(spots_group, group, 1, False).reshape(-1)
    grad_final = jnp.dot(
        (row_places[:half, None] == spots_group[None, :]).astype(jnp.float32),
        grad_picked,
        precision=lax.Precision.HIGHEST,
        preferred_element_type=jnp.float32,
    )
    grad_table = product_tn(grad_logits, picked)

    grad_decoded, gain_six = jax.vjp(norm_rows, decoded, norm_gains[6])[1](grad_final)
    saved_decoded = dec_feed[0]
    grad_decoded, gain_five, feed_one = feed_backward(
        grad_decoded, norm_gains[5], feed_weights[1], dec_feed
    )
    feed_one = scatter_grads(feed_one)
    grad_decoded, gain_four, attend_two, grad_memory = attention_backward(
        grad_decoded, norm_gains[4], attend_weights[2], encoder_mask, memory, dec_cross
    )
    grad_stream, gain_two = jax.vjp(norm_rows, stream, norm_gains[2])[1](grad_memory)
    grad_stream, gain_one, feed_zero = feed_backward(
        grad_stream, norm_gains[1], feed_weights[0], enc_feed
    )
    feed_zero = scatter_grads(feed_zero)
    grad_decoded, gain_three, attend_one, unused_one = attention_backward(
        grad_decoded, norm_gains[3], attend_weights[1], decoder_mask, None, dec_self
    )
    middle = scatter_grads(attend_two + attend_one)
    grad_stream, gain_zero, attend_zero, unused_zero = attention_backward(
        grad_stream, norm_gains[0], attend_weights[0], encoder_mask, None, enc_attend
    )
    grad_start = jnp.stack([grad_stream, grad_decoded]).astype(low)
    place_grads = jnp.pad(flipped(grad_start), ((0, 0), (0, 0), (0, blocks - half)))
    last = scatter_grads(attend_zero + (place_grads[0], place_grads[1]))

    start_rows = grad_start.reshape(2 * half, width)

    def returned(asked, slot):
        sent = product_tn(chosen_rows(slot, slots_all), start_rows).astype(low)
        got = lax.all_to_all(
            sent.reshape(devices, SLOTS, width), EVERY, 0, 0, tiled=True
        ).reshape(slots_all, width)
        return product_tn(chosen_rows(asked, rows_owned), got)

    table_grad = grad_table + returned(asked_first, slot_in(0))
    table_grad = lax.while_loop(
        lambda state: state[0] < rounds_all,
        lambda state: (
            state[0] + 1,
            state[1] + returned(ask_again(state[0]), slot_in(state[0])),
        ),
        (jnp.int32(1), table_grad),
    )[1]

    gain_partial = jnp.stack(
        [gain_zero, gain_one, gain_two, gain_three, gain_four, gain_five, gain_six]
    )
    gain_own = jnp.sum(
        lax.all_to_all(gain_partial.reshape(devices, -1), EVERY, 0, 0, tiled=True), axis=0
    )
    entry_grad = jnp.stack([last[:3], middle[4:7], middle[:3]])
    leave_grad = flipped(jnp.stack([last[3], middle[7], middle[3]]))
    expand_grad = jnp.stack([feed_zero[0], feed_one[0]])
    shrink_grad = flipped(jnp.stack([feed_zero[1], feed_one[1]]))
    place_grad = flipped(last[4:6, :, :half])
    squares = jnp.sum(gain_own * gain_own)
    for grad in (entry_grad, leave_grad, expand_grad, shrink_grad, table_grad, place_grad):
        squares = squares + jnp.sum(grad * grad)
    last_words = to_all(jnp.concatenate([gain_own, squares[None]]))
    gain_grad = last_words[:, :-1].reshape(norm_gains.shape)
    gradient_norm = jnp.sqrt(jnp.sum(last_words[:, -1]))
    clip = jnp.minimum(1.0, MAX_NORM / (gradient_norm + 1e-06))
    steps = step_count[0].astype(jnp.float32)
    fix_one = 1 - FIRST_DECAY**steps
    fix_two = 1 - SECOND_DECAY**steps
    masters = (
        entry_weight,
        exit_weight,
        expand_weight,
        reduce_weight,
        norm_gains,
        token_table,
        place_table,
    )
    firsts = (
        entry_first,
        exit_first,
        expand_first,
        reduce_first,
        gains_first,
        table_first,
        place_first,
    )
    seconds = (
        entry_second,
        exit_second,
        expand_second,
        reduce_second,
        gains_second,
        table_second,
        place_second,
    )
    grads = (entry_grad, leave_grad, expand_grad, shrink_grad, gain_grad, table_grad, place_grad)
    rates = (LEARN_RATE, LEARN_RATE, LEARN_RATE, LEARN_RATE, GAIN_RATE, LEARN_RATE, LEARN_RATE)
    results = [mean_loss, gradient_norm, pair_losses]
    for master, first, second, grad, rate in zip(masters, firsts, seconds, grads, rates):
        results.extend(adam_step(master, first, second, grad, clip, fix_one, fix_two, rate))
    return tuple(results)


def solution(mesh):
    return jax.shard_map(
        local,
        mesh=mesh,
        in_specs=(
            P("dp", "tensor"),
            P("dp", "tensor"),
            P("dp", "tensor"),
            P("dp", "tensor"),
            P("dp"),
            P("dp"),
            P(),
            P(),
            P(None, None, "dp", "tensor"),
            P(None, None, "dp", "tensor"),
            P(None, None, "dp", "tensor"),
            P(None, "tensor", "dp"),
            P(None, "tensor", "dp"),
            P(None, "tensor", "dp"),
            P(None, "dp", "tensor"),
            P(None, "dp", "tensor"),
            P(None, "dp", "tensor"),
            P(None, "tensor", "dp"),
            P(None, "tensor", "dp"),
            P(None, "tensor", "dp"),
            P(),
            P(),
            P(),
            P(("dp", "tensor"), None),
            P(("dp", "tensor"), None),
            P(("dp", "tensor"), None),
            P(None, "tensor", "dp"),
            P(None, "tensor", "dp"),
            P(None, "tensor", "dp"),
        ),
        out_specs=(
            P(),
            P(),
            P("dp", "tensor"),
            P(None, None, "dp", "tensor"),
            P(None, None, "dp", "tensor"),
            P(None, None, "dp", "tensor"),
            P(None, "tensor", "dp"),
            P(None, "tensor", "dp"),
            P(None, "tensor", "dp"),
            P(None, "dp", "tensor"),
            P(None, "dp", "tensor"),
            P(None, "dp", "tensor"),
            P(None, "tensor", "dp"),
            P(None, "tensor", "dp"),
            P(None, "tensor", "dp"),
            P(),
            P(),
            P(),
            P(("dp", "tensor"), None),
            P(("dp", "tensor"), None),
            P(("dp", "tensor"), None),
            P(None, "tensor", "dp"),
            P(None, "tensor", "dp"),
            P(None, "tensor", "dp"),
        ),
        check_vma=False,
    )
```

time: 3430 us -> 1160 us (0.34)
  blocking collectives: 2120 us -> 50.4 us
  other arithmetic: 264 us -> 104 us
  local copies, waits for them, and re-layouts: 136 us -> 59.7 us
  matrix products: 284 us -> 240 us
  waiting for transfers between devices: 589 us -> 629 us
    unnamed x3 -> x0, blocking collectives: 1830 us -> none
    all_gather x6 -> x3, waiting for transfers between devices: 514 us -> 132 us  [gather_weights(): return lax.all_gather(shards, 'dp', axis=1, tiled=True)]
    reduce_scatter x15 -> x4, waiting for transfers between devices: 66.9 us -> 347 us  [scatter_grads(): lax.psum_scatter(stacked, 'dp', scatter_dimension=1, tiled=True)]
    all_gather x18 -> x0, blocking collectives: 244 us -> none  [the longest x1 49.6 us: local(): lax.all_gather(place_table.astype(jnp.bfloat16), 'dp', axis=2, tiled=True)]
    scatter-add x2 -> x0, other arithmetic: 141 us -> none  [the longest x1 139 us: local(): jax.ops.segment_sum(grad_rows_all.reshape(-1, width).astype(jnp.float32),...]
    all_to_all x0 -> x6, waiting for transfers between devices: none -> 131 us  [the longest x1 56.2 us: looked_up(): lax.all_to_all(sent.reshape(devices, SLOTS, width), EVERY, 0, 0, tiled=True)]
    unnamed x445 -> x485, local copies, waits for them, and re-layouts: 87.9 us -> 18.6 us
    all_to_all x0 -> x2, blocking collectives: none -> 50.4 us  [the longest x1 25.7 us: to_all(): lax.all_to_all(jnp.broadcast_to(values[None], (size,) + values.shape), ax...]
  transfers between devices with their start and end apart: 23 -> 39, of which waited for: 14 -> 24; matrix products, arithmetic and copies ran while one was open for 65% -> 22% of each run, Pallas kernels for 0% -> 0%
where the time goes in v1:
time: 1160 us; the launch traced here: 1150 us
  waiting for transfers between devices  629 us (54%)
  matrix products  240 us (21%)
  other arithmetic  104 us (9%)
  local copies, waits for them, and re-layouts  59.7 us (5%)
  blocking collectives  50.4 us (4%)
  between operations  31.6 us (3%)
  starting transfers between devices  29.5 us (3%)
    reduce_scatter x4, waiting for transfers between devices, scatter_grads(): lax.psum_scatter(stacked, 'dp', scatter_dimension=1, tiled=True)  347 us
    all_gather x3, waiting for transfers between devices, gather_weights(): return lax.all_gather(shards, 'dp', axis=1, tiled=True)  132 us
    dot_general x20, matrix products, product(): return jnp.dot(left, right, preferred_element_type=jnp.float32)  67.5 us
    all_to_all x1, waiting for transfers between devices, looked_up(): lax.all_to_all(sent.reshape(devices, SLOTS, width), EVERY, 0, 0, tiled=True)  56.2 us
    all_to_all x1, waiting for transfers between devices, returned(): lax.all_to_all(sent.reshape(devices, SLOTS, width), EVERY, 0, 0, tiled=True)  52.1 us
    dot_general x3, matrix products, attend_backward(): jnp.einsum('hqk,khd->qhd', grad_scores, heads_of(key), preferred_element_...  38.3 us
    dot_general x3, matrix products, attend_backward(): jnp.einsum('hqk,qhd->khd', grad_scores, heads_of(query), preferred_elemen...  36.7 us
    dot_general x19, matrix products, product_tn(): lax.dot_general(left, right, (((0,), (0,)), ((), ())), preferred_element_...  36.1 us
  transfers between devices with their start and end apart: 39, of which 24 were waited for; matrix products, arithmetic and copies ran while one was open for 22% of the time, Pallas kernels for 0%

profile of v1, /device:TPU:0, one launch (start us, length us, event | category | flops | bytes accessed | tf_op | source)
XLA Modules:
  0.0 1146.4 jit_solution(7418299059980921054)
XLA Ops:
  19.4 7.3 all-to-all-start.4
  26.7 4.0 convert_element_type.366
  30.8 3.6 all-to-all-done.4
  35.1 6.1 fusion.163
  41.2 2.8 all-to-all-start.5
  46.4 56.2 %all-to-all-done.5 = bf16[32,32,768]{2,1,0:T(8,128)(2,1)S(1)} async-done(((bf16[32,32,768]{2,1,0:T(8,128)(2,1)}), bf16[32,32,768]{2,1,0:T(8,128)(2,1)S(1)}, u32[]{:S(2)}, u32[]{:S(2)}) %all-to-all-start.5) | async-done | bytes 1572896 | tf_op jit(solution)/shard_map/all_to_all | solution.py:328
  104.8 47.4 %all-gather.4.cloned.1.call-done = bf16[14,768,384]{2,1,0:T(8,128)(2,1)} async-done(((bf16[14,48,384]{2,1,0:T(8,128)(2,1)}), bf16[14,768,384]{2,1,0:T(8,128)(2,1)}) %all-gather.4.cloned.1.call-update) | async-done | bytes 8257552 | tf_op jit(solution)/shard_map/all_gather | solution.py:186
  196.2 38.0 %all-gather.6.cloned.1.call-done = bf16[2,768,1536]{2,1,0:T(8,128)(2,1)} async-done(((bf16[2,48,1536]{2,1,0:T(8,128)(2,1)}), bf16[2,768,1536]{2,1,0:T(8,128)(2,1)}) %all-gather.6.cloned.1.call-update) | async-done | bytes 4718608 | tf_op jit(solution)/shard_map/all_gather | solution.py:186
  234.2 10.9 multiply_convert_fusion.5
  269.0 47.0 %all-gather.8.cloned.1.call-done = bf16[2,768,1536]{2,1,0:T(8,128)(2,1)} async-done(((bf16[2,48,1536]{2,1,0:T(8,128)(2,1)}), bf16[2,768,1536]{2,1,0:T(8,128)(2,1)}) %all-gather.8.cloned.1.call-update) | async-done | bytes 4718608 | tf_op jit(solution)/shard_map/all_gather | solution.py:186
  316.0 11.1 multiply_convert_fusion.4
  334.5 25.7 %all_to_all.115 = bf16[16,32,768]{2,1,0:T(8,128)(2,1)} all-to-all(bf16[16,32,768]{2,1,0:T(8,128)(2,1)S(1)} %broadcast_in_dim.175), channel_id=1, replica_groups=mesh['dp'=16,'tensor'=2] {'dp'}, dimensions={0} | all-to-all | bytes 1572864 | tf_op jit(solution)/shard_map/all_to_all | solution.py:41
  364.5 5.0 fusion.364
  385.8 3.3 all-to-all-start.7
  390.7 9.1 all-to-all-done.7
  408.7 6.5 fusion.321
  415.5 3.4 collective-permute-done.13
  419.1 24.7 %all_to_all.116 = bf16[16,32,768]{2,1,0:T(8,128)(2,1)S(1)} all-to-all(bf16[16,32,768]{2,1,0:T(8,128)(2,1)S(1)} %bitcast.433), channel_id=1, replica_groups=mesh['dp'=16,'tensor'=2] {'dp'}, dimensions={0} | all-to-all | bytes 1572864 | tf_op jit(solution)/shard_map/all_to_all | solution.py:421
  454.1 4.8 fusion.80
  467.0 4.2 fusion.151
  477.7 3.6 fusion.366
  481.3 12.3 %fusion.189 = bf16[6,64,512]{2,1,0:T(8,128)(2,1)S(1)} fusion(bf16[512,6,64]{0,2,1:T(8,128)(2,1)S(1)} %bitcast.490, f32[6,512,512]{1,2,0:T(8,128)} %fusion.366, f32[6,512,512]{1,2,0:T(8,128)} %copy-done.3, f32[6,512]{1,0:T(8,128)} %copy-done.129, pred[512]{0:T(512)(128)(4,1)} %copy-done.146), kind=kOutput, calls=%fused_computation.263 | convolution fusion | flops 218828288 | bytes 13382144 | tf_op jit(solution)/shard_map/hqk,qhd->khd/dot_general | solution.py:101
  493.6 12.0 %fusion.192 = bf16[6,64,512]{2,1,0:T(8,128)(2,1)S(1)} fusion(bf16[512,6,64]{0,2,1:T(8,128)(2,1)S(1)} %bitcast.492, f32[6,512,512]{1,2,0:T(8,128)} %fusion.366, f32[6,512,512]{1,2,0:T(8,128)} %copy-done.3, f32[6,512]{1,0:T(8,128)} %copy-done.129, pred[512]{0:T(512)(128)(4,1)} %copy-done.146), kind=kOutput, calls=%fused_computation.264 | convolution fusion | flops 218828288 | bytes 13382144 | tf_op jit(solution)/shard_map/hqk,khd->qhd/dot_general | solution.py:98
  529.0 4.0 fusion.87
  539.2 3.6 fusion.368
  542.8 13.4 %fusion.201 = bf16[6,64,512]{2,1,0:T(8,128)(2,1)} fusion(bf16[512,6,64]{0,2,1:T(8,128)(2,1)S(1)} %bitcast.488, f32[6,512,512]{1,2,0:T(8,128)} %fusion.368, f32[6,512,512]{1,2,0:T(8,128)} %copy-done.8, f32[6,512]{1,0:T(8,128)S(1)} %copy-done.173, pred[512,512]{0,1:T(8,128)(4,1)S(1)} %copy-done.35), kind=kOutput, calls=%fused_computation.267 | convolution fusion | flops 218828288 | bytes 13643776 | tf_op jit(solution)/shard_map/hqk,khd->qhd/dot_general | solution.py:98
  556.2 11.1 fusion.204
  569.2 4.8 convolution_convert_fusion.18
  582.4 3.7 fusion.367
  586.1 13.0 %fusion.195 = bf16[6,64,512]{2,1,0:T(8,128)(2,1)} fusion(bf16[512,6,64]{0,2,1:T(8,128)(2,1)} %bitcast.484, f32[6,512,512]{1,2,0:T(8,128)} %fusion.367, f32[6,512,512]{1,2,0:T(8,128)} %copy-done.2, f32[6,512]{1,0:T(8,128)} %copy-done.128, pred[512]{0:T(512)(128)(4,1)} %copy-done.146), kind=kOutput, calls=%fused_computation.265 | convolution fusion | flops 218828288 | bytes 13382144 | tf_op jit(solution)/shard_map/hqk,khd->qhd/dot_general | solution.py:98
  599.0 13.3 %fusion.198 = bf16[6,64,512]{2,1,0:T(8,128)(2,1)} fusion(bf16[512,6,64]{0,2,1:T(8,128)(2,1)} %bitcast.482, f32[6,512,512]{1,2,0:T(8,128)} %fusion.367, f32[6,512,512]{1,2,0:T(8,128)} %copy-done.2, f32[6,512]{1,0:T(8,128)} %copy-done.128, pred[512]{0:T(512)(128)(4,1)} %copy-done.146), kind=kOutput, calls=%fused_computation.266 | convolution fusion | flops 218828288 | bytes 13382144 | tf_op jit(solution)/shard_map/hqk,qhd->khd/dot_general | solution.py:101
  629.3 6.7 copy.317
  644.0 5.0 copy.319
  655.6 4.9 all-to-all-done.9
  660.5 3.4 all-to-all-start.10
  665.3 3.2 fusion.149
  673.2 52.1 %all-to-all-done.10 = bf16[32,32,768]{2,1,0:T(8,128)(2,1)} async-done(((bf16[32,32,768]{2,1,0:T(8,128)(2,1)}), bf16[32,32,768]{2,1,0:T(8,128)(2,1)}, u32[]{:S(2)}, u32[]{:S(2)}) %all-to-all-start.10) | async-done | bytes 1572896 | tf_op jit(solution)/shard_map/all_to_all | solution.py:464
  725.3 5.2 fusion.37
  730.6 5.3 convolution_add_fusion
  737.1 4.3 multiply_reduce_fusion.3
  742.4 66.5 %reduce-scatter.5.cloned.1.call-done = bf16[6,48,384]{2,0,1:T(8,128)(2,1)} async-done(((bf16[6,768,384]{2,0,1:T(8,128)(2,1)}), bf16[6,48,384]{2,0,1:T(8,128)(2,1)}) %reduce-scatter.5.cloned.1.call-update) | async-done | bytes 221200 | tf_op jit(solution)/shard_map/reduce_scatter | solution.py:191
  810.6 139.8 %reduce-scatter.7.cloned.1.call-done = bf16[8,48,384]{2,0,1:T(8,128)(2,1)} async-done(((bf16[8,768,384]{2,0,1:T(8,128)(2,1)}), bf16[8,48,384]{2,0,1:T(8,128)(2,1)}) %reduce-scatter.7.cloned.1.call-update) | async-done | bytes 294928 | tf_op jit(solution)/shard_map/reduce_scatter | solution.py:191
  952.8 140.7 %reduce-scatter.9.cloned.1.call-done = bf16[2,48,1536]{2,1,0:T(8,128)(2,1)} async-done(((bf16[2,768,1536]{2,1,0:T(8,128)(2,1)}), bf16[2,48,1536]{2,1,0:T(8,128)(2,1)}) %reduce-scatter.9.cloned.1.call-update) | async-done | bytes 294928 | tf_op jit(solution)/shard_map/reduce_scatter | solution.py:191
  1102.7 3.7 all-to-all-start.11
  1108.3 5.4 all-to-all-done.11
  1119.1 2.9 multiply_subtract_fusion.2
  1122.0 2.9 multiply_subtract_fusion.3
  1127.6 8.9 multiply_subtract_fusion
  (812 shorter events, 238.0 us)
Async XLA Ops:
  7.2 145.1 %all-gather.4.cloned.1.call-start = ((), (), s32[]{:S(2)}) async-start(), calls=%async_computation.16 | async-start | bytes 8773632 | tf_op jit(solution)/shard_map/all_gather | solution.py:186
  19.4 14.9 %all-to-all-start.4 = ((s32[32,1,129]{2,1,0:T(1,128)}), s32[32,1,129]{2,1,0:T(1,128)S(1)}, u32[]{:S(2)}, u32[]{:S(2)}) async-start(s32[32,1,129]{2,1,0:T(1,128)} %all_to_all.73), calls=%async_computation.4 | async-start | bytes 65536 | tf_op jit(solution)/shard_map/all_to_all | solution.py:318
  41.2 61.4 %all-to-all-start.5 = ((bf16[32,32,768]{2,1,0:T(8,128)(2,1)}), bf16[32,32,768]{2,1,0:T(8,128)(2,1)S(1)}, u32[]{:S(2)}, u32[]{:S(2)}) async-start(bf16[32,32,768]{2,1,0:T(8,128)(2,1)} %bitcast.451), calls=%async_computation.5 | async-start | bytes 3145728 | tf_op jit(solution)/shard_map/all_to_all | solution.py:328
  44.0 190.2 %all-gather.6.cloned.1.call-start = ((), (), s32[]{:S(2)}) async-start(), calls=%async_computation.17 | async-start | bytes 5013504 | tf_op jit(solution)/shard_map/all_gather | solution.py:186
  45.0 271.0 %all-gather.8.cloned.1.call-start = ((), (), s32[]{:S(2)}) async-start(), calls=%async_computation.18 | async-start | bytes 5013504 | tf_op jit(solution)/shard_map/all_gather | solution.py:186
  45.7 113.3 %copy-start.117 = (f32[768]{0:T(1024)}, f32[768]{0:T(1024)S(1)}, u32[]{:S(2)}) copy-start(f32[768]{0:T(1024)S(1)} %get-tuple-element.733) | copy-start | bytes 9220
  45.7 133.0 %copy-start.119 = (f32[768]{0:T(1024)}, f32[768]{0:T(1024)S(1)}, u32[]{:S(2)}) copy-start(f32[768]{0:T(1024)S(1)} %get-tuple-element.734) | copy-start | bytes 9220
  45.7 135.6 %copy-start.121 = (f32[768]{0:T(1024)}, f32[768]{0:T(1024)S(1)}, u32[]{:S(2)}) copy-start(f32[768]{0:T(1024)S(1)} %get-tuple-element.732) | copy-start | bytes 9220
  45.7 203.1 %copy-start.123 = (f32[768]{0:T(1024)}, f32[768]{0:T(1024)S(1)}, u32[]{:S(2)}) copy-start(f32[768]{0:T(1024)S(1)} %get-tuple-element.730) | copy-start | bytes 9220
  45.7 204.2 %copy-start.125 = (f32[768]{0:T(1024)}, f32[768]{0:T(1024)S(1)}, u32[]{:S(2)}) copy-start(f32[768]{0:T(1024)S(1)} %get-tuple-element.731) | copy-start | bytes 9220
  159.2 1.8 collective-permute-start.2
  160.0 99.6 %copy-start.146 = (pred[512]{0:T(512)(128)(4,1)}, pred[512]{0:T(512)(128)(4,1)S(1)}, u32[]{:S(2)}) copy-start(pred[512]{0:T(512)(128)(4,1)S(1)} %get-tuple-element.886) | copy-start | bytes 1540
  175.3 2.5 collective-permute-start.3
  180.3 1.8 collective-permute-start
  181.5 52.7 %collective-permute-start.4 = (bf16[256,768]{1,0:T(8,128)(2,1)S(1)}, bf16[256,768]{1,0:T(8,128)(2,1)}, u32[]{:S(2)}, u32[]{:S(2)}) collective-permute-start(bf16[256,768]{1,0:T(8,128)(2,1)S(1)} %multiply_convert_fusion.10), channel_id=1, source_target_pairs={{0,1},{1,0},{2,3},{3,2},{4,5},{5,4},{6,7},{7,6},{8,9},{9,8},{10,11... | collective-permute-start | bytes 1179656 | tf_op jit(solution)/shard_map/ppermute | solution.py:27
  196.0 50.8 %collective-permute-start.1 = (f32[256,768]{1,0:T(8,128)S(1)}, f32[256,768]{1,0:T(8,128)}, u32[]{:S(2)}, u32[]{:S(2)}) collective-permute-start(f32[256,768]{1,0:T(8,128)S(1)} %slice.456), channel_id=1, source_target_pairs={{0,1},{1,0},{2,3},{3,2},{4,5},{5,4},{6,7},{7,6},{8,9},{9,8},{10,11... | collective-permute-start | bytes 2359304 | tf_op jit(solution)/shard_map/ppermute | solution.py:27
  246.7 2.7 collective-permute-start.5
  249.0 1.8 collective-permute-start.7
  250.1 2.5 collective-permute-start.6
  263.9 2.4 collective-permute-start.8
  268.9 47.2 %collective-permute-start.9 = (bf16[256,768]{1,0:T(8,128)(2,1)}, bf16[256,768]{1,0:T(8,128)(2,1)}, u32[]{:S(2)}, u32[]{:S(2)}) collective-permute-start(bf16[256,768]{1,0:T(8,128)(2,1)} %multiply_convert_fusion.7), channel_id=1, source_target_pairs={{0,1},{1,0},{2,3},{3,2},{4,5},{5,4},{6,7},{7,6},{8,9},{9,8},{10,11... | collective-permute-start | bytes 1179656 | tf_op jit(solution)/shard_map/ppermute | solution.py:27
  328.7 2.4 collective-permute-start.10
  332.4 1.8 collective-permute-start.11
  360.3 2.7 collective-permute-start.12
  385.8 13.9 %all-to-all-start.7 = ((f32[32,2,1024]{2,1,0:T(2,128)}), f32[32,2,1024]{2,1,0:T(2,128)}, u32[]{:S(2)}, u32[]{:S(2)}) async-start(f32[32,2,1024]{2,1,0:T(2,128)} %broadcast_in_dim.283), calls=%async_computation.7 | async-start | bytes 524288 | tf_op jit(solution)/shard_map/all_to_all | solution.py:41
  389.2 352.3 %reduce-scatter.11.cloned.1.call-start = ((), (), s32[]{:S(2)}) async-start(), calls=%async_computation.22 | async-start | bytes 5013504 | tf_op jit(solution)/shard_map/reduce_scatter | solution.py:191
  415.4 3.5 collective-permute-start.13
  444.5 2.6 collective-permute-start.14
  452.2 1.9 collective-permute-start.15
  460.5 2.4 collective-permute-start.16
  466.6 7.4 collective-permute-start.17
  509.5 8.9 collective-permute-start.23
  515.3 6.0 collective-permute-start.18
  518.3 290.6 %reduce-scatter.5.cloned.1.call-start = ((), (), s32[]{:S(2)}) async-start(), calls=%async_computation.19 | async-start | bytes 5013504 | tf_op jit(solution)/shard_map/reduce_scatter | solution.py:191
  525.6 1.8 collective-permute-start.19
  526.4 10.3 collective-permute-start.24
  536.5 37.5 %collective-permute-start.20 = (f32[256,768]{1,0:T(8,128)}, f32[256,768]{1,0:T(8,128)S(1)}, u32[]{:S(2)}, u32[]{:S(2)}) collective-permute-start(f32[256,768]{1,0:T(8,128)} %slice.502), channel_id=1, source_target_pairs={{0,1},{1,0},{2,3},{3,2},{4,5},{5,4},{6,7},{7,6},{8,9},{9,8},{10,11... | collective-permute-start | bytes 2359304 | tf_op jit(solution)/shard_map/ppermute | solution.py:27
  575.7 4.9 collective-permute-start.21
  580.4 44.3 %collective-permute-start.25 = (f32[256,768]{1,0:T(8,128)}, f32[256,768]{1,0:T(8,128)S(1)}, u32[]{:S(2)}, u32[]{:S(2)}) collective-permute-start(f32[256,768]{1,0:T(8,128)} %slice.508), channel_id=1, source_target_pairs={{0,1},{1,0},{2,3},{3,2},{4,5},{5,4},{6,7},{7,6},{8,9},{9,8},{10,11... | collective-permute-start | bytes 2359304 | tf_op jit(solution)/shard_map/ppermute | solution.py:27
  619.2 5.5 collective-permute-start.22
  636.1 314.4 %reduce-scatter.7.cloned.1.call-start = ((), (), s32[]{:S(2)}) async-start(), calls=%async_computation.20 | async-start | bytes 5013504 | tf_op jit(solution)/shard_map/reduce_scatter | solution.py:191
  650.7 9.8 all-to-all-start.9
  660.5 64.7 %all-to-all-start.10 = ((bf16[32,32,768]{2,1,0:T(8,128)(2,1)}), bf16[32,32,768]{2,1,0:T(8,128)(2,1)}, u32[]{:S(2)}, u32[]{:S(2)}) async-start(bf16[32,32,768]{2,1,0:T(8,128)(2,1)} %bitcast.125), calls=%async_computation.14 | async-start | bytes 3145728 | tf_op jit(solution)/shard_map/all_to_all | solution.py:464
  664.0 429.5 %reduce-scatter.9.cloned.1.call-start = ((), (), s32[]{:S(2)}) async-start(), calls=%async_computation.21 | async-start | bytes 5013504 | tf_op jit(solution)/shard_map/reduce_scatter | solution.py:191
  951.6 163.6 %copy-start.94 = (f32[2,256,48]{1,2,0:T(8,128)S(1)}, f32[2,256,48]{1,2,0:T(8,128)}, u32[]{:S(2)}) copy-start(f32[2,256,48]{1,2,0:T(8,128)} %param.59) | copy-start | bytes 294916
  952.7 164.3 %copy-start.54 = (f32[3,384,48]{1,2,0:T(8,128)S(1)}, f32[3,384,48]{1,2,0:T(8,128)}, u32[]{:S(2)}) copy-start(f32[3,384,48]{1,2,0:T(8,128)} %param.44) | copy-start | bytes 663556
  952.8 166.3 %copy-start.31 = (f32[2,1536,48]{1,2,0:T(8,128)S(1)}, f32[2,1536,48]{1,2,0:T(8,128)}, u32[]{:S(2)}) copy-start(f32[2,1536,48]{1,2,0:T(8,128)} %param.50) | copy-start | bytes 1769476
  1102.7 10.9 all-to-all-start.11
  (229 other events, 1425.7 us)
Sparse Core Ops, SparseCore 0:
  11.3 140.8 all-gather.3
  155.5 78.6 all-gather.5
  236.9 79.0 all-gather.7
  518.4 135.0 reduce-scatter.10
  659.9 148.9 reduce-scatter.4
  814.5 135.8 reduce-scatter.6
  956.4 137.0 reduce-scatter.8

commit v2 on v1

--- a/solution.py
+++ b/solution.py
@@ -102,47 +102,103 @@
         "hqk,qhd->khd", grad_scores, heads_of(query), preferred_element_type=jnp.float32
     )
     return tuple(
-        grad.astype(jnp.bfloat16).reshape(query.shape)
-        for grad in (grad_query, grad_key, grad_value)
-    )
-
-
-def attention_forward(stream, gain, weights, allowed, memory):
+        grad.astype(jnp.bfloat16).reshape(like.shape)
+        for grad, like in ((grad_query, query), (grad_key, key), (grad_value, value))
+    )
+
+
+def pick_rows(index, rows):
+    return product(index, rows).astype(jnp.bfloat16)
+
+
+def place_exact(index, rows):
+    return jnp.dot(
+        index.astype(jnp.float32),
+        rows,
+        precision=lax.Precision.HIGHEST,
+        preferred_element_type=jnp.float32,
+    )
+
+
+def both(partial_rows):
+    return partial_rows + swap(partial_rows)
+
+
+def norm_backward(values, gain, grad):
+    grad_values, grad_gain = jax.vjp(norm_rows, values, gain)[1](grad)
+    return grad_values, grad_gain
+
+
+def own_half(rows):
+    half = rows.shape[0] // 2
+    return jnp.where(lax.axis_index("tensor") == 0, rows[:half], rows[half:])
+
+
+def in_order(rows):
+    other = swap(rows)
+    return jnp.where(
+        lax.axis_index("tensor") == 0,
+        jnp.concatenate([rows, other]),
+        jnp.concatenate([other, rows]),
+    )
+
+
+def norm_backward_shared(values, gain, grad):
+    grad_values = jax.vjp(lambda rows: norm_rows(rows, gain), values)[1](grad)[0]
+    own = own_half(values)
+    grad_gain = jax.vjp(lambda scale: norm_rows(own, scale), gain)[1](own_half(grad))[0]
+    return grad_values, grad_gain
+
+
+def low_rounded(*values):
+    return tuple(value.astype(jnp.bfloat16) for value in values)
+
+
+def encode_attention(stream, gain, weights, allowed):
     gathered = spread(norm_rows(stream, gain).astype(jnp.bfloat16))
-    source = gathered if memory is None else memory
-    query = product(gathered, weights[0]).astype(jnp.bfloat16)
-    key = product(source, weights[1]).astype(jnp.bfloat16)
-    value = product(source, weights[2]).astype(jnp.bfloat16)
+    query, key, value = low_rounded(*[product(gathered, weights[b]) for b in range(3)])
     mixed, log_total = attend_forward(query, key, value, allowed)
     output = collect(product_nt(mixed, weights[3]))
     return (output, (stream, gathered, query, key, value, mixed, log_total))
 
 
-def attention_backward(grad_out, gain, weights, allowed, memory, saved):
+def encode_attention_backward(grad_out, gain, weights, allowed, saved):
     stream, gathered, query, key, value, mixed, log_total = saved
     grad_rows = spread(grad_out.astype(jnp.bfloat16))
     grad_leave = product_tn(grad_rows, mixed)
     grad_mixed = product(grad_rows, weights[3]).astype(jnp.bfloat16)
+    inner_grads = attend_backward(query, key, value, log_total, grad_mixed, allowed)
+    grads = [product_tn(gathered, grad) for grad in inner_grads]
+    back = sum(product_nt(grad, weight) for grad, weight in zip(inner_grads, weights))
+    grad_stream, grad_gain = norm_backward(stream, gain, collect(back))
+    return (grad_stream + grad_out, grad_gain, low_rounded(*grads, grad_leave))
+
+
+def decode_attention(rows, source, weights, allowed):
+    query = product(rows, weights[0]).astype(jnp.bfloat16)
+    key, value = low_rounded(product(source, weights[1]), product(source, weights[2]))
+    mixed, log_total = attend_forward(query, key, value, allowed)
+    output = both(product_nt(mixed, weights[3]))
+    return (output, (rows, source, query, key, value, mixed, log_total))
+
+
+def decode_attention_backward(grad_out, weights, allowed, saved):
+    rows, source, query, key, value, mixed, log_total = saved
+    grad_rows = grad_out.astype(jnp.bfloat16)
+    grad_leave = product_tn(grad_rows, mixed)
+    grad_mixed = product(grad_rows, weights[3]).astype(jnp.bfloat16)
     grad_query, grad_key, grad_value = attend_backward(
         query, key, value, log_total, grad_mixed, allowed
     )
-    source = gathered if memory is None else memory
-    grads = (
-        product_tn(gathered, grad_query),
+    grads = low_rounded(
+        product_tn(rows, grad_query),
         product_tn(source, grad_key),
         product_tn(source, grad_value),
         grad_leave,
     )
-    back_query = product_nt(grad_query, weights[0])
+    back_rows = product_nt(grad_query, weights[0])
     back_source = product_nt(grad_key, weights[1]) + product_nt(grad_value, weights[2])
-    if memory is None:
-        grad_normed = collect(back_query + back_source)
-        grad_memory = None
-    else:
-        grad_normed = collect(back_query)
-        grad_memory = collect(back_source)
-    grad_stream, grad_gain = jax.vjp(norm_rows, stream, gain)[1](grad_normed)
-    return (grad_stream + grad_out, grad_gain, grads, grad_memory)
+    return (back_rows, back_source, grads)
 
 
 def gelu_exact(values):
@@ -160,15 +216,33 @@
 def feed_backward(grad_out, gain, weights, saved):
     stream, gathered, inner, hidden = saved
     grad_rows = spread(grad_out.astype(jnp.bfloat16))
+    grad_shrink = product_tn(grad_rows, hidden).astype(jnp.bfloat16)
+    grad_hidden = product(grad_rows, weights[1]).astype(jnp.bfloat16)
+    grad_inner = jax.vjp(gelu_exact, inner)[1](grad_hidden.astype(jnp.float32))[0].astype(
+        jnp.bfloat16
+    )
+    grad_expand = product_tn(gathered, grad_inner).astype(jnp.bfloat16)
+    grad_normed = collect(product_nt(grad_inner, weights[0]))
+    grad_stream, grad_gain = jax.vjp(norm_rows, stream, gain)[1](grad_normed)
+    return (grad_stream + grad_out, grad_gain, (grad_expand, grad_shrink))
+
+
+def decode_feed(rows, weights):
+    inner = product(rows, weights[0])
+    hidden = gelu_exact(inner).astype(jnp.bfloat16)
+    return (both(product_nt(hidden, weights[1])), (rows, inner, hidden))
+
+
+def decode_feed_backward(grad_out, weights, saved):
+    rows, inner, hidden = saved
+    grad_rows = grad_out.astype(jnp.bfloat16)
     grad_shrink = product_tn(grad_rows, hidden)
     grad_hidden = product(grad_rows, weights[1]).astype(jnp.bfloat16)
     grad_inner = jax.vjp(gelu_exact, inner)[1](grad_hidden.astype(jnp.float32))[0].astype(
         jnp.bfloat16
     )
-    grad_expand = product_tn(gathered, grad_inner)
-    grad_normed = collect(product_nt(grad_inner, weights[0]))
-    grad_stream, grad_gain = jax.vjp(norm_rows, stream, gain)[1](grad_normed)
-    return (grad_stream + grad_out, grad_gain, (grad_expand, grad_shrink))
+    grad_expand = product_tn(rows, grad_inner)
+    return (both(product_nt(grad_inner, weights[0])), low_rounded(grad_expand, grad_shrink))
 
 
 def adam_step(master, first, second, grad, clip, fix_one, fix_two, rate):
@@ -182,13 +256,45 @@
     return (master_new, first_new, second_new)
 
 
-def gather_weights(shards):
-    return lax.all_gather(shards, "dp", axis=1, tiled=True)
-
-
-def scatter_grads(grads):
-    stacked = jnp.stack([grad.astype(jnp.bfloat16) for grad in grads])
-    return lax.psum_scatter(stacked, "dp", scatter_dimension=1, tiled=True).astype(jnp.float32)
+def bit_order(turn):
+    count = (lax.axis_size("dp") - 1).bit_length()
+    order = list(range(count - 1, -1, -1))
+    if turn % 2:
+        for first in range(0, count - 1, 2):
+            order[first], order[first + 1] = order[first + 1], order[first]
+    return order
+
+
+def swap_bit(values, bit):
+    pairs = [(group, group ^ (1 << bit)) for group in range(lax.axis_size("dp"))]
+    return lax.ppermute(values, "dp", pairs)
+
+
+def gather_weights(shard, turn):
+    held = shard[None]
+    bits = []
+    for bit in bit_order(turn):
+        got = swap_bit(held, bit)
+        above = sum(1 for other in bits if other > bit)
+        shape = (2**above, 2 ** (len(bits) - above)) + shard.shape
+        held = jnp.stack([held.reshape(shape), got.reshape(shape)], axis=1)
+        held = held.reshape((-1,) + shard.shape)
+        bits.append(bit)
+    return held.reshape(-1, shard.shape[1])
+
+
+def scatter_grads(grads, turn):
+    groups = lax.axis_size("dp")
+    held = grads.reshape((groups, grads.shape[0] // groups, grads.shape[1]))
+    bits = sorted(bit_order(turn), reverse=True)
+    for bit in reversed(bit_order(turn)):
+        above = bits.index(bit)
+        halves = held.reshape((2**above, 2, -1) + held.shape[1:])
+        got = swap_bit(halves[:, 1].astype(jnp.bfloat16), bit)
+        held = halves[:, 0].astype(jnp.float32) + got.astype(jnp.float32)
+        held = held.reshape((-1,) + held.shape[2:])
+        bits.remove(bit)
+    return held[0]
 
 
 def flipped(values):
@@ -258,31 +364,56 @@
     half = source_ids.shape[1]
     spot_share = score_places.shape[1]
 
+    share = width // groups
+    feature = jnp.arange(width)
+    home = (feature // share ^ group) * share + feature % share
+    order = home[:, None] == feature[None, :]
+
+    def reordered(values):
+        return product(values, order.astype(low))
+
+    def reordered_exact(values):
+        return jnp.dot(
+            values,
+            order.astype(jnp.float32),
+            precision=lax.Precision.HIGHEST,
+            preferred_element_type=jnp.float32,
+        )
+
+    gains = reordered_exact(norm_gains)
     blocks = entry_weight.shape[3]
     entry_low = entry_weight.astype(low)
     leave_low = flipped(exit_weight.astype(low))
     place_low = flipped(place_table.astype(low))
-    place_low = jnp.pad(place_low, ((0, 0), (0, 0), (0, blocks - half)))
     expand_low = expand_weight.astype(low)
     shrink_low = flipped(reduce_weight.astype(low))
-    narrow = gather_weights(
-        jnp.concatenate(
-            [
-                entry_low[0],
-                leave_low[:1],
-                entry_low[1],
-                leave_low[1:2],
-                entry_low[2],
-                leave_low[2:],
-                place_low,
-            ]
+    wide = expand_low.shape[2]
+
+    def beside(*pieces):
+        return jnp.concatenate(pieces, axis=1)
+
+    first_two = [
+        gather_weights(
+            beside(entry_low[a, 0], entry_low[a, 1], entry_low[a, 2], leave_low[a], place_low[a]), a
         )
-    )
-    attend_weights = [[narrow[4 * a + b] for b in range(4)] for a in range(3)]
-    places = flipped(narrow[12:14, :, :half])
-    feed_weights = [
-        gather_weights(jnp.stack([expand_low[b], shrink_low[b]])) for b in range(2)
+        for a in range(2)
     ]
+    next_one = gather_weights(beside(expand_low[0], entry_low[2, 0], entry_low[2, 1]), 0)
+    next_two = gather_weights(beside(shrink_low[0], entry_low[2, 2], leave_low[2]), 1)
+    last_two = [gather_weights(expand_low[1], 0), gather_weights(shrink_low[1], 1)]
+
+    def pieces_of(values, first, count):
+        return [
+            values[:, first + b * blocks : first + (b + 1) * blocks] for b in range(count)
+        ]
+
+    attend_weights = [
+        pieces_of(first_two[0], 0, 4),
+        pieces_of(first_two[1], 0, 4),
+        pieces_of(next_one, wide, 2) + pieces_of(next_two, wide, 2),
+    ]
+    feed_weights = [(next_one[:, :wide], next_two[:, :wide]), last_two]
+    places = jnp.stack([flipped(values[:, 4 * blocks :]) for values in first_two])
 
     ids = jnp.concatenate([source_ids[0], target_ids[0]])
     owner, rank, leads = request_slots(ids, rows_owned)
@@ -344,43 +475,50 @@
         ),
         (jnp.int32(1), start),
     )[1]
-    start = start.reshape(2, half, width) + places.astype(jnp.float32)
+    start = reordered(start.astype(low)).reshape(2, half, width) + places.astype(jnp.float32)
 
     row_places = jnp.concatenate(
         [part * half + jnp.arange(half), (1 - part) * half + jnp.arange(half)]
     )
     length = row_places.shape[0]
+    spots_group = lax.dynamic_index_in_dim(
+        spots_all.reshape(groups, parts, spot_share), group, 0, False
+    )
+    spots_group = spots_group.reshape(-1)
     encoder_mask = jnp.broadcast_to(row_places[None, :] < source_lengths[0], (length, length))
-    decoder_mask = (row_places[None, :] <= row_places[:, None]) & (
+    cross_mask = encoder_mask[: spots_group.shape[0]]
+    decoder_mask = (row_places[None, :] <= spots_group[:, None]) & (
         row_places[None, :] < target_lengths[0]
     )
+    scored_row = spots_group[:, None] == row_places[None, :]
     stream = start[0]
-    output, enc_attend = attention_forward(
-        stream, norm_gains[0], attend_weights[0], encoder_mask, None
-    )
+    output, enc_attend = encode_attention(stream, gains[0], attend_weights[0], encoder_mask)
     stream = stream + output
-    decoded = start[1]
-    output, dec_self = attention_forward(
-        decoded, norm_gains[3], attend_weights[1], decoder_mask, None
+    target_rows = spread(start[1])
+    target_normed = norm_rows(target_rows, gains[3]).astype(low)
+    decoded = place_exact(scored_row, target_rows)
+    output, dec_self = decode_attention(
+        pick_rows(scored_row.astype(low), target_normed),
+        target_normed,
+        attend_weights[1],
+        decoder_mask,
     )
     decoded = decoded + output
-    output, enc_feed = feed_forward(stream, norm_gains[1], feed_weights[0])
+    output, enc_feed = feed_forward(stream, gains[1], feed_weights[0])
     stream = stream + output
-    memory = spread(norm_rows(stream, norm_gains[2]).astype(low))
-    output, dec_cross = attention_forward(
-        decoded, norm_gains[4], attend_weights[2], encoder_mask, memory
-    )
-    decoded = decoded + output
-    output, dec_feed = feed_forward(decoded, norm_gains[5], feed_weights[1])
-    decoded = decoded + output
-    final = spread(norm_rows(decoded, norm_gains[6]).astype(low))
-
-    picked_own = product(
-        (spots[:, None] == row_places[None, :]).astype(low), final
-    ).astype(low)
+    memory = spread(norm_rows(stream, gains[2]).astype(low))
+    after_self = decoded
+    output, dec_cross = decode_attention(
+        norm_rows(after_self, gains[4]).astype(low), memory, attend_weights[2], cross_mask
+    )
+    after_cross = after_self + output
+    output, dec_feed = decode_feed(norm_rows(after_cross, gains[5]).astype(low), feed_weights[1])
+    after_feed = after_cross + output
+    final = norm_rows(after_feed, gains[6]).astype(low)
+
+    picked_own = reordered(own_half(final)).astype(low)
     picked_group = to_all(picked_own, "dp")
     picked = jnp.concatenate([picked_group, swap(picked_group)]).reshape(-1, width)
-    scored = picked.shape[0]
 
     def own_first(values):
         values = values.reshape(groups, parts, spot_share)
@@ -421,43 +559,42 @@
     grad_picked = lax.all_to_all(
         grad_picked.astype(low).reshape(groups, spot_share, width), "dp", 0, 0, tiled=True
     )
-    grad_picked = spread(jnp.sum(grad_picked.astype(jnp.float32), axis=0))
-    spots_group = own_first(spots_all).reshape(parts, groups, spot_share)
-    spots_group = lax.dynamic_index_in_dim(spots_group, group, 1, False).reshape(-1)
-    grad_final = jnp.dot(
-        (row_places[:half, None] == spots_group[None, :]).astype(jnp.float32),
-        grad_picked,
-        precision=lax.Precision.HIGHEST,
-        preferred_element_type=jnp.float32,
-    )
+    grad_picked = reordered(grad_picked.reshape(-1, width)).reshape(groups, spot_share, width)
+    grad_picked = in_order(jnp.sum(grad_picked, axis=0))
     grad_table = product_tn(grad_logits, picked)
 
-    grad_decoded, gain_six = jax.vjp(norm_rows, decoded, norm_gains[6])[1](grad_final)
-    saved_decoded = dec_feed[0]
-    grad_decoded, gain_five, feed_one = feed_backward(
-        grad_decoded, norm_gains[5], feed_weights[1], dec_feed
-    )
-    feed_one = scatter_grads(feed_one)
-    grad_decoded, gain_four, attend_two, grad_memory = attention_backward(
-        grad_decoded, norm_gains[4], attend_weights[2], encoder_mask, memory, dec_cross
-    )
-    grad_stream, gain_two = jax.vjp(norm_rows, stream, norm_gains[2])[1](grad_memory)
+    grad_normed = grad_picked
+    grad_rows, gain_six = norm_backward_shared(after_feed, gains[6], grad_normed)
+    grad_normed, feed_one = decode_feed_backward(grad_rows, feed_weights[1], dec_feed)
+    feed_one = [scatter_grads(feed_one[b], b) for b in range(2)]
+    grad_values, gain_five = norm_backward_shared(after_cross, gains[5], grad_normed)
+    grad_rows = grad_rows + grad_values
+    back_rows, back_source, attend_two = decode_attention_backward(
+        grad_rows, attend_weights[2], cross_mask, dec_cross
+    )
+    cross_grads = [scatter_grads(beside(*attend_two[2 * b : 2 * b + 2]), b) for b in range(2)]
+    grad_stream, gain_two = norm_backward(stream, gains[2], collect(back_source))
     grad_stream, gain_one, feed_zero = feed_backward(
-        grad_stream, norm_gains[1], feed_weights[0], enc_feed
-    )
-    feed_zero = scatter_grads(feed_zero)
-    grad_decoded, gain_three, attend_one, unused_one = attention_backward(
-        grad_decoded, norm_gains[3], attend_weights[1], decoder_mask, None, dec_self
-    )
-    middle = scatter_grads(attend_two + attend_one)
-    grad_stream, gain_zero, attend_zero, unused_zero = attention_backward(
-        grad_stream, norm_gains[0], attend_weights[0], encoder_mask, None, enc_attend
-    )
-    grad_start = jnp.stack([grad_stream, grad_decoded]).astype(low)
-    place_grads = jnp.pad(flipped(grad_start), ((0, 0), (0, 0), (0, blocks - half)))
-    last = scatter_grads(attend_zero + (place_grads[0], place_grads[1]))
-
-    start_rows = grad_start.reshape(2 * half, width)
+        grad_stream, gains[1], feed_weights[0], enc_feed
+    )
+    feed_zero = [scatter_grads(feed_zero[b], b) for b in range(2)]
+    grad_values, gain_four = norm_backward_shared(after_self, gains[4], both(back_rows))
+    grad_rows = grad_rows + grad_values
+    back_rows, back_source, attend_one = decode_attention_backward(
+        grad_rows, attend_weights[1], decoder_mask, dec_self
+    )
+    back_source = back_source + place_exact(scored_row.T, back_rows)
+    grad_decoded, gain_three = norm_backward(start[1], gains[3], collect(back_source))
+    grad_decoded = grad_decoded + place_exact(scored_row[:, :half].T, grad_rows)
+    start_decoded = grad_decoded.astype(low)
+    self_grads = scatter_grads(beside(*attend_one, flipped(start_decoded)), 0)
+    grad_stream, gain_zero, attend_zero = encode_attention_backward(
+        grad_stream, gains[0], attend_weights[0], encoder_mask, enc_attend
+    )
+    start_stream = grad_stream.astype(low)
+    first_grads = scatter_grads(beside(*attend_zero, flipped(start_stream)), 1)
+
+    start_rows = reordered(jnp.concatenate([start_stream, start_decoded])).astype(low)
 
     def returned(asked, slot):
         sent = product_tn(chosen_rows(slot, slots_all), start_rows).astype(low)
@@ -479,14 +616,22 @@
     gain_partial = jnp.stack(
         [gain_zero, gain_one, gain_two, gain_three, gain_four, gain_five, gain_six]
     )
+    gain_partial = reordered_exact(gain_partial)
     gain_own = jnp.sum(
         lax.all_to_all(gain_partial.reshape(devices, -1), EVERY, 0, 0, tiled=True), axis=0
     )
-    entry_grad = jnp.stack([last[:3], middle[4:7], middle[:3]])
-    leave_grad = flipped(jnp.stack([last[3], middle[7], middle[3]]))
+    first_pieces = pieces_of(first_grads, 0, 4)
+    self_pieces = pieces_of(self_grads, 0, 4)
+    cross_pieces = pieces_of(cross_grads[0], 0, 2) + pieces_of(cross_grads[1], 0, 2)
+    entry_grad = jnp.stack(
+        [jnp.stack(pieces[:3]) for pieces in (first_pieces, self_pieces, cross_pieces)]
+    )
+    leave_grad = flipped(jnp.stack([first_pieces[3], self_pieces[3], cross_pieces[3]]))
     expand_grad = jnp.stack([feed_zero[0], feed_one[0]])
     shrink_grad = flipped(jnp.stack([feed_zero[1], feed_one[1]]))
-    place_grad = flipped(last[4:6, :, :half])
+    place_grad = flipped(
+        jnp.stack([first_grads[:, 4 * blocks :], self_grads[:, 4 * blocks :]])
+    )
     squares = jnp.sum(gain_own * gain_own)
     for grad in (entry_grad, leave_grad, expand_grad, shrink_grad, table_grad, place_grad):
         squares = squares + jnp.sum(grad * grad)

time: 1160 us -> 882 us (0.76)
  waiting for transfers between devices: 629 us -> 330 us
  starting transfers between devices: 29.5 us -> 95.8 us
  matrix products: 240 us -> 186 us
  other arithmetic: 104 us -> 140 us
  blocking collectives: 50.4 us -> 14.5 us
  local copies, waits for them, and re-layouts: 59.7 us -> 86.2 us
  between operations: 31.6 us -> 18.7 us
    reduce_scatter x4 -> x0, waiting for transfers between devices: 347 us -> none  [scatter_grads(): lax.psum_scatter(stacked, 'dp', scatter_dimension=1, tiled=True)]
    ppermute x0 -> x56, waiting for transfers between devices: none -> 259 us  [swap_bit(): return lax.ppermute(values, 'dp', pairs)]
    all_gather x3 -> x0, waiting for transfers between devices: 132 us -> none  [gather_weights(): return lax.all_gather(shards, 'dp', axis=1, tiled=True)]
    ppermute x0 -> x56, starting transfers between devices: none -> 64.2 us  [swap_bit(): return lax.ppermute(values, 'dp', pairs)]
    all_to_all x1, waiting for transfers between devices: 56.2 us -> 0.01 us  [looked_up(): lax.all_to_all(sent.reshape(devices, SLOTS, width), EVERY, 0, 0, tiled=True)]
    all_to_all x1, waiting for transfers between devices: 52.1 us -> 2.58 us  [returned(): lax.all_to_all(sent.reshape(devices, SLOTS, width), EVERY, 0, 0, tiled=True)]
    another operation x6 -> x51, other arithmetic: 7.02 us -> 39.3 us  [the longest x26 26.1 us: gather_weights(): held = jnp.stack([held.reshape(shape), got.reshape(shape)], axis=1)]
    all_to_all x1 -> x0, blocking collectives: 24.7 us -> none  [local(): lax.all_to_all(grad_picked.astype(low).reshape(groups, spot_share, width)...]
  transfers between devices with their start and end apart: 39 -> 83, of which waited for: 24 -> 39; matrix products, arithmetic and copies ran while one was open for 22% -> 34% of each run, Pallas kernels for 0% -> 0%
where the time goes in v2:
time: 882 us; the launch traced here: 873 us
  waiting for transfers between devices  330 us (37%)
  matrix products  186 us (21%)
  other arithmetic  140 us (16%)
  starting transfers between devices  95.8 us (11%)
  local copies, waits for them, and re-layouts  86.2 us (10%)
  between operations  18.7 us (2%)
  blocking collectives  14.5 us (2%)
    ppermute x56, waiting for transfers between devices, swap_bit(): return lax.ppermute(values, 'dp', pairs)  259 us
    ppermute x56, starting transfers between devices, swap_bit(): return lax.ppermute(values, 'dp', pairs)  64.2 us
    dot_general x24, matrix products, product(): return jnp.dot(left, right, preferred_element_type=jnp.float32)  54.4 us
    dot_general x19, matrix products, product_tn(): lax.dot_general(left, right, (((0,), (0,)), ((), ())), preferred_element_...  35.6 us
    dot_general x17, matrix products, product_nt(): lax.dot_general(left, right, (((1,), (1,)), ((), ())), preferred_element_...  27.6 us
    another operation x26, other arithmetic, gather_weights(): held = jnp.stack([held.reshape(shape), got.reshape(shape)], axis=1)  26.1 us
    all_to_all x2, waiting for transfers between devices, to_all(): lax.all_to_all(jnp.broadcast_to(values[None], (size,) + values.shape), ax...  25.6 us
    unnamed x510, local copies, waits for them, and re-layouts  24 us
  transfers between devices with their start and end apart: 83, of which 39 were waited for; matrix products, arithmetic and copies ran while one was open for 34% of the time, Pallas kernels for 0%

profile of v2, /device:TPU:0, one launch (start us, length us, event | category | flops | bytes accessed | tf_op | source)
XLA Modules:
  0.0 872.5 jit_solution(1363688935780783612)
XLA Ops:
  25.4 3.8 all-to-all-start.4
  29.8 4.0 convert_element_type.824
  37.4 6.0 fusion.105
  45.4 5.2 collective-permute-done.28
  61.3 4.3 collective-permute-done.25
  65.7 10.6 %collective-permute-done.29 = bf16[2,48,1536]{2,1,0:T(8,128)(2,1)S(1)} collective-permute-done((bf16[2,48,1536]{2,1,0:T(8,128)(2,1)S(1)}, bf16[2,48,1536]{2,1,0:T(8,128)(2,1)S(1)}, u32[]{:S(2)}, u32[]{:S(2)}) %collective-permute-start.29) | collective-permute-done | bytes 294944 | tf_op jit(solution)/shard_map/ppermute | solution.py:270
  77.2 15.9 %collective-permute-done.5 = bf16[2,48,1792]{2,1,0:T(8,128)(2,1)S(1)} collective-permute-done((bf16[2,48,1792]{2,1,0:T(8,128)(2,1)S(1)}, bf16[2,48,1792]{2,1,0:T(8,128)(2,1)S(1)}, u32[]{:S(2)}, u32[]{:S(2)}) %collective-permute-start.5) | collective-permute-done | bytes 344096 | tf_op jit(solution)/shard_map/ppermute | solution.py:270
  95.4 5.3 collective-permute-done.18
  113.0 4.5 collective-permute-done.6
  124.2 6.4 collective-permute-done.2
  132.7 16.2 %collective-permute-done.19 = bf16[4,48,2304]{2,1,0:T(8,128)(2,1)S(1)} collective-permute-done((bf16[4,48,2304]{2,1,0:T(8,128)(2,1)}, bf16[4,48,2304]{2,1,0:T(8,128)(2,1)S(1)}, u32[]{:S(2)}, u32[]{:S(2)}) %collective-permute-start.19) | collective-permute-done | bytes 884768 | tf_op jit(solution)/shard_map/ppermute | solution.py:270
  157.1 27.2 %collective-permute-done.7 = bf16[8,48,1792]{2,1,0:T(8,128)(2,1)S(1)} collective-permute-done((bf16[8,48,1792]{2,1,0:T(8,128)(2,1)S(1)}, bf16[8,48,1792]{2,1,0:T(8,128)(2,1)S(1)}, u32[]{:S(2)}, u32[]{:S(2)}) %collective-permute-start.7) | collective-permute-done | bytes 1376288 | tf_op jit(solution)/shard_map/ppermute | solution.py:270
  188.1 15.7 %collective-permute-done.3 = bf16[8,48,1792]{2,1,0:T(8,128)(2,1)} collective-permute-done((bf16[8,48,1792]{2,1,0:T(8,128)(2,1)S(1)}, bf16[8,48,1792]{2,1,0:T(8,128)(2,1)}, u32[]{:S(2)}, u32[]{:S(2)}) %collective-permute-start.3) | collective-permute-done | bytes 1376288 | tf_op jit(solution)/shard_map/ppermute | solution.py:270
  207.4 3.6 fusion.95
  215.8 28.9 %collective-permute-done.20 = bf16[8,48,2304]{2,1,0:T(8,128)(2,1)} collective-permute-done((bf16[8,48,2304]{2,1,0:T(8,128)(2,1)}, bf16[8,48,2304]{2,1,0:T(8,128)(2,1)}, u32[]{:S(2)}, u32[]{:S(2)}) %collective-permute-start.20) | collective-permute-done | bytes 1769504 | tf_op jit(solution)/shard_map/ppermute | solution.py:270
  278.7 9.3 %multiply_convert_fusion.2 = (bf16[512,1536]{1,0:T(8,128)(2,1)S(1)}, f32[512,1536]{1,0:T(8,128)}, f32[512,1536]{1,0:T(8,128)}) fusion(bf16[768,2304]{1,0:T(8,128)(2,1)S(1)} %bitcast.870, bf16[256,768]{1,0:T(8,128)(2,1)S(1)} %collective-permute-done.12, bf16[256,768]{1,0:T(8,128)(2,1)S(1)} %multiply_convert_fusion.5), kind=kOutput, calls=%fused_computation.109 | convolution fusion | flops 1260650496 | bytes 11010048 | tf_op jit(solution)/shard_map/dot_general | solution.py:47
  319.6 4.7 all-to-all-start.6
  324.3 20.1 %all-to-all-done.6 = bf16[16,32,768]{2,1,0:T(8,128)(2,1)} async-done(((bf16[16,32,768]{2,1,0:T(8,128)(2,1)}), bf16[16,32,768]{2,1,0:T(8,128)(2,1)}, u32[]{:S(2)}, u32[]{:S(2)}) %all-to-all-start.6) | async-done | bytes 786464 | tf_op jit(solution)/shard_map/all_to_all | solution.py:41
  361.4 14.5 %all_to_all.116 = f32[32,2,1024]{2,1,0:T(2,128)S(1)} all-to-all(f32[32,2,1024]{2,1,0:T(2,128)S(1)} %broadcast_in_dim.320), channel_id=1, replica_groups=mesh['dp'=16,'tensor'=2] {'dp','tensor'}, dimensions={0} | all-to-all | bytes 524288 | tf_op jit(solution)/shard_map/all_to_all | solution.py:41
  383.8 6.5 fusion.390
  400.7 4.5 all-to-all-start.8
  410.5 14.9 %all-to-all-done.8 = bf16[16,32,768]{2,1,0:T(8,128)(2,1)} async-done(((bf16[16,32,768]{2,1,0:T(8,128)(2,1)}), bf16[16,32,768]{2,1,0:T(8,128)(2,1)}, u32[]{:S(2)}, u32[]{:S(2)}) %all-to-all-start.8) | async-done | bytes 786464 | tf_op jit(solution)/shard_map/all_to_all | solution.py:559
  447.9 4.5 convolution_convert_fusion.23
  452.4 4.4 convolution_convert_fusion.33
  493.5 4.5 convolution_convert_fusion.19
  498.0 3.8 convolution_convert_fusion.32
  543.4 4.2 collective-permute-done.55
  562.1 8.5 collective-permute-done.66
  572.2 13.7 %collective-permute-done.74 = bf16[1,2,48,1536]{3,2,1,0:T(8,128)(2,1)S(1)} collective-permute-done((bf16[1,2,48,1536]{3,2,1,0:T(8,128)(2,1)S(1)}, bf16[1,2,48,1536]{3,2,1,0:T(8,128)(2,1)S(1)}, u32[]{:S(2)}, u32[]{:S(2)}) %collective-permute-start.74) | collective-permute-done | bytes 294944 | tf_op jit(solution)/shard_map/ppermute | solution.py:270
  590.3 5.5 collective-permute-done.67
  603.6 12.7 %fusion.132 = bf16[6,64,512]{2,1,0:T(8,128)(2,1)} fusion(bf16[512,6,64]{0,2,1:T(8,128)(2,1)S(1)} %bitcast.974, f32[6,512,512]{1,2,0:T(8,128)} %fusion.434, f32[6,512,512]{1,2,0:T(8,128)} %copy-done, f32[6,512]{1,0:T(8,128)S(1)} %copy-done.151, pred[512]{0:T(512)(128)(4,1)S(1)} %copy-done.186), kind=kOutput, calls=%fused_computation.232 | convolution fusion | flops 218828288 | bytes 13382144 | tf_op jit(solution)/shard_map/hqk,khd->qhd/dot_general | solution.py:98
  618.1 13.5 %fusion.135 = bf16[6,64,512]{2,1,0:T(8,128)(2,1)} fusion(bf16[512,6,64]{0,2,1:T(8,128)(2,1)} %bitcast.972, f32[6,512,512]{1,2,0:T(8,128)} %fusion.434, f32[6,512,512]{1,2,0:T(8,128)} %copy-done, f32[6,512]{1,0:T(8,128)S(1)} %copy-done.151, pred[512]{0:T(512)(128)(4,1)S(1)} %copy-done.186), kind=kOutput, calls=%fused_computation.233 | convolution fusion | flops 218828288 | bytes 13382144 | tf_op jit(solution)/shard_map/hqk,qhd->khd/dot_general | solution.py:101
  648.0 8.0 collective-permute-done.61
  668.6 4.5 copy.409
  677.6 4.5 copy.407
  687.5 4.2 all-to-all-start.9
  695.2 20.9 %all-to-all-done.9 = f32[32,1,168]{2,1,0:T(1,128)S(1)} async-done(((f32[32,1,168]{2,1,0:T(1,128)}), f32[32,1,168]{2,1,0:T(1,128)S(1)}, u32[]{:S(2)}, u32[]{:S(2)}) %all-to-all-start.9) | async-done | bytes 21536 | tf_op jit(solution)/shard_map/all_to_all | solution.py:621
  723.0 6.4 collective-permute-done.71
  736.8 12.5 %collective-permute-done.49 = bf16[4,1,48,1792]{3,2,0,1:T(8,128)(2,1)S(1)} collective-permute-done((bf16[4,1,48,1792]{3,2,0,1:T(8,128)(2,1)S(1)}, bf16[4,1,48,1792]{3,2,0,1:T(8,128)(2,1)S(1)}, u32[]{:S(2)}, u32[]{:S(2)}) %collective-permute-start.49) | collective-permute-done | bytes 688160 | tf_op jit(solution)/shard_map/ppermute | solution.py:270
  752.2 9.4 %collective-permute-done.50 = bf16[2,1,48,1792]{3,2,0,1:T(8,128)(2,1)S(1)} collective-permute-done((bf16[2,1,48,1792]{3,2,0,1:T(8,128)(2,1)S(1)}, bf16[2,1,48,1792]{3,2,0,1:T(8,128)(2,1)S(1)}, u32[]{:S(2)}, u32[]{:S(2)}) %collective-permute-start.50) | collective-permute-done | bytes 344096 | tf_op jit(solution)/shard_map/ppermute | solution.py:270
  762.4 11.3 %collective-permute-done.46 = bf16[1,2,48,1792]{3,2,1,0:T(8,128)(2,1)S(1)} collective-permute-done((bf16[1,2,48,1792]{3,2,1,0:T(8,128)(2,1)S(1)}, bf16[1,2,48,1792]{3,2,1,0:T(8,128)(2,1)S(1)}, u32[]{:S(2)}, u32[]{:S(2)}) %collective-permute-start.46) | collective-permute-done | bytes 344096 | tf_op jit(solution)/shard_map/ppermute | solution.py:270
  781.1 26.8 %collective-permute-done.47 = bf16[1,1,48,1792]{3,2,1,0:T(8,128)(2,1)S(1)} collective-permute-done((bf16[1,1,48,1792]{3,2,1,0:T(8,128)(2,1)S(1)}, bf16[1,1,48,1792]{3,2,1,0:T(8,128)(2,1)S(1)}, u32[]{:S(2)}, u32[]{:S(2)}) %collective-permute-start.47) | collective-permute-done | bytes 172064 | tf_op jit(solution)/shard_map/ppermute | solution.py:270
  815.9 5.2 fusion.37
  821.2 8.9 %convolution_add_fusion = f32[1572,768]{1,0:T(8,128)} fusion(f32[1572,768]{1,0:T(8,128)S(1)} %fusion.37, bf16[1024,768]{1,0:T(8,128)(2,1)S(1)} %bitcast.926, f32[1024,1572]{0,1:T(8,128)} %copy-done.32, f32[1024]{0:T(1024)S(1)} %copy-done.206, f32[1024]{0:T(1024)S(1)} %copy-done.207, s32[1024]{0:T(1024)S(1)} %copy-done.180), kind=kOutput, calls=%fused_computation.89 | convolution fusion | flops 2483407872 | bytes 17682432 | tf_op jit(solution)/shard_map/dot_general | solution.py:51
  831.1 4.3 multiply_reduce_fusion.1
  837.4 4.0 all-to-all-start.11
  843.2 5.5 all-to-all-done.11
  859.6 9.0 %multiply_subtract_fusion = (f32[1572,768]{1,0:T(8,128)}, f32[1572,768]{1,0:T(8,128)}, f32[1572,768]{1,0:T(8,128)}) fusion(f32[1572,768]{1,0:T(8,128)S(1)} %bitcast.819, f32[]{:T(128)} %bitcast.307, f32[]{:T(128)} %bitcast.306, f32[1572,768]{1,0:T(8,128)S(1)} %bitcast.821, f32[]{:T(128)S(6)} %min.3, f32[1572,768]{1,0:T(8,128)} %param.58, f32[1572,768]{1,0:T(8,128)} %param.57), kind=kLoop, calls=%fused_computation.82 | loop fusion | flops 19316736 | bytes 33804300 | tf_op jit(solution)/shard_map/sub | solution.py:252
  (1037 shorter events, 400.7 us)
Async XLA Ops:
  3.9 47.1 %collective-permute-start.4 = (bf16[1,48,1792]{2,1,0:T(8,128)(2,1)S(1)}, bf16[1,48,1792]{2,1,0:T(8,128)(2,1)S(1)}, u32[]{:S(2)}, u32[]{:S(2)}) collective-permute-start(bf16[1,48,1792]{2,1,0:T(8,128)(2,1)S(1)} %bitcast.999), channel_id=1, source_target_pairs={{0,8},{2,10},{4,12},{6,14},{8,0},{10,2},{12,4},{14,6},{16,24},{18,... | collective-permute-start | bytes 516104 | tf_op jit(solution)/shard_map/ppermute | solution.py:270
  6.9 47.3 %collective-permute-start = (bf16[1,48,1792]{2,1,0:T(8,128)(2,1)S(1)}, bf16[1,48,1792]{2,1,0:T(8,128)(2,1)}, u32[]{:S(2)}, u32[]{:S(2)}) collective-permute-start(bf16[1,48,1792]{2,1,0:T(8,128)(2,1)S(1)} %bitcast.997), channel_id=1, source_target_pairs={{0,16},{2,18},{4,20},{6,22},{8,24},{10,26},{12,28},{14,30},{16,0},... | collective-permute-start | bytes 516104 | tf_op jit(solution)/shard_map/ppermute | solution.py:270
  9.7 46.9 %collective-permute-start.17 = (bf16[1,48,2304]{2,1,0:T(8,128)(2,1)S(1)}, bf16[1,48,2304]{2,1,0:T(8,128)(2,1)}, u32[]{:S(2)}, u32[]{:S(2)}) collective-permute-start(bf16[1,48,2304]{2,1,0:T(8,128)(2,1)S(1)} %get-tuple-element.774), channel_id=1, source_target_pairs={{0,8},{2,10},{4,12},{6,14},{8,0},{10,2},{12,4},{14,6},{16,24},{18,... | collective-permute-start | bytes 663560 | tf_op jit(solution)/shard_map/ppermute | solution.py:270
  11.0 48.4 %collective-permute-start.13 = (bf16[1,48,2304]{2,1,0:T(8,128)(2,1)}, bf16[1,48,2304]{2,1,0:T(8,128)(2,1)S(1)}, u32[]{:S(2)}, u32[]{:S(2)}) collective-permute-start(bf16[1,48,2304]{2,1,0:T(8,128)(2,1)} %get-tuple-element.772), channel_id=1, source_target_pairs={{0,16},{2,18},{4,20},{6,22},{8,24},{10,26},{12,28},{14,30},{16,0},... | collective-permute-start | bytes 663560 | tf_op jit(solution)/shard_map/ppermute | solution.py:270
  11.1 33.7 %collective-permute-start.24 = (bf16[1,48,1536]{2,1,0:T(8,128)(2,1)S(1)}, bf16[1,48,1536]{2,1,0:T(8,128)(2,1)S(1)}, u32[]{:S(2)}, u32[]{:S(2)}) collective-permute-start(bf16[1,48,1536]{2,1,0:T(8,128)(2,1)S(1)} %get-tuple-element.768), channel_id=1, source_target_pairs={{0,16},{2,18},{4,20},{6,22},{8,24},{10,26},{12,28},{14,30},{16,0},... | collective-permute-start | bytes 442376 | tf_op jit(solution)/shard_map/ppermute | solution.py:270
  51.7 24.6 %collective-permute-start.29 = (bf16[2,48,1536]{2,1,0:T(8,128)(2,1)S(1)}, bf16[2,48,1536]{2,1,0:T(8,128)(2,1)S(1)}, u32[]{:S(2)}, u32[]{:S(2)}) collective-permute-start(bf16[2,48,1536]{2,1,0:T(8,128)(2,1)S(1)} %get-tuple-element.761), channel_id=1, source_target_pairs={{0,16},{2,18},{4,20},{6,22},{8,24},{10,26},{12,28},{14,30},{16,0},... | collective-permute-start | bytes 884744 | tf_op jit(solution)/shard_map/ppermute | solution.py:270
  54.3 38.8 %collective-permute-start.5 = (bf16[2,48,1792]{2,1,0:T(8,128)(2,1)S(1)}, bf16[2,48,1792]{2,1,0:T(8,128)(2,1)S(1)}, u32[]{:S(2)}, u32[]{:S(2)}) collective-permute-start(bf16[2,48,1792]{2,1,0:T(8,128)(2,1)S(1)} %get-tuple-element.750), channel_id=1, source_target_pairs={{0,16},{2,18},{4,20},{6,22},{8,24},{10,26},{12,28},{14,30},{16,0},... | collective-permute-start | bytes 1032200 | tf_op jit(solution)/shard_map/ppermute | solution.py:270
  56.6 37.4 %collective-permute-start.1 = (bf16[2,48,1792]{2,1,0:T(8,128)(2,1)S(1)}, bf16[2,48,1792]{2,1,0:T(8,128)(2,1)S(1)}, u32[]{:S(2)}, u32[]{:S(2)}) collective-permute-start(bf16[2,48,1792]{2,1,0:T(8,128)(2,1)S(1)} %get-tuple-element.748), channel_id=1, source_target_pairs={{0,8},{2,10},{4,12},{6,14},{8,0},{10,2},{12,4},{14,6},{16,24},{18,... | collective-permute-start | bytes 1032200 | tf_op jit(solution)/shard_map/ppermute | solution.py:270
  59.4 41.2 %collective-permute-start.18 = (bf16[2,48,2304]{2,1,0:T(8,128)(2,1)S(1)}, bf16[2,48,2304]{2,1,0:T(8,128)(2,1)S(1)}, u32[]{:S(2)}, u32[]{:S(2)}) collective-permute-start(bf16[2,48,2304]{2,1,0:T(8,128)(2,1)S(1)} %get-tuple-element.738), channel_id=1, source_target_pairs={{0,16},{2,18},{4,20},{6,22},{8,24},{10,26},{12,28},{14,30},{16,0},... | collective-permute-start | bytes 1327112 | tf_op jit(solution)/shard_map/ppermute | solution.py:270
  65.6 40.4 %collective-permute-start.14 = (bf16[2,48,2304]{2,1,0:T(8,128)(2,1)}, bf16[2,48,2304]{2,1,0:T(8,128)(2,1)}, u32[]{:S(2)}, u32[]{:S(2)}) collective-permute-start(bf16[2,48,2304]{2,1,0:T(8,128)(2,1)} %get-tuple-element.736), channel_id=1, source_target_pairs={{0,8},{2,10},{4,12},{6,14},{8,0},{10,2},{12,4},{14,6},{16,24},{18,... | collective-permute-start | bytes 1327112 | tf_op jit(solution)/shard_map/ppermute | solution.py:270
  76.3 32.7 %collective-permute-start.26 = (bf16[4,48,1536]{2,1,0:T(8,128)(2,1)S(1)}, bf16[4,48,1536]{2,1,0:T(8,128)(2,1)}, u32[]{:S(2)}, u32[]{:S(2)}) collective-permute-start(bf16[4,48,1536]{2,1,0:T(8,128)(2,1)S(1)} %bitcast.905), channel_id=1, source_target_pairs={{0,4},{2,6},{4,0},{6,2},{8,12},{10,14},{12,8},{14,10},{16,20},{18,... | collective-permute-start | bytes 1769480 | tf_op jit(solution)/shard_map/ppermute | solution.py:270
  93.1 28.4 %collective-permute-start.30 = (bf16[4,48,1536]{2,1,0:T(8,128)(2,1)S(1)}, bf16[4,48,1536]{2,1,0:T(8,128)(2,1)}, u32[]{:S(2)}, u32[]{:S(2)}) collective-permute-start(bf16[4,48,1536]{2,1,0:T(8,128)(2,1)S(1)} %bitcast.899), channel_id=1, source_target_pairs={{0,2},{2,0},{4,6},{6,4},{8,10},{10,8},{12,14},{14,12},{16,18},{18,... | collective-permute-start | bytes 1769480 | tf_op jit(solution)/shard_map/ppermute | solution.py:270
  94.0 23.5 %collective-permute-start.6 = (bf16[4,48,1792]{2,1,0:T(8,128)(2,1)S(1)}, bf16[4,48,1792]{2,1,0:T(8,128)(2,1)}, u32[]{:S(2)}, u32[]{:S(2)}) collective-permute-start(bf16[4,48,1792]{2,1,0:T(8,128)(2,1)S(1)} %bitcast.897), channel_id=1, source_target_pairs={{0,2},{2,0},{4,6},{6,4},{8,10},{10,8},{12,14},{14,12},{16,18},{18,... | collective-permute-start | bytes 2064392 | tf_op jit(solution)/shard_map/ppermute | solution.py:270
  100.6 30.1 %collective-permute-start.2 = (bf16[4,48,1792]{2,1,0:T(8,128)(2,1)S(1)}, bf16[4,48,1792]{2,1,0:T(8,128)(2,1)}, u32[]{:S(2)}, u32[]{:S(2)}) collective-permute-start(bf16[4,48,1792]{2,1,0:T(8,128)(2,1)S(1)} %bitcast.895), channel_id=1, source_target_pairs={{0,4},{2,6},{4,0},{6,2},{8,12},{10,14},{12,8},{14,10},{16,20},{18,... | collective-permute-start | bytes 2064392 | tf_op jit(solution)/shard_map/ppermute | solution.py:270
  102.4 105.0 %all-to-all-start.5 = ((bf16[32,32,768]{2,1,0:T(8,128)(2,1)}), bf16[32,32,768]{2,1,0:T(8,128)(2,1)}, u32[]{:S(2)}, u32[]{:S(2)}) async-start(bf16[32,32,768]{2,1,0:T(8,128)(2,1)} %bitcast.927), calls=%async_computation.5 | async-start | bytes 3145728 | tf_op jit(solution)/shard_map/all_to_all | solution.py:459
  106.1 42.9 %collective-permute-start.19 = (bf16[4,48,2304]{2,1,0:T(8,128)(2,1)}, bf16[4,48,2304]{2,1,0:T(8,128)(2,1)S(1)}, u32[]{:S(2)}, u32[]{:S(2)}) collective-permute-start(bf16[4,48,2304]{2,1,0:T(8,128)(2,1)} %bitcast.100), channel_id=1, source_target_pairs={{0,2},{2,0},{4,6},{6,4},{8,10},{10,8},{12,14},{14,12},{16,18},{18,... | collective-permute-start | bytes 2654216 | tf_op jit(solution)/shard_map/ppermute | solution.py:270
  109.0 45.8 %collective-permute-start.15 = (bf16[4,48,2304]{2,1,0:T(8,128)(2,1)S(1)}, bf16[4,48,2304]{2,1,0:T(8,128)(2,1)S(1)}, u32[]{:S(2)}, u32[]{:S(2)}) collective-permute-start(bf16[4,48,2304]{2,1,0:T(8,128)(2,1)S(1)} %bitcast.892), channel_id=1, source_target_pairs={{0,4},{2,6},{4,0},{6,2},{8,12},{10,14},{12,8},{14,10},{16,20},{18,... | collective-permute-start | bytes 2654216 | tf_op jit(solution)/shard_map/ppermute | solution.py:270
  117.5 173.5 %collective-permute-start.27 = (bf16[8,48,1536]{2,1,0:T(8,128)(2,1)}, bf16[8,48,1536]{2,1,0:T(8,128)(2,1)}, u32[]{:S(2)}, u32[]{:S(2)}) collective-permute-start(bf16[8,48,1536]{2,1,0:T(8,128)(2,1)} %bitcast.119), channel_id=1, source_target_pairs={{0,2},{2,0},{4,6},{6,4},{8,10},{10,8},{12,14},{14,12},{16,18},{18,... | collective-permute-start | bytes 3538952 | tf_op jit(solution)/shard_map/ppermute | solution.py:270
  121.5 62.8 %collective-permute-start.7 = (bf16[8,48,1792]{2,1,0:T(8,128)(2,1)S(1)}, bf16[8,48,1792]{2,1,0:T(8,128)(2,1)S(1)}, u32[]{:S(2)}, u32[]{:S(2)}) collective-permute-start(bf16[8,48,1792]{2,1,0:T(8,128)(2,1)S(1)} %bitcast.949), channel_id=1, source_target_pairs={{0,4},{2,6},{4,0},{6,2},{8,12},{10,14},{12,8},{14,10},{16,20},{18,... | collective-permute-start | bytes 4128776 | tf_op jit(solution)/shard_map/ppermute | solution.py:270
  130.7 174.9 %collective-permute-start.31 = (bf16[8,48,1536]{2,1,0:T(8,128)(2,1)}, bf16[8,48,1536]{2,1,0:T(8,128)(2,1)}, u32[]{:S(2)}, u32[]{:S(2)}) collective-permute-start(bf16[8,48,1536]{2,1,0:T(8,128)(2,1)} %bitcast.131), channel_id=1, source_target_pairs={{0,4},{2,6},{4,0},{6,2},{8,12},{10,14},{12,8},{14,10},{16,20},{18,... | collective-permute-start | bytes 3538952 | tf_op jit(solution)/shard_map/ppermute | solution.py:270
  148.9 54.9 %collective-permute-start.3 = (bf16[8,48,1792]{2,1,0:T(8,128)(2,1)S(1)}, bf16[8,48,1792]{2,1,0:T(8,128)(2,1)}, u32[]{:S(2)}, u32[]{:S(2)}) collective-permute-start(bf16[8,48,1792]{2,1,0:T(8,128)(2,1)S(1)} %bitcast.876), channel_id=1, source_target_pairs={{0,2},{2,0},{4,6},{6,4},{8,10},{10,8},{12,14},{14,12},{16,18},{18,... | collective-permute-start | bytes 4128776 | tf_op jit(solution)/shard_map/ppermute | solution.py:270
  154.8 89.9 %collective-permute-start.20 = (bf16[8,48,2304]{2,1,0:T(8,128)(2,1)}, bf16[8,48,2304]{2,1,0:T(8,128)(2,1)}, u32[]{:S(2)}, u32[]{:S(2)}) collective-permute-start(bf16[8,48,2304]{2,1,0:T(8,128)(2,1)} %bitcast.103), channel_id=1, source_target_pairs={{0,4},{2,6},{4,0},{6,2},{8,12},{10,14},{12,8},{14,10},{16,20},{18,... | collective-permute-start | bytes 5308424 | tf_op jit(solution)/shard_map/ppermute | solution.py:270
  184.3 64.3 %collective-permute-start.16 = (bf16[8,48,2304]{2,1,0:T(8,128)(2,1)}, bf16[8,48,2304]{2,1,0:T(8,128)(2,1)}, u32[]{:S(2)}, u32[]{:S(2)}) collective-permute-start(bf16[8,48,2304]{2,1,0:T(8,128)(2,1)} %bitcast.86), channel_id=1, source_target_pairs={{0,2},{2,0},{4,6},{6,4},{8,10},{10,8},{12,14},{14,12},{16,18},{18,... | collective-permute-start | bytes 5308424 | tf_op jit(solution)/shard_map/ppermute | solution.py:270
  215.3 50.0 %collective-permute-start.8 = (f32[256,768]{1,0:T(8,128)S(1)}, f32[256,768]{1,0:T(8,128)S(1)}, u32[]{:S(2)}, u32[]{:S(2)}) collective-permute-start(f32[256,768]{1,0:T(8,128)S(1)} %get-tuple-element.730), channel_id=1, source_target_pairs={{0,1},{1,0},{2,3},{3,2},{4,5},{5,4},{6,7},{7,6},{8,9},{9,8},{10,11... | collective-permute-start | bytes 2359304 | tf_op jit(solution)/shard_map/ppermute | solution.py:27
  319.6 24.8 %all-to-all-start.6 = ((bf16[16,32,768]{2,1,0:T(8,128)(2,1)}), bf16[16,32,768]{2,1,0:T(8,128)(2,1)}, u32[]{:S(2)}, u32[]{:S(2)}) async-start(bf16[16,32,768]{2,1,0:T(8,128)(2,1)} %broadcast_in_dim.197), calls=%async_computation.6 | async-start | bytes 1572864 | tf_op jit(solution)/shard_map/all_to_all | solution.py:41
  400.7 24.7 %all-to-all-start.8 = ((bf16[16,32,768]{2,1,0:T(8,128)(2,1)}), bf16[16,32,768]{2,1,0:T(8,128)(2,1)}, u32[]{:S(2)}, u32[]{:S(2)}) async-start(bf16[16,32,768]{2,1,0:T(8,128)(2,1)} %bitcast.894), calls=%async_computation.8 | async-start | bytes 1572864 | tf_op jit(solution)/shard_map/all_to_all | solution.py:559
  435.6 94.3 %collective-permute-start.64 = (bf16[8,1,48,1536]{3,2,0,1:T(8,128)(2,1)}, bf16[8,1,48,1536]{3,2,0,1:T(8,128)(2,1)}, u32[]{:S(2)}, u32[]{:S(2)}) collective-permute-start(bf16[8,1,48,1536]{3,2,0,1:T(8,128)(2,1)} %slice_bitcast_fusion.12), channel_id=1, source_target_pairs={{0,2},{2,0},{4,6},{6,4},{8,10},{10,8},{12,14},{14,12},{16,18},{18,... | collective-permute-start | bytes 3538952 | tf_op jit(solution)/shard_map/ppermute | solution.py:270
  437.4 94.7 %collective-permute-start.72 = (bf16[4,2,48,1536]{3,2,1,0:T(8,128)(2,1)}, bf16[4,2,48,1536]{3,2,1,0:T(8,128)(2,1)}, u32[]{:S(2)}, u32[]{:S(2)}) collective-permute-start(bf16[4,2,48,1536]{3,2,1,0:T(8,128)(2,1)} %slice_bitcast_fusion.6), channel_id=1, source_target_pairs={{0,4},{2,6},{4,0},{6,2},{8,12},{10,14},{12,8},{14,10},{16,20},{18,... | collective-permute-start | bytes 3538952 | tf_op jit(solution)/shard_map/ppermute | solution.py:270
  467.9 49.4 %collective-permute-start.37 = (f32[256,768]{1,0:T(8,128)}, f32[256,768]{1,0:T(8,128)}, u32[]{:S(2)}, u32[]{:S(2)}) collective-permute-start(f32[256,768]{1,0:T(8,128)} %slice.831), channel_id=1, source_target_pairs={{0,1},{1,0},{2,3},{3,2},{4,5},{5,4},{6,7},{7,6},{8,9},{9,8},{10,11... | collective-permute-start | bytes 2359304 | tf_op jit(solution)/shard_map/ppermute | solution.py:27
  475.6 38.2 %collective-permute-start.56 = (bf16[4,2,48,768]{3,2,1,0:T(8,128)(2,1)}, bf16[4,2,48,768]{3,2,1,0:T(8,128)(2,1)}, u32[]{:S(2)}, u32[]{:S(2)}) collective-permute-start(bf16[4,2,48,768]{3,2,1,0:T(8,128)(2,1)} %slice_bitcast_fusion.24), channel_id=1, source_target_pairs={{0,4},{2,6},{4,0},{6,2},{8,12},{10,14},{12,8},{14,10},{16,20},{18,... | collective-permute-start | bytes 1769480 | tf_op jit(solution)/shard_map/ppermute | solution.py:270
  483.5 31.7 %collective-permute-start.52 = (bf16[8,1,48,768]{3,2,0,1:T(8,128)(2,1)}, bf16[8,1,48,768]{3,2,0,1:T(8,128)(2,1)}, u32[]{:S(2)}, u32[]{:S(2)}) collective-permute-start(bf16[8,1,48,768]{3,2,0,1:T(8,128)(2,1)} %slice_bitcast_fusion.26), channel_id=1, source_target_pairs={{0,2},{2,0},{4,6},{6,4},{8,10},{10,8},{12,14},{14,12},{16,18},{18,... | collective-permute-start | bytes 1769480 | tf_op jit(solution)/shard_map/ppermute | solution.py:270
  513.8 147.6 %collective-permute-start.43 = (f32[256,768]{1,0:T(8,128)}, f32[256,768]{1,0:T(8,128)}, u32[]{:S(2)}, u32[]{:S(2)}) collective-permute-start(f32[256,768]{1,0:T(8,128)} %slice.837), channel_id=1, source_target_pairs={{0,1},{1,0},{2,3},{3,2},{4,5},{5,4},{6,7},{7,6},{8,9},{9,8},{10,11... | collective-permute-start | bytes 2359304 | tf_op jit(solution)/shard_map/ppermute | solution.py:27
  524.6 24.4 %collective-permute-start.38 = (bf16[256,768]{1,0:T(8,128)(2,1)S(1)}, bf16[256,768]{1,0:T(8,128)(2,1)S(1)}, u32[]{:S(2)}, u32[]{:S(2)}) collective-permute-start(bf16[256,768]{1,0:T(8,128)(2,1)S(1)} %add_convert_fusion.1), channel_id=1, source_target_pairs={{0,1},{1,0},{2,3},{3,2},{4,5},{5,4},{6,7},{7,6},{8,9},{9,8},{10,11... | collective-permute-start | bytes 1179656 | tf_op jit(solution)/shard_map/ppermute | solution.py:27
  532.2 27.6 %collective-permute-start.65 = (bf16[4,1,48,1536]{3,2,0,1:T(8,128)(2,1)S(1)}, bf16[4,1,48,1536]{3,2,0,1:T(8,128)(2,1)S(1)}, u32[]{:S(2)}, u32[]{:S(2)}) collective-permute-start(bf16[4,1,48,1536]{3,2,0,1:T(8,128)(2,1)S(1)} %fusion.180), channel_id=1, source_target_pairs={{0,4},{2,6},{4,0},{6,2},{8,12},{10,14},{12,8},{14,10},{16,20},{18,... | collective-permute-start | bytes 1769480 | tf_op jit(solution)/shard_map/ppermute | solution.py:270
  536.2 25.2 %collective-permute-start.73 = (bf16[4,1,48,1536]{3,2,0,1:T(8,128)(2,1)S(1)}, bf16[4,1,48,1536]{3,2,0,1:T(8,128)(2,1)S(1)}, u32[]{:S(2)}, u32[]{:S(2)}) collective-permute-start(bf16[4,1,48,1536]{3,2,0,1:T(8,128)(2,1)S(1)} %fusion.182), channel_id=1, source_target_pairs={{0,2},{2,0},{4,6},{6,4},{8,10},{10,8},{12,14},{14,12},{16,18},{18,... | collective-permute-start | bytes 1769480 | tf_op jit(solution)/shard_map/ppermute | solution.py:270
  552.6 33.4 %collective-permute-start.39 = (f32[256,768]{1,0:T(8,128)S(1)}, f32[256,768]{1,0:T(8,128)S(1)}, u32[]{:S(2)}, u32[]{:S(2)}) collective-permute-start(f32[256,768]{1,0:T(8,128)S(1)} %slice.833), channel_id=1, source_target_pairs={{0,1},{1,0},{2,3},{3,2},{4,5},{5,4},{6,7},{7,6},{8,9},{9,8},{10,11... | collective-permute-start | bytes 2359304 | tf_op jit(solution)/shard_map/ppermute | solution.py:27
  556.1 82.6 %collective-permute-start.60 = (bf16[8,1,48,1536]{3,2,0,1:T(8,128)(2,1)}, bf16[8,1,48,1536]{3,2,0,1:T(8,128)(2,1)}, u32[]{:S(2)}, u32[]{:S(2)}) collective-permute-start(bf16[8,1,48,1536]{3,2,0,1:T(8,128)(2,1)} %slice_bitcast_fusion.15), channel_id=1, source_target_pairs={{0,2},{2,0},{4,6},{6,4},{8,10},{10,8},{12,14},{14,12},{16,18},{18,... | collective-permute-start | bytes 3538952 | tf_op jit(solution)/shard_map/ppermute | solution.py:270
  560.3 81.4 %collective-permute-start.68 = (bf16[4,2,48,1536]{3,2,1,0:T(8,128)(2,1)}, bf16[4,2,48,1536]{3,2,1,0:T(8,128)(2,1)}, u32[]{:S(2)}, u32[]{:S(2)}) collective-permute-start(bf16[4,2,48,1536]{3,2,1,0:T(8,128)(2,1)} %slice_bitcast_fusion.9), channel_id=1, source_target_pairs={{0,4},{2,6},{4,0},{6,2},{8,12},{10,14},{12,8},{14,10},{16,20},{18,... | collective-permute-start | bytes 3538952 | tf_op jit(solution)/shard_map/ppermute | solution.py:270
  638.4 22.5 %collective-permute-start.41 = (f32[256,768]{1,0:T(8,128)S(1)}, f32[256,768]{1,0:T(8,128)S(1)}, u32[]{:S(2)}, u32[]{:S(2)}) collective-permute-start(f32[256,768]{1,0:T(8,128)S(1)} %slice.835), channel_id=1, source_target_pairs={{0,1},{1,0},{2,3},{3,2},{4,5},{5,4},{6,7},{7,6},{8,9},{9,8},{10,11... | collective-permute-start | bytes 2359304 | tf_op jit(solution)/shard_map/ppermute | solution.py:27
  657.1 59.7 %collective-permute-start.62 = (bf16[2,1,48,1536]{3,2,0,1:T(8,128)(2,1)}, bf16[2,1,48,1536]{3,2,0,1:T(8,128)(2,1)}, u32[]{:S(2)}, u32[]{:S(2)}) collective-permute-start(bf16[2,1,48,1536]{3,2,0,1:T(8,128)(2,1)} %fusion.258), channel_id=1, source_target_pairs={{0,8},{2,10},{4,12},{6,14},{8,0},{10,2},{12,4},{14,6},{16,24},{18,... | collective-permute-start | bytes 884744 | tf_op jit(solution)/shard_map/ppermute | solution.py:270
  660.4 59.8 %collective-permute-start.70 = (bf16[1,2,48,1536]{3,2,1,0:T(8,128)(2,1)}, bf16[1,2,48,1536]{3,2,1,0:T(8,128)(2,1)}, u32[]{:S(2)}, u32[]{:S(2)}) collective-permute-start(bf16[1,2,48,1536]{3,2,1,0:T(8,128)(2,1)} %fusion.259), channel_id=1, source_target_pairs={{0,16},{2,18},{4,20},{6,22},{8,24},{10,26},{12,28},{14,30},{16,0},... | collective-permute-start | bytes 884744 | tf_op jit(solution)/shard_map/ppermute | solution.py:270
  675.8 55.2 %collective-permute-start.48 = (bf16[8,1,48,1792]{3,2,0,1:T(8,128)(2,1)}, bf16[8,1,48,1792]{3,2,0,1:T(8,128)(2,1)}, u32[]{:S(2)}, u32[]{:S(2)}) collective-permute-start(bf16[8,1,48,1792]{3,2,0,1:T(8,128)(2,1)} %slice_bitcast_fusion), channel_id=1, source_target_pairs={{0,2},{2,0},{4,6},{6,4},{8,10},{10,8},{12,14},{14,12},{16,18},{18,... | collective-permute-start | bytes 4128776 | tf_op jit(solution)/shard_map/ppermute | solution.py:270
  684.7 48.5 %collective-permute-start.44 = (bf16[4,2,48,1792]{3,2,1,0:T(8,128)(2,1)}, bf16[4,2,48,1792]{3,2,1,0:T(8,128)(2,1)}, u32[]{:S(2)}, u32[]{:S(2)}) collective-permute-start(bf16[4,2,48,1792]{3,2,1,0:T(8,128)(2,1)} %slice_bitcast_fusion.3), channel_id=1, source_target_pairs={{0,4},{2,6},{4,0},{6,2},{8,12},{10,14},{12,8},{14,10},{16,20},{18,... | collective-permute-start | bytes 4128776 | tf_op jit(solution)/shard_map/ppermute | solution.py:270
  687.5 28.6 %all-to-all-start.9 = ((f32[32,1,168]{2,1,0:T(1,128)}), f32[32,1,168]{2,1,0:T(1,128)S(1)}, u32[]{:S(2)}, u32[]{:S(2)}) async-start(f32[32,1,168]{2,1,0:T(1,128)} %all_to_all.91), calls=%async_computation.9 | async-start | bytes 65536 | tf_op jit(solution)/shard_map/all_to_all | solution.py:621
  751.6 22.1 %collective-permute-start.46 = (bf16[1,2,48,1792]{3,2,1,0:T(8,128)(2,1)S(1)}, bf16[1,2,48,1792]{3,2,1,0:T(8,128)(2,1)S(1)}, u32[]{:S(2)}, u32[]{:S(2)}) collective-permute-start(bf16[1,2,48,1792]{3,2,1,0:T(8,128)(2,1)S(1)} %fusion.251), channel_id=1, source_target_pairs={{0,16},{2,18},{4,20},{6,22},{8,24},{10,26},{12,28},{14,30},{16,0},... | collective-permute-start | bytes 1032200 | tf_op jit(solution)/shard_map/ppermute | solution.py:270
  761.7 19.3 %collective-permute-start.51 = (bf16[1,1,48,1792]{3,2,1,0:T(8,128)(2,1)S(1)}, bf16[1,1,48,1792]{3,2,1,0:T(8,128)(2,1)S(1)}, u32[]{:S(2)}, u32[]{:S(2)}) collective-permute-start(bf16[1,1,48,1792]{3,2,1,0:T(8,128)(2,1)S(1)} %fusion.290), channel_id=1, source_target_pairs={{0,16},{2,18},{4,20},{6,22},{8,24},{10,26},{12,28},{14,30},{16,0},... | collective-permute-start | bytes 516104 | tf_op jit(solution)/shard_map/ppermute | solution.py:270
  774.6 41.3 %all-to-all-start.10 = ((bf16[32,32,768]{2,1,0:T(8,128)(2,1)}), bf16[32,32,768]{2,1,0:T(8,128)(2,1)}, u32[]{:S(2)}, u32[]{:S(2)}) async-start(bf16[32,32,768]{2,1,0:T(8,128)(2,1)} %bitcast.928), calls=%async_computation.10 | async-start | bytes 3145728 | tf_op jit(solution)/shard_map/all_to_all | solution.py:601
  779.2 28.7 %collective-permute-start.47 = (bf16[1,1,48,1792]{3,2,1,0:T(8,128)(2,1)S(1)}, bf16[1,1,48,1792]{3,2,1,0:T(8,128)(2,1)S(1)}, u32[]{:S(2)}, u32[]{:S(2)}) collective-permute-start(bf16[1,1,48,1792]{3,2,1,0:T(8,128)(2,1)S(1)} %fusion.289), channel_id=1, source_target_pairs={{0,8},{2,10},{4,12},{6,14},{8,0},{10,2},{12,4},{14,6},{16,24},{18,... | collective-permute-start | bytes 516104 | tf_op jit(solution)/shard_map/ppermute | solution.py:270
  (286 other events, 2158.3 us)

commit v3 on v2

v3 whole, which is shorter than its diff:
```python
import functools

import jax
import jax.numpy as jnp
from jax import lax
from jax.experimental import pallas as pl
from jax.experimental.pallas import tpu as pltpu
from jax.sharding import PartitionSpec as P

HEAD_DIM = 64
MAX_NORM = 0.01
LEARN_RATE = 0.03
GAIN_RATE = 0.3
FIRST_DECAY = 0.9
SECOND_DECAY = 0.999
ADAM_EPSILON = 1e-08
WEIGHT_DECAY = 0.01
SCORE_FLOOR = -1000000000.0
EVERY = ("dp", "tensor")
CORE_SWAP = ((0, 1), (1, 0))
SLOTS = 32


def norm_rows(values, gain):
    centered = values - jnp.mean(values, axis=-1, keepdims=True)
    variance = jnp.mean(centered * centered, axis=-1, keepdims=True)
    return centered * lax.rsqrt(variance + 1e-05) * gain


def swap(values):
    return lax.ppermute(values, "tensor", CORE_SWAP)


def spread(rows):
    return jnp.concatenate([rows, swap(rows)], axis=0)


def collect(partial_rows):
    half = partial_rows.shape[0] // 2
    return partial_rows[:half] + swap(partial_rows[half:])


def to_all(values, axis=EVERY):
    size = lax.axis_size(axis)
    return lax.all_to_all(
        jnp.broadcast_to(values[None], (size,) + values.shape), axis, 0, 0, tiled=True
    )


def product(left, right):
    return jnp.dot(left, right, preferred_element_type=jnp.float32)


def product_tn(left, right):
    return lax.dot_general(
        left, right, (((0,), (0,)), ((), ())), preferred_element_type=jnp.float32
    )


def product_nt(left, right):
    return lax.dot_general(
        left, right, (((1,), (1,)), ((), ())), preferred_element_type=jnp.float32
    )


def attend_forward_kernel(places, width, *refs):
    allowed_ref, mixed_ref = refs[-2:]
    allowed = allowed_ref[...] > 0
    for first in range(0, width, HEAD_DIM):
        query, key, value = [
            refs[ref][:, start + first : start + first + HEAD_DIM] for ref, start in places
        ]
        scores = jnp.where(allowed, product_nt(query, key) * HEAD_DIM ** (-0.5), SCORE_FLOOR)
        powers = jnp.exp(scores - jnp.max(scores, axis=1, keepdims=True))
        weights = powers * (1.0 / jnp.sum(powers, axis=1, keepdims=True))
        mixed = product(weights.astype(jnp.bfloat16), value)
        mixed_ref[:, first : first + HEAD_DIM] = mixed.astype(jnp.bfloat16)


def attend_backward_kernel(places, width, *refs):
    count = (len(refs) - 2) // 2
    grad_ref, allowed_ref = refs[count : count + 2]
    out_refs = refs[count + 2 :]
    allowed = allowed_ref[...] > 0
    for first in range(0, width, HEAD_DIM):
        query, key, value = [
            refs[ref][:, start + first : start + first + HEAD_DIM] for ref, start in places
        ]
        grad = grad_ref[:, first : first + HEAD_DIM]
        scores = jnp.where(allowed, product_nt(key, query) * HEAD_DIM ** (-0.5), SCORE_FLOOR)
        powers = jnp.exp(scores - jnp.max(scores, axis=0, keepdims=True))
        weights = powers * (1.0 / jnp.sum(powers, axis=0, keepdims=True))
        grad_value = product(weights.astype(jnp.bfloat16), grad)
        grad_weights = product_nt(value, grad)
        inner = jnp.sum(weights * grad_weights, axis=0, keepdims=True)
        grad_scores = (weights * (grad_weights - inner) * HEAD_DIM ** (-0.5)).astype(jnp.bfloat16)
        grads = (product_tn(grad_scores, key), product(grad_scores, query), grad_value)
        for (ref, start), values in zip(places, grads):
            out_refs[ref][:, start + first : start + first + HEAD_DIM] = values.astype(jnp.bfloat16)


def kernel_call(kernel, outputs, operands, flops):
    size = sum(value.size * value.dtype.itemsize for value in operands)
    return pl.pallas_call(
        kernel,
        out_shape=outputs,
        in_specs=[pl.BlockSpec(memory_space=pltpu.VMEM)] * len(operands),
        out_specs=jax.tree.map(lambda _: pl.BlockSpec(memory_space=pltpu.VMEM), outputs),
        compiler_params=pltpu.CompilerParams(vmem_limit_bytes=32 * 1024 * 1024),
        cost_estimate=pl.CostEstimate(flops=flops, bytes_accessed=2 * size, transcendentals=0),
    )(*operands)


def attend_forward(arrays, places, width, allowed):
    rows = arrays[places[0][0]].shape[0]
    return kernel_call(
        functools.partial(attend_forward_kernel, places, width),
        jax.ShapeDtypeStruct((rows, width), jnp.bfloat16),
        arrays + (allowed.astype(jnp.float32),),
        16 * rows * width * arrays[places[1][0]].shape[0],
    )


def attend_backward(arrays, places, width, grad_mixed, allowed):
    rows = grad_mixed.shape[0]
    return kernel_call(
        functools.partial(attend_backward_kernel, places, width),
        tuple(jax.ShapeDtypeStruct(array.shape, array.dtype) for array in arrays),
        arrays + (grad_mixed, allowed.astype(jnp.float32).T),
        40 * rows * width * arrays[places[1][0]].shape[0],
    )


def pick_rows(index, rows):
    return product(index, rows).astype(jnp.bfloat16)


def place_exact(index, rows):
    return jnp.dot(
        index.astype(jnp.float32),
        rows,
        precision=lax.Precision.HIGHEST,
        preferred_element_type=jnp.float32,
    )


def both(partial_rows):
    return partial_rows + swap(partial_rows)


def norm_backward(values, gain, grad):
    grad_values, grad_gain = jax.vjp(norm_rows, values, gain)[1](grad)
    return grad_values, grad_gain


def own_half(rows):
    half = rows.shape[0] // 2
    return jnp.where(lax.axis_index("tensor") == 0, rows[:half], rows[half:])


def in_order(rows):
    other = swap(rows)
    return jnp.where(
        lax.axis_index("tensor") == 0,
        jnp.concatenate([rows, other]),
        jnp.concatenate([other, rows]),
    )


def norm_backward_shared(values, gain, grad):
    grad_values = jax.vjp(lambda rows: norm_rows(rows, gain), values)[1](grad)[0]
    own = own_half(values)
    grad_gain = jax.vjp(lambda scale: norm_rows(own, scale), gain)[1](own_half(grad))[0]
    return grad_values, grad_gain


def tie(*values):
    return lax.optimization_barrier(values)


def low_grad(left, right):
    return product_tn(left, right).astype(jnp.bfloat16)


def low_product(left, right):
    return product(left, right).astype(jnp.bfloat16)


def gelu_exact(values):
    return jax.nn.gelu(values, approximate=False)


def gelu_backward(inner, grad_hidden):
    return jax.vjp(gelu_exact, inner)[1](grad_hidden.astype(jnp.float32))[0].astype(jnp.bfloat16)


def adam_step(master, first, second, grad, clip, fix_one, fix_two, rate):
    grad = grad * clip
    first_new = FIRST_DECAY * first + (1 - FIRST_DECAY) * grad
    second_new = SECOND_DECAY * second + (1 - SECOND_DECAY) * grad * grad
    master_new = master - rate * (
        first_new / fix_one / (jnp.sqrt(second_new / fix_two) + ADAM_EPSILON)
        + WEIGHT_DECAY * master
    )
    return (master_new, first_new, second_new)


def bit_order(turn):
    count = (lax.axis_size("dp") - 1).bit_length()
    order = list(range(count - 1, -1, -1))
    if turn % 2:
        for first in range(0, count - 1, 2):
            order[first], order[first + 1] = order[first + 1], order[first]
    return order


def swap_bit(values, bit):
    pairs = [(group, group ^ (1 << bit)) for group in range(lax.axis_size("dp"))]
    return lax.ppermute(values, "dp", pairs)


class Gather:
    def __init__(self, shard, turn):
        self.held = shard[None]
        self.order = bit_order(turn)
        self.bits = []

    def step(self):
        bit = self.order[len(self.bits)]
        got = swap_bit(self.held, bit)
        block = self.held.shape[1:]
        above = sum(1 for other in self.bits if other > bit)
        shape = (2**above, 2 ** (len(self.bits) - above)) + block
        held = jnp.stack([self.held.reshape(shape), got.reshape(shape)], axis=1)
        self.held = held.reshape((-1,) + block)
        self.bits.append(bit)

    def columns(self, first, last):
        part = Gather(self.held[0, :, first:last], 0)
        part.held, part.order, part.bits = self.held[:, :, first:last], self.order, list(self.bits)
        return part

    def left(self):
        return len(self.order) - len(self.bits)

    def rows(self):
        while self.left():
            self.step()
        return self.held.reshape(-1, self.held.shape[2])


class Scatter:
    def __init__(self, grads, turn):
        groups = lax.axis_size("dp")
        self.held = grads.reshape((groups, grads.shape[0] // groups, grads.shape[1]))
        self.order = bit_order(turn)
        self.bits = sorted(self.order, reverse=True)

    def step(self):
        bit = self.order.pop()
        above = self.bits.index(bit)
        block = self.held.shape[1:]
        halves = self.held.reshape((2**above, 2, -1) + block)
        got = swap_bit(halves[:, 1].astype(jnp.bfloat16), bit)
        held = halves[:, 0].astype(jnp.float32) + got.astype(jnp.float32)
        self.held = held.reshape((-1,) + block)
        self.bits.remove(bit)

    def left(self):
        return len(self.order)

    def rows(self):
        while self.left():
            self.step()
        return self.held[0]


def joined(scatters):
    whole = Scatter(jnp.zeros((lax.axis_size("dp"), 1)), 0)
    whole.held = jnp.concatenate([scatter.held for scatter in scatters], axis=2)
    whole.order, whole.bits = list(scatters[0].order), list(scatters[0].bits)
    return whole


def advance(movers):
    for mover in movers:
        if mover.left():
            mover.step()


def meet(value, movers):
    tied = tie(value, *[mover.held for mover in movers])
    for mover, held in zip(movers, tied[1:]):
        mover.held = held
    return tied[0]


def flipped(values):
    return jnp.swapaxes(values, -1, -2)


def request_slots(ids, rows_owned):
    owner = ids // rows_owned
    here = jnp.arange(ids.shape[0])
    earlier = here[None, :] < here[:, None]
    same = ids[:, None] == ids[None, :]
    leads = jnp.sum((same & earlier).astype(jnp.int32), axis=1) == 0
    leader = jnp.min(jnp.where(same, here[None, :], ids.shape[0]), axis=1)
    rank = jnp.sum(
        (
            (here[None, :] < leader[:, None])
            & leads[None, :]
            & (owner[:, None] == owner[None, :])
        ).astype(jnp.int32),
        axis=1,
    )
    return owner, rank, leads


def chosen_rows(index, count, dtype=jnp.bfloat16):
    return (index[:, None] == jnp.arange(count)[None, :]).astype(dtype)


def local(
    source_ids,
    target_ids,
    score_places,
    target_labels,
    source_lengths,
    target_lengths,
    pair_order,
    step_count,
    entry_weight,
    entry_first,
    entry_second,
    exit_weight,
    exit_first,
    exit_second,
    expand_weight,
    expand_first,
    expand_second,
    reduce_weight,
    reduce_first,
    reduce_second,
    norm_gains,
    gains_first,
    gains_second,
    token_table,
    table_first,
    table_second,
    place_table,
    place_first,
    place_second,
):
    groups = lax.axis_size("dp")
    parts = lax.axis_size("tensor")
    devices = groups * parts
    group = lax.axis_index("dp")
    part = lax.axis_index("tensor")
    low = jnp.bfloat16
    rows_owned, width = token_table.shape
    half = source_ids.shape[1]
    spot_share = score_places.shape[1]

    share = width // groups
    feature = jnp.arange(width)
    home = (feature // share ^ group) * share + feature % share
    order = home[:, None] == feature[None, :]

    def reordered(values):
        return product(values, order.astype(low))

    def reordered_exact(values):
        return jnp.dot(
            values,
            order.astype(jnp.float32),
            precision=lax.Precision.HIGHEST,
            preferred_element_type=jnp.float32,
        )

    gains = reordered_exact(norm_gains)
    blocks = entry_weight.shape[3]
    entry_low = entry_weight.astype(low)
    leave_low = flipped(exit_weight.astype(low))
    place_low = flipped(place_table.astype(low))
    expand_low = expand_weight.astype(low)
    shrink_low = flipped(reduce_weight.astype(low))
    wide = expand_low.shape[2]

    def beside(*pieces):
        return jnp.concatenate(pieces, axis=1)

    attend_gathers = [
        Gather(beside(entry_low[0, 0], entry_low[0, 1]), 0),
        Gather(beside(entry_low[0, 2], leave_low[0], place_low[0]), 1),
    ]
    late_gathers = [
        Gather(
            beside(entry_low[1, 0], entry_low[1, 1], entry_low[1, 2], leave_low[1], place_low[1]),
            0,
        ),
        Gather(beside(entry_low[2, 0], entry_low[2, 1], entry_low[2, 2], leave_low[2]), 1),
    ]
    advance(attend_gathers)
    feed_weights = [
        lax.all_gather(jnp.stack([expand_low[b], shrink_low[b]]), "dp", axis=1, tiled=True)
        for b in range(2)
    ]

    def pieces_of(values, first, count):
        return [
            values[:, first + b * blocks : first + (b + 1) * blocks] for b in range(count)
        ]

    ids = jnp.concatenate([source_ids[0], target_ids[0]])
    owner, rank, leads = request_slots(ids, rows_owned)
    rounds = jnp.max(rank) // SLOTS + 1
    slots_all = devices * SLOTS
    slot_names = jnp.arange(slots_all)

    def slot_in(turn):
        return jnp.where(rank // SLOTS == turn, owner * SLOTS + rank % SLOTS, -1)

    def requests_in(turn):
        asked = (slot_names[:, None] == slot_in(turn)[None, :]) & leads[None, :]
        return jnp.sum(
            jnp.where(asked, ids[None, :] % rows_owned + 1, 0), axis=1
        ).reshape(devices, SLOTS)

    spots = score_places[0]
    extras = jnp.concatenate(
        [
            spots,
            target_labels[0],
            (spots < target_lengths[0]).astype(jnp.int32),
            rounds[None],
        ]
    )
    message = jnp.concatenate(
        [
            requests_in(0),
            jnp.broadcast_to(extras[None], (devices, extras.shape[0])),
        ],
        axis=1,
    )
    heard = lax.all_to_all(message, EVERY, 0, 0, tiled=True)
    heard = meet(heard, attend_gathers)
    advance(attend_gathers)
    asked_first = heard[:, :SLOTS].reshape(-1) - 1
    spots_all = heard[:, SLOTS : SLOTS + spot_share]
    labels_all = heard[:, SLOTS + spot_share : SLOTS + 2 * spot_share]
    valid_all = heard[:, SLOTS + 2 * spot_share : SLOTS + 3 * spot_share]
    rounds_all = jnp.max(heard[:, -1])
    own_table = token_table.astype(low)

    def picked_rows(asked):
        return product(chosen_rows(asked, rows_owned), own_table).astype(low)

    def answer(sent):
        return lax.all_to_all(
            sent.reshape(devices, SLOTS, width), EVERY, 0, 0, tiled=True
        ).reshape(slots_all, width)

    def looked_up(got, slot):
        return product(chosen_rows(slot, slots_all), got)

    def ask_again(turn):
        return (
            lax.all_to_all(requests_in(turn), EVERY, 0, 0, tiled=True).reshape(-1) - 1
        )

    asked_rows = meet(picked_rows(asked_first), attend_gathers)
    got = answer(asked_rows)
    advance(attend_gathers)
    advance(attend_gathers)
    got = meet(got, attend_gathers)
    got, feed_weights[0], late_gathers[0].held, late_gathers[1].held = tie(
        got, feed_weights[0], late_gathers[0].held, late_gathers[1].held
    )
    advance(late_gathers)
    expand_zero = pick_rows(order.astype(low), feed_weights[0][0])
    shrink_zero = pick_rows(order.astype(low), feed_weights[0][1])
    start = looked_up(got, slot_in(0))
    start = lax.while_loop(
        lambda state: state[0] < rounds_all,
        lambda state: (
            state[0] + 1,
            state[1] + looked_up(answer(picked_rows(ask_again(state[0]))), slot_in(state[0])),
        ),
        (jnp.int32(1), start),
    )[1]
    first_one, first_two = [gather.rows() for gather in attend_gathers]
    value_zero = first_two[:, :blocks]
    leave_zero = first_two[:, blocks : 2 * blocks]
    start = reordered(start.astype(low)).reshape(2, half, width)

    row_places = jnp.concatenate(
        [part * half + jnp.arange(half), (1 - part) * half + jnp.arange(half)]
    )
    spots_group = lax.dynamic_index_in_dim(
        spots_all.reshape(groups, parts, spot_share), group, 0, False
    )
    spots_group = spots_group.reshape(-1)
    encoder_mask = row_places[None, :] < source_lengths[0]
    decoder_mask = (row_places[None, :] <= spots_group[:, None]) & (
        row_places[None, :] < target_lengths[0]
    )
    scored_row = spots_group[:, None] == row_places[None, :]
    heads = ((0, 0), (0, blocks), (1, 0))
    enc_start = start[0] + flipped(first_two[:, 2 * blocks :]).astype(jnp.float32)
    enc_rows = spread(norm_rows(enc_start, gains[0]).astype(low))
    enc_pair = meet(low_product(enc_rows, first_one), late_gathers)
    advance(late_gathers)
    enc_arrays = (enc_pair, low_product(enc_rows, value_zero))
    enc_mixed = attend_forward(enc_arrays, heads, blocks, encoder_mask)
    enc_mixed = meet(enc_mixed, late_gathers)
    advance(late_gathers)
    stream = enc_start + collect(product_nt(enc_mixed, leave_zero))

    feed_rows = meet(norm_rows(stream, gains[1]).astype(low), late_gathers)
    advance(late_gathers)
    feed_rows = spread(feed_rows)
    feed_inner = product(feed_rows, expand_zero)
    feed_hidden = gelu_exact(feed_inner).astype(low)
    after_feed = stream + collect(product_nt(feed_hidden, shrink_zero))
    memory = norm_rows(after_feed, gains[2]).astype(low)

    split = ((0, 0), (1, 0), (1, blocks))
    memory = spread(meet(memory, late_gathers))
    self_weights, cross_weights = [gather.rows() for gather in late_gathers]
    self_query = self_weights[:, :blocks]
    self_keyval = self_weights[:, blocks : 3 * blocks]
    self_leave_weight = self_weights[:, 3 * blocks : 4 * blocks]
    dec_start = start[1] + flipped(self_weights[:, 4 * blocks :]).astype(jnp.float32)
    target_rows = spread(dec_start)
    dec_source = norm_rows(target_rows, gains[3]).astype(low)
    dec_rows = pick_rows(scored_row.astype(low), dec_source)
    dec_arrays = (low_product(dec_rows, self_query), low_product(dec_source, self_keyval))
    dec_mixed = attend_forward(dec_arrays, split, blocks, decoder_mask)
    after_self = place_exact(scored_row, target_rows) + both(
        product_nt(dec_mixed, self_leave_weight)
    )

    cross_query_weight = cross_weights[:, :blocks]
    cross_keyval_weight = cross_weights[:, blocks : 3 * blocks]
    cross_leave_weight = cross_weights[:, 3 * blocks :]
    cross_rows = norm_rows(after_self, gains[4]).astype(low)
    cross_rows, last_weights = tie(cross_rows, feed_weights[1])
    cross_arrays = (
        low_product(cross_rows, cross_query_weight),
        low_product(memory, cross_keyval_weight),
    )
    cross_mixed = attend_forward(cross_arrays, split, blocks, encoder_mask)
    after_cross = after_self + both(product_nt(cross_mixed, cross_leave_weight))

    after_cross = reordered_exact(after_cross)
    expand_one, shrink_one = last_weights[0], last_weights[1]
    last_rows = norm_rows(after_cross, norm_gains[5]).astype(low)
    last_inner = product(last_rows, expand_one)
    last_hidden = gelu_exact(last_inner).astype(low)
    after_last = after_cross + both(product_nt(last_hidden, shrink_one))
    final = norm_rows(after_last, norm_gains[6]).astype(low)

    picked_group = to_all(own_half(final), "dp")
    picked = in_order(picked_group.reshape(-1, width))

    def cores_first(values):
        return jnp.swapaxes(values.reshape(groups, parts, spot_share), 0, 1).reshape(-1)

    label_row = cores_first(labels_all) - (group * parts + part) * rows_owned
    valid = cores_first(valid_all).astype(jnp.float32)
    count = jnp.sum(valid)
    scored_half = picked.shape[0] // 2
    logits = product_nt(picked, own_table)
    onehot = chosen_rows(label_row, rows_owned, jnp.bool_)
    highest = jnp.max(logits, axis=-1)
    log_here = highest + jnp.log(jnp.sum(jnp.exp(logits - highest[:, None]), axis=-1))
    golden_here = jnp.sum(jnp.where(onehot, logits, 0.0), axis=-1)
    stats = to_all(jnp.stack([log_here, golden_here]))
    top = jnp.max(stats[:, 0], axis=0)
    log_total = top + jnp.log(jnp.sum(jnp.exp(stats[:, 0] - top[None]), axis=0))
    golden = jnp.sum(stats[:, 1], axis=0)
    losses = (log_total - golden) * valid
    mean_loss = jnp.sum(losses) / count
    of_group = (pair_order == group).astype(jnp.float32)
    pair_rows = jnp.sum(
        losses.reshape(parts, groups, spot_share) * of_group[None, :, None], axis=1
    )
    pair_losses = jnp.where(part == 0, pair_rows[0], pair_rows[1])[None]
    probs = jnp.exp(logits - log_total[:, None])
    grad_logits = (
        (probs - onehot.astype(jnp.float32)) * (valid / count)[:, None]
    ).astype(low)
    grad_picked = product(grad_logits, own_table)
    kept = own_half(grad_picked)
    sent = jnp.where(part == 0, grad_picked[scored_half:], grad_picked[:scored_half])
    grad_picked = lax.all_to_all(
        (kept + swap(sent)).astype(low).reshape(groups, spot_share, width),
        "dp",
        0,
        0,
        tiled=True,
    )
    grad_final = in_order(jnp.sum(grad_picked.astype(jnp.float32), axis=0))
    grad_table = product_tn(grad_logits, picked)

    grad_rows, gain_six = norm_backward_shared(after_last, norm_gains[6], grad_final)
    grad_low = grad_rows.astype(low)
    last_grads = [low_grad(grad_low, last_hidden)]
    grad_inner = gelu_backward(last_inner, product(grad_low, shrink_one).astype(low))
    last_grads = lax.psum_scatter(
        jnp.stack([low_grad(last_rows, grad_inner)] + last_grads),
        "dp",
        scatter_dimension=1,
        tiled=True,
    ).astype(jnp.float32)
    grad_values, gain_five = norm_backward_shared(
        after_cross, norm_gains[5], both(product_nt(grad_inner, expand_one))
    )
    grad_rows = reordered_exact(grad_rows + grad_values)

    grad_low = grad_rows.astype(low)
    cross_leave = low_grad(grad_low, cross_mixed)
    grad_mixed = low_product(grad_low, cross_leave_weight)
    grad_query, grad_keyval = attend_backward(
        cross_arrays, split, blocks, grad_mixed, encoder_mask
    )
    cross_scatters = [
        Scatter(beside(low_grad(cross_rows, grad_query), cross_leave), 0),
        Scatter(low_grad(memory, grad_keyval), 1),
    ]
    advance(cross_scatters)
    back_source = product_nt(grad_keyval, cross_keyval_weight)
    back_rows = product_nt(grad_query, cross_query_weight)
    grad_stream, gain_two = norm_backward(after_feed, gains[2], collect(back_source))

    grad_all = spread(grad_stream.astype(low))
    grad_inner = gelu_backward(feed_inner, product(grad_all, shrink_zero).astype(low))
    feed_scatters = [Scatter(low_grad(grad_all, feed_hidden), 0)]
    feed_scatters.append(Scatter(low_grad(feed_rows, grad_inner), 1))
    advance(feed_scatters)
    back = product_nt(grad_inner, expand_zero)
    back, back_rows = tie(back, back_rows)
    grad_values, gain_one = norm_backward(stream, gains[1], collect(back))
    grad_stream = grad_stream + grad_values

    grad_values, gain_four = norm_backward_shared(after_self, gains[4], both(back_rows))
    grad_rows = grad_rows + grad_values
    grad_low = grad_rows.astype(low)
    self_leave = low_grad(grad_low, dec_mixed)
    grad_mixed = low_product(grad_low, self_leave_weight)
    grad_query, grad_keyval = attend_backward(
        dec_arrays, split, blocks, grad_mixed, decoder_mask
    )
    self_scatters = [
        Scatter(beside(low_grad(dec_rows, grad_query), self_leave), 0),
        Scatter(low_grad(dec_source, grad_keyval), 1),
    ]
    advance(self_scatters)
    back_source = product_nt(grad_keyval, self_keyval) + place_exact(
        scored_row.T, product_nt(grad_query, self_query)
    )
    grad_decoded, gain_three = norm_backward(dec_start, gains[3], collect(back_source))
    grad_decoded = grad_decoded + place_exact(scored_row[:, :half].T, grad_rows)
    start_decoded = grad_decoded.astype(low)

    grad_all = meet(grad_stream.astype(low), cross_scatters + feed_scatters)
    early = [joined([cross_scatters[b], feed_scatters[b]]) for b in range(2)]
    advance(early)
    grad_all = spread(grad_all)
    grad_mixed = low_product(grad_all, leave_zero)
    first_scatters = [
        Scatter(beside(low_grad(grad_all, enc_mixed), flipped(start_decoded)), 0)
    ]
    advance(first_scatters)
    grad_pair, grad_value = attend_backward(enc_arrays, heads, blocks, grad_mixed, encoder_mask)
    grad_pair = meet(grad_pair, early)
    advance(early)
    back = product_nt(grad_pair, first_one) + product_nt(grad_value, value_zero)
    first_scatters += [
        Scatter(low_grad(enc_rows, grad_pair), 1),
        Scatter(low_grad(enc_rows, grad_value), 0),
    ]
    advance(first_scatters[1:])
    grad_values, gain_zero = norm_backward(enc_start, gains[0], collect(back))
    start_stream = (grad_stream + grad_values).astype(low)
    first_scatters.append(Scatter(flipped(start_stream), 1))

    start_rows = reordered(jnp.concatenate([start_stream, start_decoded])).astype(low)

    def returned(slot):
        return answer(product_tn(chosen_rows(slot, slots_all), start_rows).astype(low))

    def placed(asked, got):
        return product_tn(chosen_rows(asked, rows_owned), got)

    got = returned(slot_in(0))
    advance(first_scatters[3:])
    late = [
        joined([self_scatters[0], first_scatters[0], first_scatters[2]]),
        joined([self_scatters[1], first_scatters[1], first_scatters[3]]),
    ]
    advance(early)
    advance(late)
    got = meet(got, early + late)
    early_rows = [scatter.rows() for scatter in early]
    late_rows = [scatter.rows() for scatter in late]
    table_grad = grad_table + placed(asked_first, got)
    table_grad = lax.while_loop(
        lambda state: state[0] < rounds_all,
        lambda state: (
            state[0] + 1,
            state[1] + placed(ask_again(state[0]), returned(slot_in(state[0]))),
        ),
        (jnp.int32(1), table_grad),
    )[1]

    gain_partial = jnp.concatenate(
        [
            reordered_exact(jnp.stack([gain_zero, gain_one, gain_two, gain_three, gain_four])),
            jnp.stack([gain_five, gain_six]),
        ]
    )
    gain_own = jnp.sum(
        lax.all_to_all(gain_partial.reshape(devices, -1), EVERY, 0, 0, tiled=True), axis=0
    )
    def attention_grads(outer, keyval):
        return [outer[:, :blocks], keyval[:, :blocks], keyval[:, blocks:], outer[:, blocks:]]

    cross_pieces = attention_grads(*[rows[:, : 2 * blocks] for rows in early_rows])
    shrink_rows, expand_rows = [rows[:, 2 * blocks :] for rows in early_rows]
    self_pieces = attention_grads(*[rows[:, : 2 * blocks] for rows in late_rows])
    first_leave, decoded_place, first_value = jnp.split(
        late_rows[0][:, 2 * blocks :], [blocks, blocks + half], axis=1
    )
    first_pieces = pieces_of(late_rows[1], 2 * blocks, 2) + [first_value, first_leave]
    stream_place = late_rows[1][:, 4 * blocks :]
    entry_grad = jnp.stack(
        [jnp.stack(pieces[:3]) for pieces in (first_pieces, self_pieces, cross_pieces)]
    )
    leave_grad = flipped(jnp.stack([first_pieces[3], self_pieces[3], cross_pieces[3]]))
    expand_grad = jnp.stack([expand_rows, last_grads[0]])
    shrink_grad = flipped(jnp.stack([shrink_rows, last_grads[1]]))
    place_grad = flipped(jnp.stack([stream_place, decoded_place]))
    squares = jnp.sum(gain_own * gain_own)
    for grad in (entry_grad, leave_grad, expand_grad, shrink_grad, table_grad, place_grad):
        squares = squares + jnp.sum(grad * grad)
    last_words = to_all(jnp.concatenate([gain_own, squares[None]]))
    gain_grad = last_words[:, :-1].reshape(norm_gains.shape)
    gradient_norm = jnp.sqrt(jnp.sum(last_words[:, -1]))
    clip = jnp.minimum(1.0, MAX_NORM / (gradient_norm + 1e-06))
    steps = step_count[0].astype(jnp.float32)
    fix_one = 1 - FIRST_DECAY**steps
    fix_two = 1 - SECOND_DECAY**steps
    masters = (
        entry_weight,
        exit_weight,
        expand_weight,
        reduce_weight,
        norm_gains,
        token_table,
        place_table,
    )
    firsts = (
        entry_first,
        exit_first,
        expand_first,
        reduce_first,
        gains_first,
        table_first,
        place_first,
    )
    seconds = (
        entry_second,
        exit_second,
        expand_second,
        reduce_second,
        gains_second,
        table_second,
        place_second,
    )
    grads = (entry_grad, leave_grad, expand_grad, shrink_grad, gain_grad, table_grad, place_grad)
    rates = (LEARN_RATE, LEARN_RATE, LEARN_RATE, LEARN_RATE, GAIN_RATE, LEARN_RATE, LEARN_RATE)
    results = [mean_loss, gradient_norm, pair_losses]
    for master, first, second, grad, rate in zip(masters, firsts, seconds, grads, rates):
        results.extend(adam_step(master, first, second, grad, clip, fix_one, fix_two, rate))
    return tuple(results)


def solution(mesh):
    return jax.shard_map(
        local,
        mesh=mesh,
        in_specs=(
            P("dp", "tensor"),
            P("dp", "tensor"),
            P("dp", "tensor"),
            P("dp", "tensor"),
            P("dp"),
            P("dp"),
            P(),
            P(),
            P(None, None, "dp", "tensor"),
            P(None, None, "dp", "tensor"),
            P(None, None, "dp", "tensor"),
            P(None, "tensor", "dp"),
            P(None, "tensor", "dp"),
            P(None, "tensor", "dp"),
            P(None, "dp", "tensor"),
            P(None, "dp", "tensor"),
            P(None, "dp", "tensor"),
            P(None, "tensor", "dp"),
            P(None, "tensor", "dp"),
            P(None, "tensor", "dp"),
            P(),
            P(),
            P(),
            P(("dp", "tensor"), None),
            P(("dp", "tensor"), None),
            P(("dp", "tensor"), None),
            P(None, "tensor", "dp"),
            P(None, "tensor", "dp"),
            P(None, "tensor", "dp"),
        ),
        out_specs=(
            P(),
            P(),
            P("dp", "tensor"),
            P(None, None, "dp", "tensor"),
            P(None, None, "dp", "tensor"),
            P(None, None, "dp", "tensor"),
            P(None, "tensor", "dp"),
            P(None, "tensor", "dp"),
            P(None, "tensor", "dp"),
            P(None, "dp", "tensor"),
            P(None, "dp", "tensor"),
            P(None, "dp", "tensor"),
            P(None, "tensor", "dp"),
            P(None, "tensor", "dp"),
            P(None, "tensor", "dp"),
            P(),
            P(),
            P(),
            P(("dp", "tensor"), None),
            P(("dp", "tensor"), None),
            P(("dp", "tensor"), None),
            P(None, "tensor", "dp"),
            P(None, "tensor", "dp"),
            P(None, "tensor", "dp"),
        ),
        check_vma=False,
    )
```

time: 882 us -> 731 us (0.83)
  matrix products: 186 us -> 106 us
  waiting for transfers between devices: 330 us -> 284 us
  local copies, waits for them, and re-layouts: 86.2 us -> 52.5 us
  other arithmetic: 140 us -> 110 us
  Pallas kernels: 0 us -> 22.7 us
  between operations: 18.7 us -> 32.2 us
  blocking collectives: 14.5 us -> 26.1 us
  starting transfers between devices: 95.8 us -> 86.3 us
    dot_general x18 -> x0, matrix products: 63.7 us -> none  [the longest x3 22.5 us: attend_backward(): jnp.einsum('hqk,qhd->khd', grad_scores, heads_of(query), preferred_elemen...]
    another operation x52 -> x24, other arithmetic: 41.3 us -> 12.8 us  [the longest x14 6.36 us: step(): held = jnp.stack([self.held.reshape(shape), got.reshape(shape)], axis=1)]
    ppermute x56 -> x38, waiting for transfers between devices: 259 us -> 237 us  [swap_bit(): return lax.ppermute(values, 'dp', pairs)]
    pallas_call x0 -> x6, Pallas kernels: none -> 22.7 us  [kernel_call(): pl.pallas_call(kernel, out_shape=outputs, in_specs=[pl.BlockSpec(memory_s...]
    all_to_all x1, waiting for transfers between devices: 20.9 us -> 4.5 us  [local(): lax.all_to_all(gain_partial.reshape(devices, -1), EVERY, 0, 0, tiled=True)]
    ppermute x56 -> x38, starting transfers between devices: 64.2 us -> 48.8 us  [swap_bit(): return lax.ppermute(values, 'dp', pairs)]
    all_to_all x2, waiting for transfers between devices: 25.6 us -> 13.5 us  [to_all(): lax.all_to_all(jnp.broadcast_to(values[None], (size,) + values.shape), ax...]
    all_to_all x1, blocking collectives: 14.5 us -> 26.1 us  [to_all(): lax.all_to_all(jnp.broadcast_to(values[None], (size,) + values.shape), ax...]
  transfers between devices with their start and end apart: 83 -> 68, of which waited for: 39 -> 41; matrix products, arithmetic and copies ran while one was open for 34% -> 26% of each run, Pallas kernels for 0% -> 3%
where the time goes in v3:
time: 731 us; the launch traced here: 722 us
  waiting for transfers between devices  284 us (39%)
  other arithmetic  110 us (15%)
  matrix products  106 us (15%)
  starting transfers between devices  86.3 us (12%)
  local copies, waits for them, and re-layouts  52.5 us (7%)
  between operations  32.2 us (4%)
  blocking collectives  26.1 us (4%)
  Pallas kernels  22.7 us (3%)
    ppermute x38, waiting for transfers between devices, swap_bit(): return lax.ppermute(values, 'dp', pairs)  237 us
    ppermute x38, starting transfers between devices, swap_bit(): return lax.ppermute(values, 'dp', pairs)  48.8 us
    dot_general x21, matrix products, product(): return jnp.dot(left, right, preferred_element_type=jnp.float32)  47.2 us
    dot_general x16, matrix products, product_tn(): lax.dot_general(left, right, (((0,), (0,)), ((), ())), preferred_element_...  30.5 us
    all_to_all x1, blocking collectives, to_all(): lax.all_to_all(jnp.broadcast_to(values[None], (size,) + values.shape), ax...  26.1 us
    pallas_call x6, Pallas kernels, kernel_call(): pl.pallas_call(kernel, out_shape=outputs, in_specs=[pl.BlockSpec(memory_s...  22.7 us
    dot_general x14, matrix products, product_nt(): lax.dot_general(left, right, (((1,), (1,)), ((), ())), preferred_element_...  21.3 us
    sub x7, other arithmetic, adam_step(): master - rate * (first_new / fix_one / (jnp.sqrt(second_new / fix_two) +...  20.5 us
  transfers between devices with their start and end apart: 68, of which 41 were waited for; matrix products, arithmetic and copies ran while one was open for 26% of the time, Pallas kernels for 3%

profile of v3, /device:TPU:0, one launch (start us, length us, event | category | flops | bytes accessed | tf_op | source)
XLA Modules:
  0.0 722.0 jit_solution(16215176680502291134)
XLA Ops:
  11.2 4.1 collective-permute-start
  22.8 3.8 all-to-all-start.4
  28.5 4.0 convert_element_type.599
  39.0 6.0 fusion.91
  45.4 3.9 collective-permute-done.3
  49.4 13.2 %all-to-all-start.5 = ((bf16[32,32,768]{2,1,0:T(8,128)(2,1)}), bf16[32,32,768]{2,1,0:T(8,128)(2,1)}, u32[]{:S(2)}, u32[]{:S(2)}) async-start(bf16[32,32,768]{2,1,0:T(8,128)(2,1)} %bitcast.30), calls=%async_computation.5 | async-start | bytes 3145728 | tf_op jit(solution)/shard_map/all_to_all | solution.py:460
  68.8 21.0 %collective-permute-done.4 = bf16[4,48,768]{2,1,0:T(8,128)(2,1)S(1)} collective-permute-done((bf16[4,48,768]{2,1,0:T(8,128)(2,1)S(1)}, bf16[4,48,768]{2,1,0:T(8,128)(2,1)S(1)}, u32[]{:S(2)}, u32[]{:S(2)}) %collective-permute-start.4) | collective-permute-done | bytes 294944 | tf_op jit(solution)/shard_map/ppermute | solution.py:219
  89.9 3.4 collective-permute-start.5
  93.3 4.0 collective-permute-done.6
  100.9 19.3 %collective-permute-done.5 = bf16[8,48,768]{2,1,0:T(8,128)(2,1)} collective-permute-done((bf16[8,48,768]{2,1,0:T(8,128)(2,1)S(1)}, bf16[8,48,768]{2,1,0:T(8,128)(2,1)}, u32[]{:S(2)}, u32[]{:S(2)}) %collective-permute-start.5) | collective-permute-done | bytes 589856 | tf_op jit(solution)/shard_map/ppermute | solution.py:219
  127.2 3.6 fusion.80
  136.2 5.6 collective-permute-done.10
  141.8 11.3 %collective-permute-done.9 = bf16[1,48,1792]{2,1,0:T(8,128)(2,1)S(1)} collective-permute-done((bf16[1,48,1792]{2,1,0:T(8,128)(2,1)S(1)}, bf16[1,48,1792]{2,1,0:T(8,128)(2,1)S(1)}, u32[]{:S(2)}, u32[]{:S(2)}) %collective-permute-start.9) | collective-permute-done | bytes 172064 | tf_op jit(solution)/shard_map/ppermute | solution.py:219
  155.4 4.5 shard_map.460
  159.9 11.2 %collective-permute-done.12 = bf16[2,48,1536]{2,1,0:T(8,128)(2,1)S(1)} collective-permute-done((bf16[2,48,1536]{2,1,0:T(8,128)(2,1)S(1)}, bf16[2,48,1536]{2,1,0:T(8,128)(2,1)S(1)}, u32[]{:S(2)}, u32[]{:S(2)}) %collective-permute-start.12) | collective-permute-done | bytes 294944 | tf_op jit(solution)/shard_map/ppermute | solution.py:219
  176.9 10.8 %collective-permute-done.15 = bf16[4,48,1536]{2,1,0:T(8,128)(2,1)S(1)} collective-permute-done((bf16[4,48,1536]{2,1,0:T(8,128)(2,1)S(1)}, bf16[4,48,1536]{2,1,0:T(8,128)(2,1)S(1)}, u32[]{:S(2)}, u32[]{:S(2)}) %collective-permute-start.15) | collective-permute-done | bytes 589856 | tf_op jit(solution)/shard_map/ppermute | solution.py:219
  187.8 4.8 collective-permute-done.14
  198.3 9.6 %multiply_convert_fusion.1 = (bf16[512,1536]{1,0:T(8,128)(2,1)S(1)}, f32[512,1536]{1,0:T(8,128)}, f32[512,1536]{1,0:T(8,128)}) fusion(bf16[512,768]{1,0:T(8,128)(2,1)S(1)} %constant_dynamic-update-slice_fusion, bf16[768,1536]{1,0:T(8,128)(2,1)S(1)} %convolution_convert_fusion.5), kind=kOutput, calls=%fused_computation.99 | convolution fusion | flops 1259077632 | bytes 11010048 | tf_op jit(solution)/shard_map/dot_general | solution.py:51
  212.9 23.6 %collective-permute-done.19 = bf16[8,48,1536]{2,1,0:T(8,128)(2,1)} collective-permute-done((bf16[8,48,1536]{2,1,0:T(8,128)(2,1)S(1)}, bf16[8,48,1536]{2,1,0:T(8,128)(2,1)}, u32[]{:S(2)}, u32[]{:S(2)}) %collective-permute-start.19) | collective-permute-done | bytes 1179680 | tf_op jit(solution)/shard_map/ppermute | solution.py:219
  276.2 26.1 %all_to_all.116 = bf16[16,32,768]{2,1,0:T(8,128)(2,1)} all-to-all(bf16[16,32,768]{2,1,0:T(8,128)(2,1)S(1)} %broadcast_in_dim.142), channel_id=1, replica_groups=mesh['dp'=16,'tensor'=2] {'dp'}, dimensions={0} | all-to-all | bytes 1572864 | tf_op jit(solution)/shard_map/all_to_all | solution.py:45
  304.9 5.5 fusion.300
  319.0 8.0 %all-to-all-done.7 = f32[32,2,1024]{2,1,0:T(2,128)S(1)} async-done(((f32[32,2,1024]{2,1,0:T(2,128)}), f32[32,2,1024]{2,1,0:T(2,128)S(1)}, u32[]{:S(2)}, u32[]{:S(2)}) %all-to-all-start.7) | async-done | bytes 262176 | tf_op jit(solution)/shard_map/all_to_all | solution.py:45
  327.4 6.5 fusion.264
  339.0 4.4 all-to-all-start.8
  345.4 18.0 %all-to-all-done.8 = bf16[16,32,768]{2,1,0:T(8,128)(2,1)} async-done(((bf16[16,32,768]{2,1,0:T(8,128)(2,1)}), bf16[16,32,768]{2,1,0:T(8,128)(2,1)}, u32[]{:S(2)}, u32[]{:S(2)}) %all-to-all-start.8) | async-done | bytes 786464 | tf_op jit(solution)/shard_map/all_to_all | solution.py:597
  367.3 3.1 add_convert_fusion.3
  382.7 3.2 shard_map.463
  403.6 10.6 %collective-permute-done.32 = bf16[8,1,48,768]{3,2,0,1:T(8,128)(2,1)S(1)} collective-permute-done((bf16[8,1,48,768]{3,2,0,1:T(8,128)(2,1)S(1)}, bf16[8,1,48,768]{3,2,0,1:T(8,128)(2,1)S(1)}, u32[]{:S(2)}, u32[]{:S(2)}) %collective-permute-start.32) | collective-permute-done | bytes 589856 | tf_op jit(solution)/shard_map/ppermute | solution.py:219
  432.1 3.2 shard_map.465
  447.7 27.4 %collective-permute-done.46 = bf16[8,1,48,768]{3,2,0,1:T(8,128)(2,1)S(1)} collective-permute-done((bf16[8,1,48,768]{3,2,0,1:T(8,128)(2,1)S(1)}, bf16[8,1,48,768]{3,2,0,1:T(8,128)(2,1)S(1)}, u32[]{:S(2)}, u32[]{:S(2)}) %collective-permute-start.46) | collective-permute-done | bytes 589856 | tf_op jit(solution)/shard_map/ppermute | solution.py:219
  491.5 7.1 shard_map.464
  502.6 17.2 %collective-permute-done.48 = bf16[8,1,48,384]{3,2,0,1:T(8,128)(2,1)S(1)} collective-permute-done((bf16[8,1,48,384]{3,2,0,1:T(8,128)(2,1)S(1)}, bf16[8,1,48,384]{3,2,0,1:T(8,128)(2,1)S(1)}, u32[]{:S(2)}, u32[]{:S(2)}) %collective-permute-start.48) | collective-permute-done | bytes 294944 | tf_op jit(solution)/shard_map/ppermute | solution.py:219
  528.7 15.7 %collective-permute-done.42 = bf16[2,1,48,2304]{3,2,0,1:T(8,128)(2,1)S(1)} collective-permute-done((bf16[2,1,48,2304]{3,2,0,1:T(8,128)(2,1)S(1)}, bf16[2,1,48,2304]{3,2,0,1:T(8,128)(2,1)S(1)}, u32[]{:S(2)}, u32[]{:S(2)}) %collective-permute-start.42) | collective-permute-done | bytes 442400 | tf_op jit(solution)/shard_map/ppermute | solution.py:219
  550.0 7.5 %collective-permute-done.43 = bf16[1,1,48,2304]{3,2,1,0:T(8,128)(2,1)S(1)} collective-permute-done((bf16[1,1,48,2304]{3,2,1,0:T(8,128)(2,1)S(1)}, bf16[1,1,48,2304]{3,2,1,0:T(8,128)(2,1)S(1)}, u32[]{:S(2)}, u32[]{:S(2)}) %collective-permute-start.43) | collective-permute-done | bytes 221216 | tf_op jit(solution)/shard_map/ppermute | solution.py:219
  570.2 3.4 fusion.90
  576.3 3.8 all-to-all-start.9
  582.9 4.5 all-to-all-done.9
  587.4 3.6 all-to-all-start.10
  602.1 21.6 %collective-permute-done.53 = bf16[4,1,48,1792]{3,2,0,1:T(8,128)(2,1)} collective-permute-done((bf16[4,1,48,1792]{3,2,0,1:T(8,128)(2,1)}, bf16[4,1,48,1792]{3,2,0,1:T(8,128)(2,1)}, u32[]{:S(2)}, u32[]{:S(2)}) %collective-permute-start.53) | collective-permute-done | bytes 688160 | tf_op jit(solution)/shard_map/ppermute | solution.py:219
  638.0 5.1 fusion.34
  643.9 8.3 %convolution_add_fusion = f32[1572,768]{1,0:T(8,128)} fusion(f32[1572,768]{1,0:T(8,128)S(1)} %fusion.34, bf16[512,768]{1,0:T(8,128)(2,1)} %collective-permute-done.25, bf16[512,768]{1,0:T(8,128)(2,1)} %bitcast.102, pred[]{:T(512)S(6)} %eq.398, f32[1024,1572]{0,1:T(8,128)S(1)} %bitcast.638, f32[1024]{0:T(1024)S(1)} %copy-done.193, f32[1024]{0:T(1024)S(1)} %copy-done.195, ...), kind=kOutput, calls=%fused_computation.80 | convolution fusion | flops 2490485760 | bytes 17682432 | tf_op jit(solution)/shard_map/dot_general | solution.py:55
  653.1 4.3 multiply_reduce_fusion
  661.0 4.1 collective-permute-done.55
  665.1 5.3 collective-permute-done.57
  685.2 5.5 all-to-all-done.11
  692.3 3.0 multiply_subtract_fusion.1
  696.3 3.4 multiply_subtract_fusion.3
  702.6 9.0 %multiply_subtract_fusion = (f32[1572,768]{1,0:T(8,128)}, f32[1572,768]{1,0:T(8,128)}, f32[1572,768]{1,0:T(8,128)}) fusion(f32[1572,768]{1,0:T(8,128)S(1)} %bitcast.616, f32[]{:T(128)} %bitcast.225, f32[]{:T(128)} %bitcast.224, f32[1572,768]{1,0:T(8,128)S(1)} %bitcast.618, f32[]{:T(128)S(6)} %min.3, f32[1572,768]{1,0:T(8,128)} %param.58, f32[1572,768]{1,0:T(8,128)} %param.57), kind=kLoop, calls=%fused_computation.73 | loop fusion | flops 19316736 | bytes 33804300 | tf_op jit(solution)/shard_map/sub | solution.py:201
  (945 shorter events, 273.7 us)
Async XLA Ops:
  7.2 120.0 %all-gather.3.cloned.1.call-start = ((), (), s32[]{:S(2)}) async-start(), calls=%async_computation.13 | async-start | bytes 5013504 | tf_op jit(solution)/shard_map/all_gather | solution.py:406
  11.2 22.8 %collective-permute-start = (bf16[1,48,768]{2,1,0:T(8,128)(2,1)S(1)}, bf16[1,48,768]{2,1,0:T(8,128)(2,1)S(1)}, u32[]{:S(2)}, u32[]{:S(2)}) collective-permute-start(bf16[1,48,768]{2,1,0:T(8,128)(2,1)S(1)} %get-tuple-element.851), channel_id=1, source_target_pairs={{0,16},{2,18},{4,20},{6,22},{8,24},{10,26},{12,28},{14,30},{16,0},... | collective-permute-start | bytes 221192 | tf_op jit(solution)/shard_map/ppermute | solution.py:219
  22.8 11.2 %all-to-all-start.4 = ((s32[32,1,129]{2,1,0:T(1,128)}), s32[32,1,129]{2,1,0:T(1,128)S(1)}, u32[]{:S(2)}, u32[]{:S(2)}) async-start(s32[32,1,129]{2,1,0:T(1,128)} %all_to_all.73), calls=%async_computation.4 | async-start | bytes 65536 | tf_op jit(solution)/shard_map/all_to_all | solution.py:446
  36.2 13.1 %collective-permute-start.3 = (bf16[2,48,1024]{2,1,0:T(8,128)(2,1)S(1)}, bf16[2,48,1024]{2,1,0:T(8,128)(2,1)S(1)}, u32[]{:S(2)}, u32[]{:S(2)}) collective-permute-start(bf16[2,48,1024]{2,1,0:T(8,128)(2,1)S(1)} %maximum_bitcast_fusion.5), channel_id=1, source_target_pairs={{0,16},{2,18},{4,20},{6,22},{8,24},{10,26},{12,28},{14,30},{16,0},... | collective-permute-start | bytes 589832 | tf_op jit(solution)/shard_map/ppermute | solution.py:219
  49.4 74.6 %all-to-all-start.5 = ((bf16[32,32,768]{2,1,0:T(8,128)(2,1)}), bf16[32,32,768]{2,1,0:T(8,128)(2,1)}, u32[]{:S(2)}, u32[]{:S(2)}) async-start(bf16[32,32,768]{2,1,0:T(8,128)(2,1)} %bitcast.30), calls=%async_computation.5 | async-start | bytes 3145728 | tf_op jit(solution)/shard_map/all_to_all | solution.py:460
  62.5 197.6 %all-gather.5.cloned.1.call-start = ((), (), s32[]{:S(2)}) async-start(), calls=%async_computation.14 | async-start | bytes 5013504 | tf_op jit(solution)/shard_map/all_gather | solution.py:406
  64.9 24.9 %collective-permute-start.4 = (bf16[4,48,768]{2,1,0:T(8,128)(2,1)S(1)}, bf16[4,48,768]{2,1,0:T(8,128)(2,1)S(1)}, u32[]{:S(2)}, u32[]{:S(2)}) collective-permute-start(bf16[4,48,768]{2,1,0:T(8,128)(2,1)S(1)} %bitcast.714), channel_id=1, source_target_pairs={{0,4},{2,6},{4,0},{6,2},{8,12},{10,14},{12,8},{14,10},{16,20},{18,... | collective-permute-start | bytes 884744 | tf_op jit(solution)/shard_map/ppermute | solution.py:219
  66.7 30.6 %collective-permute-start.6 = (bf16[4,48,1024]{2,1,0:T(8,128)(2,1)S(1)}, bf16[4,48,1024]{2,1,0:T(8,128)(2,1)S(1)}, u32[]{:S(2)}, u32[]{:S(2)}) collective-permute-start(bf16[4,48,1024]{2,1,0:T(8,128)(2,1)S(1)} %bitcast.698), channel_id=1, source_target_pairs={{0,2},{2,0},{4,6},{6,4},{8,10},{10,8},{12,14},{14,12},{16,18},{18,... | collective-permute-start | bytes 1179656 | tf_op jit(solution)/shard_map/ppermute | solution.py:219
  89.9 30.2 %collective-permute-start.5 = (bf16[8,48,768]{2,1,0:T(8,128)(2,1)S(1)}, bf16[8,48,768]{2,1,0:T(8,128)(2,1)}, u32[]{:S(2)}, u32[]{:S(2)}) collective-permute-start(bf16[8,48,768]{2,1,0:T(8,128)(2,1)S(1)} %bitcast.675), channel_id=1, source_target_pairs={{0,2},{2,0},{4,6},{6,4},{8,10},{10,8},{12,14},{14,12},{16,18},{18,... | collective-permute-start | bytes 1769480 | tf_op jit(solution)/shard_map/ppermute | solution.py:219
  97.4 25.1 %collective-permute-start.7 = (bf16[8,48,1024]{2,1,0:T(8,128)(2,1)S(1)}, bf16[8,48,1024]{2,1,0:T(8,128)(2,1)}, u32[]{:S(2)}, u32[]{:S(2)}) collective-permute-start(bf16[8,48,1024]{2,1,0:T(8,128)(2,1)S(1)} %bitcast.725), channel_id=1, source_target_pairs={{0,4},{2,6},{4,0},{6,2},{8,12},{10,14},{12,8},{14,10},{16,20},{18,... | collective-permute-start | bytes 2359304 | tf_op jit(solution)/shard_map/ppermute | solution.py:219
  135.6 17.6 %collective-permute-start.8 = (bf16[256,768]{1,0:T(8,128)(2,1)S(1)}, bf16[256,768]{1,0:T(8,128)(2,1)S(1)}, u32[]{:S(2)}, u32[]{:S(2)}) collective-permute-start(bf16[256,768]{1,0:T(8,128)(2,1)S(1)} %multiply_convert_fusion.5), channel_id=1, source_target_pairs={{0,1},{1,0},{2,3},{3,2},{4,5},{5,4},{6,7},{7,6},{8,9},{9,8},{10,11... | collective-permute-start | bytes 1179656 | tf_op jit(solution)/shard_map/ppermute | solution.py:31
  135.7 17.4 %collective-permute-start.9 = (bf16[1,48,1792]{2,1,0:T(8,128)(2,1)S(1)}, bf16[1,48,1792]{2,1,0:T(8,128)(2,1)S(1)}, u32[]{:S(2)}, u32[]{:S(2)}) collective-permute-start(bf16[1,48,1792]{2,1,0:T(8,128)(2,1)S(1)} %bitcast.740), channel_id=1, source_target_pairs={{0,16},{2,18},{4,20},{6,22},{8,24},{10,26},{12,28},{14,30},{16,0},... | collective-permute-start | bytes 516104 | tf_op jit(solution)/shard_map/ppermute | solution.py:219
  154.0 19.8 %collective-permute-start.11 = (bf16[2,48,1792]{2,1,0:T(8,128)(2,1)S(1)}, bf16[2,48,1792]{2,1,0:T(8,128)(2,1)S(1)}, u32[]{:S(2)}, u32[]{:S(2)}) collective-permute-start(bf16[2,48,1792]{2,1,0:T(8,128)(2,1)S(1)} %maximum_bitcast_fusion), channel_id=1, source_target_pairs={{0,8},{2,10},{4,12},{6,14},{8,0},{10,2},{12,4},{14,6},{16,24},{18,... | collective-permute-start | bytes 1032200 | tf_op jit(solution)/shard_map/ppermute | solution.py:219
  154.1 17.0 %collective-permute-start.12 = (bf16[2,48,1536]{2,1,0:T(8,128)(2,1)S(1)}, bf16[2,48,1536]{2,1,0:T(8,128)(2,1)S(1)}, u32[]{:S(2)}, u32[]{:S(2)}) collective-permute-start(bf16[2,48,1536]{2,1,0:T(8,128)(2,1)S(1)} %maximum_bitcast_fusion.1), channel_id=1, source_target_pairs={{0,16},{2,18},{4,20},{6,22},{8,24},{10,26},{12,28},{14,30},{16,0},... | collective-permute-start | bytes 884744 | tf_op jit(solution)/shard_map/ppermute | solution.py:219
  173.9 13.7 %collective-permute-start.15 = (bf16[4,48,1536]{2,1,0:T(8,128)(2,1)S(1)}, bf16[4,48,1536]{2,1,0:T(8,128)(2,1)S(1)}, u32[]{:S(2)}, u32[]{:S(2)}) collective-permute-start(bf16[4,48,1536]{2,1,0:T(8,128)(2,1)S(1)} %bitcast.677), channel_id=1, source_target_pairs={{0,2},{2,0},{4,6},{6,4},{8,10},{10,8},{12,14},{14,12},{16,18},{18,... | collective-permute-start | bytes 1769480 | tf_op jit(solution)/shard_map/ppermute | solution.py:219
  174.7 19.3 %collective-permute-start.13 = (f32[256,768]{1,0:T(8,128)S(1)}, f32[256,768]{1,0:T(8,128)S(1)}, u32[]{:S(2)}, u32[]{:S(2)}) collective-permute-start(f32[256,768]{1,0:T(8,128)S(1)} %slice.623), channel_id=1, source_target_pairs={{0,1},{1,0},{2,3},{3,2},{4,5},{5,4},{6,7},{7,6},{8,9},{9,8},{10,11... | collective-permute-start | bytes 2359304 | tf_op jit(solution)/shard_map/ppermute | solution.py:31
  174.7 17.9 %collective-permute-start.14 = (bf16[4,48,1792]{2,1,0:T(8,128)(2,1)S(1)}, bf16[4,48,1792]{2,1,0:T(8,128)(2,1)S(1)}, u32[]{:S(2)}, u32[]{:S(2)}) collective-permute-start(bf16[4,48,1792]{2,1,0:T(8,128)(2,1)S(1)} %bitcast.668), channel_id=1, source_target_pairs={{0,4},{2,6},{4,0},{6,2},{8,12},{10,14},{12,8},{14,10},{16,20},{18,... | collective-permute-start | bytes 2064392 | tf_op jit(solution)/shard_map/ppermute | solution.py:219
  197.5 39.0 %collective-permute-start.19 = (bf16[8,48,1536]{2,1,0:T(8,128)(2,1)S(1)}, bf16[8,48,1536]{2,1,0:T(8,128)(2,1)}, u32[]{:S(2)}, u32[]{:S(2)}) collective-permute-start(bf16[8,48,1536]{2,1,0:T(8,128)(2,1)S(1)} %bitcast.658), channel_id=1, source_target_pairs={{0,4},{2,6},{4,0},{6,2},{8,12},{10,14},{12,8},{14,10},{16,20},{18,... | collective-permute-start | bytes 3538952 | tf_op jit(solution)/shard_map/ppermute | solution.py:219
  210.6 29.0 %collective-permute-start.17 = (f32[256,768]{1,0:T(8,128)S(1)}, f32[256,768]{1,0:T(8,128)}, u32[]{:S(2)}, u32[]{:S(2)}) collective-permute-start(f32[256,768]{1,0:T(8,128)S(1)} %slice.626), channel_id=1, source_target_pairs={{0,1},{1,0},{2,3},{3,2},{4,5},{5,4},{6,7},{7,6},{8,9},{9,8},{10,11... | collective-permute-start | bytes 2359304 | tf_op jit(solution)/shard_map/ppermute | solution.py:31
  210.9 32.8 %collective-permute-start.18 = (bf16[8,48,1792]{2,1,0:T(8,128)(2,1)}, bf16[8,48,1792]{2,1,0:T(8,128)(2,1)S(1)}, u32[]{:S(2)}, u32[]{:S(2)}) collective-permute-start(bf16[8,48,1792]{2,1,0:T(8,128)(2,1)} %bitcast.644), channel_id=1, source_target_pairs={{0,2},{2,0},{4,6},{6,4},{8,10},{10,8},{12,14},{14,12},{16,18},{18,... | collective-permute-start | bytes 4128776 | tf_op jit(solution)/shard_map/ppermute | solution.py:219
  313.9 13.2 %all-to-all-start.7 = ((f32[32,2,1024]{2,1,0:T(2,128)}), f32[32,2,1024]{2,1,0:T(2,128)S(1)}, u32[]{:S(2)}, u32[]{:S(2)}) async-start(f32[32,2,1024]{2,1,0:T(2,128)} %broadcast_in_dim.144), calls=%async_computation.7 | async-start | bytes 524288 | tf_op jit(solution)/shard_map/all_to_all | solution.py:45
  339.0 24.5 %all-to-all-start.8 = ((bf16[16,32,768]{2,1,0:T(8,128)(2,1)}), bf16[16,32,768]{2,1,0:T(8,128)(2,1)}, u32[]{:S(2)}, u32[]{:S(2)}) async-start(bf16[16,32,768]{2,1,0:T(8,128)(2,1)} %bitcast.667), calls=%async_computation.8 | async-start | bytes 1572864 | tf_op jit(solution)/shard_map/all_to_all | solution.py:597
  343.4 331.3 %reduce-scatter.2.cloned.1.call-start = ((), (), s32[]{:S(2)}) async-start(), calls=%async_computation.15 | async-start | bytes 5013504 | tf_op jit(solution)/shard_map/reduce_scatter | solution.py:611
  389.0 11.5 %collective-permute-start.29 = (f32[256,768]{1,0:T(8,128)}, f32[256,768]{1,0:T(8,128)S(1)}, u32[]{:S(2)}, u32[]{:S(2)}) collective-permute-start(f32[256,768]{1,0:T(8,128)} %slice.646), channel_id=1, source_target_pairs={{0,1},{1,0},{2,3},{3,2},{4,5},{5,4},{6,7},{7,6},{8,9},{9,8},{10,11... | collective-permute-start | bytes 2359304 | tf_op jit(solution)/shard_map/ppermute | solution.py:31
  394.8 19.4 %collective-permute-start.32 = (bf16[8,1,48,768]{3,2,0,1:T(8,128)(2,1)S(1)}, bf16[8,1,48,768]{3,2,0,1:T(8,128)(2,1)S(1)}, u32[]{:S(2)}, u32[]{:S(2)}) collective-permute-start(bf16[8,1,48,768]{3,2,0,1:T(8,128)(2,1)S(1)} %slice_bitcast_fusion.17), channel_id=1, source_target_pairs={{0,2},{2,0},{4,6},{6,4},{8,10},{10,8},{12,14},{14,12},{16,18},{18,... | collective-permute-start | bytes 1769480 | tf_op jit(solution)/shard_map/ppermute | solution.py:219
  397.5 18.1 %collective-permute-start.33 = (bf16[4,2,48,768]{3,2,1,0:T(8,128)(2,1)S(1)}, bf16[4,2,48,768]{3,2,1,0:T(8,128)(2,1)S(1)}, u32[]{:S(2)}, u32[]{:S(2)}) collective-permute-start(bf16[4,2,48,768]{3,2,1,0:T(8,128)(2,1)S(1)} %slice_bitcast_fusion.15), channel_id=1, source_target_pairs={{0,4},{2,6},{4,0},{6,2},{8,12},{10,14},{12,8},{14,10},{16,20},{18,... | collective-permute-start | bytes 1769480 | tf_op jit(solution)/shard_map/ppermute | solution.py:219
  403.5 13.8 %collective-permute-start.30 = (bf16[256,768]{1,0:T(8,128)(2,1)S(1)}, bf16[256,768]{1,0:T(8,128)(2,1)S(1)}, u32[]{:S(2)}, u32[]{:S(2)}) collective-permute-start(bf16[256,768]{1,0:T(8,128)(2,1)S(1)} %add_convert_fusion.2), channel_id=1, source_target_pairs={{0,1},{1,0},{2,3},{3,2},{4,5},{5,4},{6,7},{7,6},{8,9},{9,8},{10,11... | collective-permute-start | bytes 1179656 | tf_op jit(solution)/shard_map/ppermute | solution.py:31
  423.4 54.8 %collective-permute-start.31 = (f32[256,768]{1,0:T(8,128)}, f32[256,768]{1,0:T(8,128)}, u32[]{:S(2)}, u32[]{:S(2)}) collective-permute-start(f32[256,768]{1,0:T(8,128)} %slice.519), channel_id=1, source_target_pairs={{0,1},{1,0},{2,3},{3,2},{4,5},{5,4},{6,7},{7,6},{8,9},{9,8},{10,11... | collective-permute-start | bytes 2359304 | tf_op jit(solution)/shard_map/ppermute | solution.py:31
  426.0 57.4 %collective-permute-start.34 = (bf16[8,1,48,1536]{3,2,0,1:T(8,128)(2,1)}, bf16[8,1,48,1536]{3,2,0,1:T(8,128)(2,1)}, u32[]{:S(2)}, u32[]{:S(2)}) collective-permute-start(bf16[8,1,48,1536]{3,2,0,1:T(8,128)(2,1)} %slice_bitcast_fusion.5), channel_id=1, source_target_pairs={{0,2},{2,0},{4,6},{6,4},{8,10},{10,8},{12,14},{14,12},{16,18},{18,... | collective-permute-start | bytes 3538952 | tf_op jit(solution)/shard_map/ppermute | solution.py:219
  428.6 56.7 %collective-permute-start.35 = (bf16[4,2,48,1536]{3,2,1,0:T(8,128)(2,1)}, bf16[4,2,48,1536]{3,2,1,0:T(8,128)(2,1)}, u32[]{:S(2)}, u32[]{:S(2)}) collective-permute-start(bf16[4,2,48,1536]{3,2,1,0:T(8,128)(2,1)} %slice_bitcast_fusion.3), channel_id=1, source_target_pairs={{0,4},{2,6},{4,0},{6,2},{8,12},{10,14},{12,8},{14,10},{16,20},{18,... | collective-permute-start | bytes 3538952 | tf_op jit(solution)/shard_map/ppermute | solution.py:219
  442.5 32.6 %collective-permute-start.46 = (bf16[8,1,48,768]{3,2,0,1:T(8,128)(2,1)S(1)}, bf16[8,1,48,768]{3,2,0,1:T(8,128)(2,1)S(1)}, u32[]{:S(2)}, u32[]{:S(2)}) collective-permute-start(bf16[8,1,48,768]{3,2,0,1:T(8,128)(2,1)S(1)} %slice_bitcast_fusion.13), channel_id=1, source_target_pairs={{0,2},{2,0},{4,6},{6,4},{8,10},{10,8},{12,14},{14,12},{16,18},{18,... | collective-permute-start | bytes 1769480 | tf_op jit(solution)/shard_map/ppermute | solution.py:219
  444.3 32.8 %collective-permute-start.50 = (bf16[4,2,48,768]{3,2,1,0:T(8,128)(2,1)S(1)}, bf16[4,2,48,768]{3,2,1,0:T(8,128)(2,1)S(1)}, u32[]{:S(2)}, u32[]{:S(2)}) collective-permute-start(bf16[4,2,48,768]{3,2,1,0:T(8,128)(2,1)S(1)} %slice_bitcast_fusion.11), channel_id=1, source_target_pairs={{0,4},{2,6},{4,0},{6,2},{8,12},{10,14},{12,8},{14,10},{16,20},{18,... | collective-permute-start | bytes 1769480 | tf_op jit(solution)/shard_map/ppermute | solution.py:219
  487.6 33.0 %collective-permute-start.37 = (bf16[4,1,48,2304]{3,2,0,1:T(8,128)(2,1)S(1)}, bf16[4,1,48,2304]{3,2,0,1:T(8,128)(2,1)S(1)}, u32[]{:S(2)}, u32[]{:S(2)}) collective-permute-start(bf16[4,1,48,2304]{3,2,0,1:T(8,128)(2,1)S(1)} %fusion.121), channel_id=1, source_target_pairs={{0,4},{2,6},{4,0},{6,2},{8,12},{10,14},{12,8},{14,10},{16,20},{18,... | collective-permute-start | bytes 2654216 | tf_op jit(solution)/shard_map/ppermute | solution.py:219
  489.5 31.3 %collective-permute-start.38 = (bf16[4,1,48,2304]{3,2,0,1:T(8,128)(2,1)S(1)}, bf16[4,1,48,2304]{3,2,0,1:T(8,128)(2,1)S(1)}, u32[]{:S(2)}, u32[]{:S(2)}) collective-permute-start(bf16[4,1,48,2304]{3,2,0,1:T(8,128)(2,1)S(1)} %fusion.122), channel_id=1, source_target_pairs={{0,2},{2,0},{4,6},{6,4},{8,10},{10,8},{12,14},{14,12},{16,18},{18,... | collective-permute-start | bytes 2654216 | tf_op jit(solution)/shard_map/ppermute | solution.py:219
  499.6 20.1 %collective-permute-start.48 = (bf16[8,1,48,384]{3,2,0,1:T(8,128)(2,1)S(1)}, bf16[8,1,48,384]{3,2,0,1:T(8,128)(2,1)S(1)}, u32[]{:S(2)}, u32[]{:S(2)}) collective-permute-start(bf16[8,1,48,384]{3,2,0,1:T(8,128)(2,1)S(1)} %slice_bitcast_fusion.27), channel_id=1, source_target_pairs={{0,2},{2,0},{4,6},{6,4},{8,10},{10,8},{12,14},{14,12},{16,18},{18,... | collective-permute-start | bytes 884744 | tf_op jit(solution)/shard_map/ppermute | solution.py:219
  523.0 34.6 %collective-permute-start.39 = (f32[256,768]{1,0:T(8,128)S(1)}, f32[256,768]{1,0:T(8,128)S(1)}, u32[]{:S(2)}, u32[]{:S(2)}) collective-permute-start(f32[256,768]{1,0:T(8,128)S(1)} %slice.660), channel_id=1, source_target_pairs={{0,1},{1,0},{2,3},{3,2},{4,5},{5,4},{6,7},{7,6},{8,9},{9,8},{10,11... | collective-permute-start | bytes 2359304 | tf_op jit(solution)/shard_map/ppermute | solution.py:31
  523.1 21.3 %collective-permute-start.42 = (bf16[2,1,48,2304]{3,2,0,1:T(8,128)(2,1)S(1)}, bf16[2,1,48,2304]{3,2,0,1:T(8,128)(2,1)S(1)}, u32[]{:S(2)}, u32[]{:S(2)}) collective-permute-start(bf16[2,1,48,2304]{3,2,0,1:T(8,128)(2,1)S(1)} %fusion.163), channel_id=1, source_target_pairs={{0,8},{2,10},{4,12},{6,14},{8,0},{10,2},{12,4},{14,6},{16,24},{18,... | collective-permute-start | bytes 1327112 | tf_op jit(solution)/shard_map/ppermute | solution.py:219
  525.2 22.8 %collective-permute-start.44 = (bf16[1,2,48,2304]{3,2,1,0:T(8,128)(2,1)S(1)}, bf16[1,2,48,2304]{3,2,1,0:T(8,128)(2,1)S(1)}, u32[]{:S(2)}, u32[]{:S(2)}) collective-permute-start(bf16[1,2,48,2304]{3,2,1,0:T(8,128)(2,1)S(1)} %fusion.162), channel_id=1, source_target_pairs={{0,16},{2,18},{4,20},{6,22},{8,24},{10,26},{12,28},{14,30},{16,0},... | collective-permute-start | bytes 1327112 | tf_op jit(solution)/shard_map/ppermute | solution.py:219
  527.2 21.6 %collective-permute-start.51 = (bf16[4,2,48,768]{3,2,1,0:T(8,128)(2,1)S(1)}, bf16[4,2,48,768]{3,2,1,0:T(8,128)(2,1)S(1)}, u32[]{:S(2)}, u32[]{:S(2)}) collective-permute-start(bf16[4,2,48,768]{3,2,1,0:T(8,128)(2,1)S(1)} %slice_bitcast_fusion.9), channel_id=1, source_target_pairs={{0,4},{2,6},{4,0},{6,2},{8,12},{10,14},{12,8},{14,10},{16,20},{18,... | collective-permute-start | bytes 1769480 | tf_op jit(solution)/shard_map/ppermute | solution.py:219
  544.5 13.0 %collective-permute-start.43 = (bf16[1,1,48,2304]{3,2,1,0:T(8,128)(2,1)S(1)}, bf16[1,1,48,2304]{3,2,1,0:T(8,128)(2,1)S(1)}, u32[]{:S(2)}, u32[]{:S(2)}) collective-permute-start(bf16[1,1,48,2304]{3,2,1,0:T(8,128)(2,1)S(1)} %fusion.185), channel_id=1, source_target_pairs={{0,16},{2,18},{4,20},{6,22},{8,24},{10,26},{12,28},{14,30},{16,0},... | collective-permute-start | bytes 663560 | tf_op jit(solution)/shard_map/ppermute | solution.py:219
  548.8 50.9 %collective-permute-start.45 = (bf16[1,1,48,2304]{3,2,1,0:T(8,128)(2,1)}, bf16[1,1,48,2304]{3,2,1,0:T(8,128)(2,1)}, u32[]{:S(2)}, u32[]{:S(2)}) collective-permute-start(bf16[1,1,48,2304]{3,2,1,0:T(8,128)(2,1)} %fusion.186), channel_id=1, source_target_pairs={{0,8},{2,10},{4,12},{6,14},{8,0},{10,2},{12,4},{14,6},{16,24},{18,... | collective-permute-start | bytes 663560 | tf_op jit(solution)/shard_map/ppermute | solution.py:219
  567.8 27.3 %collective-permute-start.47 = (bf16[8,1,48,640]{3,2,0,1:T(8,128)(2,1)}, bf16[8,1,48,640]{3,2,0,1:T(8,128)(2,1)}, u32[]{:S(2)}, u32[]{:S(2)}) collective-permute-start(bf16[8,1,48,640]{3,2,0,1:T(8,128)(2,1)} %slice_bitcast_fusion.19), channel_id=1, source_target_pairs={{0,2},{2,0},{4,6},{6,4},{8,10},{10,8},{12,14},{14,12},{16,18},{18,... | collective-permute-start | bytes 1474568 | tf_op jit(solution)/shard_map/ppermute | solution.py:219
  576.3 11.1 %all-to-all-start.9 = ((f32[32,1,168]{2,1,0:T(1,128)}), f32[32,1,168]{2,1,0:T(1,128)S(1)}, u32[]{:S(2)}, u32[]{:S(2)}) async-start(f32[32,1,168]{2,1,0:T(1,128)} %all_to_all.91), calls=%async_computation.9 | async-start | bytes 65536 | tf_op jit(solution)/shard_map/all_to_all | solution.py:725
  587.4 41.6 %all-to-all-start.10 = ((bf16[32,32,768]{2,1,0:T(8,128)(2,1)}), bf16[32,32,768]{2,1,0:T(8,128)(2,1)}, u32[]{:S(2)}, u32[]{:S(2)}) async-start(bf16[32,32,768]{2,1,0:T(8,128)(2,1)} %bitcast.697), calls=%async_computation.10 | async-start | bytes 3145728 | tf_op jit(solution)/shard_map/all_to_all | solution.py:460
  593.4 30.3 %collective-permute-start.53 = (bf16[4,1,48,1792]{3,2,0,1:T(8,128)(2,1)}, bf16[4,1,48,1792]{3,2,0,1:T(8,128)(2,1)}, u32[]{:S(2)}, u32[]{:S(2)}) collective-permute-start(bf16[4,1,48,1792]{3,2,0,1:T(8,128)(2,1)} %fusion.134), channel_id=1, source_target_pairs={{0,2},{2,0},{4,6},{6,4},{8,10},{10,8},{12,14},{14,12},{16,18},{18,... | collective-permute-start | bytes 2064392 | tf_op jit(solution)/shard_map/ppermute | solution.py:219
  598.2 28.3 %collective-permute-start.49 = (bf16[4,1,48,1792]{3,2,0,1:T(8,128)(2,1)S(1)}, bf16[4,1,48,1792]{3,2,0,1:T(8,128)(2,1)}, u32[]{:S(2)}, u32[]{:S(2)}) collective-permute-start(bf16[4,1,48,1792]{3,2,0,1:T(8,128)(2,1)S(1)} %fusion.135), channel_id=1, source_target_pairs={{0,4},{2,6},{4,0},{6,2},{8,12},{10,14},{12,8},{14,10},{16,20},{18,... | collective-permute-start | bytes 2064392 | tf_op jit(solution)/shard_map/ppermute | solution.py:219
  633.4 24.0 %collective-permute-start.54 = (bf16[1,2,48,1792]{3,2,1,0:T(8,128)(2,1)}, bf16[1,2,48,1792]{3,2,1,0:T(8,128)(2,1)}, u32[]{:S(2)}, u32[]{:S(2)}) collective-permute-start(bf16[1,2,48,1792]{3,2,1,0:T(8,128)(2,1)} %fusion.177), channel_id=1, source_target_pairs={{0,16},{2,18},{4,20},{6,22},{8,24},{10,26},{12,28},{14,30},{16,0},... | collective-permute-start | bytes 1032200 | tf_op jit(solution)/shard_map/ppermute | solution.py:219
  636.4 23.4 %collective-permute-start.56 = (bf16[2,1,48,1792]{3,2,0,1:T(8,128)(2,1)}, bf16[2,1,48,1792]{3,2,0,1:T(8,128)(2,1)}, u32[]{:S(2)}, u32[]{:S(2)}) collective-permute-start(bf16[2,1,48,1792]{3,2,0,1:T(8,128)(2,1)} %fusion.178), channel_id=1, source_target_pairs={{0,8},{2,10},{4,12},{6,14},{8,0},{10,2},{12,4},{14,6},{16,24},{18,... | collective-permute-start | bytes 1032200 | tf_op jit(solution)/shard_map/ppermute | solution.py:219
  (265 other events, 2944.0 us)
Sparse Core Ops, SparseCore 0:
  11.3 115.8 all-gather.2
  130.4 104.9 all-gather.4
  377.2 140.9 reduce-scatter.1

commit v4 on v3

--- a/solution.py
+++ b/solution.py
@@ -221,31 +221,32 @@
 
 class Gather:
     def __init__(self, shard, turn):
-        self.held = shard[None]
+        self.held, self.got = shard[None], None
         self.order = bit_order(turn)
         self.bits = []
 
-    def step(self):
+    def settle(self):
+        if self.got is None:
+            return
         bit = self.order[len(self.bits)]
-        got = swap_bit(self.held, bit)
         block = self.held.shape[1:]
         above = sum(1 for other in self.bits if other > bit)
         shape = (2**above, 2 ** (len(self.bits) - above)) + block
-        held = jnp.stack([self.held.reshape(shape), got.reshape(shape)], axis=1)
-        self.held = held.reshape((-1,) + block)
+        held = jnp.stack([self.held.reshape(shape), self.got.reshape(shape)], axis=1)
+        self.held, self.got = held.reshape((-1,) + block), None
         self.bits.append(bit)
 
-    def columns(self, first, last):
-        part = Gather(self.held[0, :, first:last], 0)
-        part.held, part.order, part.bits = self.held[:, :, first:last], self.order, list(self.bits)
-        return part
+    def step(self):
+        self.settle()
+        self.got = swap_bit(self.held, self.order[len(self.bits)])
 
     def left(self):
-        return len(self.order) - len(self.bits)
+        return len(self.order) - len(self.bits) - (self.got is not None)
 
     def rows(self):
         while self.left():
             self.step()
+        self.settle()
         return self.held.reshape(-1, self.held.shape[2])
 
 
@@ -253,17 +254,22 @@
     def __init__(self, grads, turn):
         groups = lax.axis_size("dp")
         self.held = grads.reshape((groups, grads.shape[0] // groups, grads.shape[1]))
+        self.got = None
         self.order = bit_order(turn)
         self.bits = sorted(self.order, reverse=True)
 
+    def settle(self):
+        if self.got is not None:
+            held = self.held.astype(jnp.float32) + self.got.astype(jnp.float32)
+            self.held, self.got = held.reshape((-1,) + held.shape[2:]), None
+
     def step(self):
+        self.settle()
         bit = self.order.pop()
         above = self.bits.index(bit)
-        block = self.held.shape[1:]
-        halves = self.held.reshape((2**above, 2, -1) + block)
-        got = swap_bit(halves[:, 1].astype(jnp.bfloat16), bit)
-        held = halves[:, 0].astype(jnp.float32) + got.astype(jnp.float32)
-        self.held = held.reshape((-1,) + block)
+        halves = self.held.reshape((2**above, 2, -1) + self.held.shape[1:])
+        self.got = swap_bit(halves[:, 1].astype(jnp.bfloat16), bit)
+        self.held = halves[:, 0]
         self.bits.remove(bit)
 
     def left(self):
@@ -272,11 +278,14 @@
     def rows(self):
         while self.left():
             self.step()
+        self.settle()
         return self.held[0]
 
 
 def joined(scatters):
     whole = Scatter(jnp.zeros((lax.axis_size("dp"), 1)), 0)
+    for scatter in scatters:
+        scatter.settle()
     whole.held = jnp.concatenate([scatter.held for scatter in scatters], axis=2)
     whole.order, whole.bits = list(scatters[0].order), list(scatters[0].bits)
     return whole
@@ -289,9 +298,10 @@
 
 
 def meet(value, movers):
-    tied = tie(value, *[mover.held for mover in movers])
-    for mover, held in zip(movers, tied[1:]):
-        mover.held = held
+    sent = [mover for mover in movers if mover.got is not None]
+    tied = tie(value, *[mover.got for mover in sent])
+    for mover, got in zip(sent, tied[1:]):
+        mover.got = got
     return tied[0]
 
 
@@ -472,11 +482,13 @@
     asked_rows = meet(picked_rows(asked_first), attend_gathers)
     got = answer(asked_rows)
     advance(attend_gathers)
+    late_gathers[0].held, late_gathers[1].held = tie(
+        meet(late_gathers[0].held, attend_gathers), late_gathers[1].held
+    )
     advance(attend_gathers)
-    got = meet(got, attend_gathers)
-    got, feed_weights[0], late_gathers[0].held, late_gathers[1].held = tie(
-        got, feed_weights[0], late_gathers[0].held, late_gathers[1].held
-    )
+    advance(late_gathers)
+    got = meet(got, attend_gathers + late_gathers)
+    got, feed_weights[0] = tie(got, feed_weights[0])
     advance(late_gathers)
     expand_zero = pick_rows(order.astype(low), feed_weights[0][0])
     shrink_zero = pick_rows(order.astype(low), feed_weights[0][1])
@@ -508,20 +520,19 @@
     scored_row = spots_group[:, None] == row_places[None, :]
     heads = ((0, 0), (0, blocks), (1, 0))
     enc_start = start[0] + flipped(first_two[:, 2 * blocks :]).astype(jnp.float32)
-    enc_rows = spread(norm_rows(enc_start, gains[0]).astype(low))
-    enc_pair = meet(low_product(enc_rows, first_one), late_gathers)
+    enc_rows = meet(norm_rows(enc_start, gains[0]).astype(low), late_gathers)
     advance(late_gathers)
+    enc_rows = spread(enc_rows)
+    enc_pair = low_product(enc_rows, first_one)
     enc_arrays = (enc_pair, low_product(enc_rows, value_zero))
     enc_mixed = attend_forward(enc_arrays, heads, blocks, encoder_mask)
     enc_mixed = meet(enc_mixed, late_gathers)
     advance(late_gathers)
     stream = enc_start + collect(product_nt(enc_mixed, leave_zero))
 
-    feed_rows = meet(norm_rows(stream, gains[1]).astype(low), late_gathers)
-    advance(late_gathers)
-    feed_rows = spread(feed_rows)
+    feed_rows = spread(norm_rows(stream, gains[1]).astype(low))
     feed_inner = product(feed_rows, expand_zero)
-    feed_hidden = gelu_exact(feed_inner).astype(low)
+    feed_hidden = meet(gelu_exact(feed_inner).astype(low), late_gathers)
     after_feed = stream + collect(product_nt(feed_hidden, shrink_zero))
     memory = norm_rows(after_feed, gains[2]).astype(low)
 
@@ -664,17 +675,15 @@
     grad_decoded = grad_decoded + place_exact(scored_row[:, :half].T, grad_rows)
     start_decoded = grad_decoded.astype(low)
 
-    grad_all = meet(grad_stream.astype(low), cross_scatters + feed_scatters)
-    early = [joined([cross_scatters[b], feed_scatters[b]]) for b in range(2)]
-    advance(early)
-    grad_all = spread(grad_all)
+    grad_all = spread(grad_stream.astype(low))
     grad_mixed = low_product(grad_all, leave_zero)
     first_scatters = [
         Scatter(beside(low_grad(grad_all, enc_mixed), flipped(start_decoded)), 0)
     ]
     advance(first_scatters)
     grad_pair, grad_value = attend_backward(enc_arrays, heads, blocks, grad_mixed, encoder_mask)
-    grad_pair = meet(grad_pair, early)
+    grad_pair = meet(grad_pair, cross_scatters + feed_scatters)
+    early = [joined([cross_scatters[b], feed_scatters[b]]) for b in range(2)]
     advance(early)
     back = product_nt(grad_pair, first_one) + product_nt(grad_value, value_zero)
     first_scatters += [
@@ -684,7 +693,8 @@
     advance(first_scatters[1:])
     grad_values, gain_zero = norm_backward(enc_start, gains[0], collect(back))
     start_stream = (grad_stream + grad_values).astype(low)
-    first_scatters.append(Scatter(flipped(start_stream), 1))
+    place_scatter = Scatter(flipped(start_stream), 1)
+    advance([place_scatter])
 
     start_rows = reordered(jnp.concatenate([start_stream, start_decoded])).astype(low)
 
@@ -695,16 +705,25 @@
         return product_tn(chosen_rows(asked, rows_owned), got)
 
     got = returned(slot_in(0))
-    advance(first_scatters[3:])
+    got = meet(got, early)
+    got = meet(got, self_scatters + first_scatters + [place_scatter])
+    got, last_grads = tie(got, last_grads)
     late = [
         joined([self_scatters[0], first_scatters[0], first_scatters[2]]),
-        joined([self_scatters[1], first_scatters[1], first_scatters[3]]),
+        joined([self_scatters[1], first_scatters[1], place_scatter]),
     ]
     advance(early)
     advance(late)
-    got = meet(got, early + late)
-    early_rows = [scatter.rows() for scatter in early]
-    late_rows = [scatter.rows() for scatter in late]
+    gain_partial = jnp.concatenate(
+        [
+            reordered_exact(jnp.stack([gain_zero, gain_one, gain_two, gain_three, gain_four])),
+            jnp.stack([gain_five, gain_six]),
+        ]
+    )
+    gain_partial, got = tie(gain_partial, got)
+    gain_own = jnp.sum(
+        lax.all_to_all(gain_partial.reshape(devices, -1), EVERY, 0, 0, tiled=True), axis=0
+    )
     table_grad = grad_table + placed(asked_first, got)
     table_grad = lax.while_loop(
         lambda state: state[0] < rounds_all,
@@ -714,16 +733,16 @@
         ),
         (jnp.int32(1), table_grad),
     )[1]
-
-    gain_partial = jnp.concatenate(
-        [
-            reordered_exact(jnp.stack([gain_zero, gain_one, gain_two, gain_three, gain_four])),
-            jnp.stack([gain_five, gain_six]),
-        ]
-    )
-    gain_own = jnp.sum(
-        lax.all_to_all(gain_partial.reshape(devices, -1), EVERY, 0, 0, tiled=True), axis=0
-    )
+    squares = jnp.sum(table_grad * table_grad)
+    squares, gain_own = tie(squares, gain_own)
+    squares = meet(squares, early + late)
+    advance(early)
+    advance(late)
+    squares = meet(squares, early + late)
+    advance(late)
+    early_rows = [scatter.rows() for scatter in early]
+    late_rows = [scatter.rows() for scatter in late]
+    stream_place = late_rows[1][:, 4 * blocks :]
     def attention_grads(outer, keyval):
         return [outer[:, :blocks], keyval[:, :blocks], keyval[:, blocks:], outer[:, blocks:]]
 
@@ -734,7 +753,6 @@
         late_rows[0][:, 2 * blocks :], [blocks, blocks + half], axis=1
     )
     first_pieces = pieces_of(late_rows[1], 2 * blocks, 2) + [first_value, first_leave]
-    stream_place = late_rows[1][:, 4 * blocks :]
     entry_grad = jnp.stack(
         [jnp.stack(pieces[:3]) for pieces in (first_pieces, self_pieces, cross_pieces)]
     )
@@ -742,8 +760,8 @@
     expand_grad = jnp.stack([expand_rows, last_grads[0]])
     shrink_grad = flipped(jnp.stack([shrink_rows, last_grads[1]]))
     place_grad = flipped(jnp.stack([stream_place, decoded_place]))
-    squares = jnp.sum(gain_own * gain_own)
-    for grad in (entry_grad, leave_grad, expand_grad, shrink_grad, table_grad, place_grad):
+    squares = squares + jnp.sum(gain_own * gain_own)
+    for grad in (entry_grad, leave_grad, expand_grad, shrink_grad, place_grad):
         squares = squares + jnp.sum(grad * grad)
     last_words = to_all(jnp.concatenate([gain_own, squares[None]]))
     gain_grad = last_words[:, :-1].reshape(norm_gains.shape)

time: 731 us -> 701 us (0.959)
  waiting for transfers between devices: 284 us -> 236 us
  other arithmetic: 110 us -> 122 us
  local copies, waits for them, and re-layouts: 52.5 us -> 62.9 us
    ppermute x38, waiting for transfers between devices: 237 us -> 184 us  [swap_bit(): return lax.ppermute(values, 'dp', pairs)]
    all_to_all x2, starting transfers between devices: 16.8 us -> 7.66 us  [answer(): lax.all_to_all(sent.reshape(devices, SLOTS, width), EVERY, 0, 0, tiled=True)]
    reshape x12 -> x0, other arithmetic: 7.9 us -> none  [step(): self.held = held.reshape((-1,) + block)]
    another operation x18 -> x22, other arithmetic: 8.62 us -> 16.4 us  [the longest x18 14 us: settle(): jnp.stack([self.held.reshape(shape), self.got.reshape(shape)], axis=1)]
    unnamed x501 -> x512, local copies, waits for them, and re-layouts: 16.1 us -> 20 us
  transfers between devices with their start and end apart: 68 -> 68, of which waited for: 41 -> 30; matrix products, arithmetic and copies ran while one was open for 26% -> 30% of each run, Pallas kernels for 3% -> 3%
where the time goes in v4:
time: 701 us; the launch traced here: 691 us
  waiting for transfers between devices  236 us (34%)
  other arithmetic  122 us (17%)
  matrix products  106 us (15%)
  starting transfers between devices  80.8 us (12%)
  local copies, waits for them, and re-layouts  62.9 us (9%)
  between operations  31.6 us (5%)
  blocking collectives  26.6 us (4%)
  Pallas kernels  22.7 us (3%)
    ppermute x38, waiting for transfers between devices, swap_bit(): return lax.ppermute(values, 'dp', pairs)  184 us
    ppermute x38, starting transfers between devices, swap_bit(): return lax.ppermute(values, 'dp', pairs)  51.8 us
    dot_general x21, matrix products, product(): return jnp.dot(left, right, preferred_element_type=jnp.float32)  45.5 us
    dot_general x16, matrix products, product_tn(): lax.dot_general(left, right, (((0,), (0,)), ((), ())), preferred_element_...  34.5 us
    all_to_all x1, blocking collectives, to_all(): lax.all_to_all(jnp.broadcast_to(values[None], (size,) + values.shape), ax...  26.6 us
    pallas_call x6, Pallas kernels, kernel_call(): pl.pallas_call(kernel, out_shape=outputs, in_specs=[pl.BlockSpec(memory_s...  22.7 us
    sub x7, other arithmetic, adam_step(): master - rate * (first_new / fix_one / (jnp.sqrt(second_new / fix_two) +...  20.9 us
    unnamed x512, local copies, waits for them, and re-layouts  20 us
  transfers between devices with their start and end apart: 68, of which 30 were waited for; matrix products, arithmetic and copies ran while one was open for 30% of the time, Pallas kernels for 3%

profile of v4, /device:TPU:0, one launch (start us, length us, event | category | flops | bytes accessed | tf_op | source)
XLA Modules:
  0.0 691.5 jit_solution(8116514316614404103)
XLA Ops:
  11.8 4.0 collective-permute-start
  25.1 2.8 all-to-all-start.4
  30.6 4.7 all-to-all-done.4
  39.2 4.4 fusion.93
  45.5 14.0 %collective-permute-done.3 = bf16[2,48,1024]{2,1,0:T(8,128)(2,1)} collective-permute-done((bf16[2,48,1024]{2,1,0:T(8,128)(2,1)S(1)}, bf16[2,48,1024]{2,1,0:T(8,128)(2,1)}, u32[]{:S(2)}, u32[]{:S(2)}) %collective-permute-start.3) | collective-permute-done | bytes 196640 | tf_op jit(solution)/shard_map/ppermute | solution.py:219
  59.5 3.6 all-to-all-start.5
  72.7 18.7 %collective-permute-done.4 = bf16[4,48,768]{2,1,0:T(8,128)(2,1)S(1)} collective-permute-done((bf16[4,48,768]{2,1,0:T(8,128)(2,1)S(1)}, bf16[4,48,768]{2,1,0:T(8,128)(2,1)S(1)}, u32[]{:S(2)}, u32[]{:S(2)}) %collective-permute-start.4) | collective-permute-done | bytes 294944 | tf_op jit(solution)/shard_map/ppermute | solution.py:219
  91.4 6.8 collective-permute-done.5
  103.1 3.2 collective-permute-start.9
  106.9 8.2 %collective-permute-done.9 = bf16[1,48,1536]{2,1,0:T(8,128)(2,1)S(1)} collective-permute-done((bf16[1,48,1536]{2,1,0:T(8,128)(2,1)S(1)}, bf16[1,48,1536]{2,1,0:T(8,128)(2,1)S(1)}, u32[]{:S(2)}, u32[]{:S(2)}) %collective-permute-start.9) | collective-permute-done | bytes 147488 | tf_op jit(solution)/shard_map/ppermute | solution.py:219
  115.1 18.0 %collective-permute-done.8 = bf16[1,48,1792]{2,1,0:T(8,128)(2,1)S(1)} collective-permute-done((bf16[1,48,1792]{2,1,0:T(8,128)(2,1)}, bf16[1,48,1792]{2,1,0:T(8,128)(2,1)S(1)}, u32[]{:S(2)}, u32[]{:S(2)}) %collective-permute-start.8) | collective-permute-done | bytes 172064 | tf_op jit(solution)/shard_map/ppermute | solution.py:219
  141.6 3.6 fusion.80
  150.0 10.4 %collective-permute-done.11 = bf16[2,48,1536]{2,1,0:T(8,128)(2,1)} collective-permute-done((bf16[2,48,1536]{2,1,0:T(8,128)(2,1)}, bf16[2,48,1536]{2,1,0:T(8,128)(2,1)}, u32[]{:S(2)}, u32[]{:S(2)}) %collective-permute-start.11) | collective-permute-done | bytes 294944 | tf_op jit(solution)/shard_map/ppermute | solution.py:219
  167.5 4.5 shard_map.460
  172.0 15.3 %collective-permute-done.14 = bf16[4,48,1536]{2,1,0:T(8,128)(2,1)S(1)} collective-permute-done((bf16[4,48,1536]{2,1,0:T(8,128)(2,1)S(1)}, bf16[4,48,1536]{2,1,0:T(8,128)(2,1)S(1)}, u32[]{:S(2)}, u32[]{:S(2)}) %collective-permute-start.14) | collective-permute-done | bytes 589856 | tf_op jit(solution)/shard_map/ppermute | solution.py:219
  197.3 9.5 %multiply_convert_fusion.1 = (bf16[512,1536]{1,0:T(8,128)(2,1)S(1)}, f32[512,1536]{1,0:T(8,128)}, f32[512,1536]{1,0:T(8,128)}) fusion(bf16[768,1536]{1,0:T(8,128)(2,1)S(1)} %convolution_convert_fusion.5, bf16[256,768]{1,0:T(8,128)(2,1)S(1)} %collective-permute-done.16, bf16[256,768]{1,0:T(8,128)(2,1)S(1)} %multiply_convert_fusion.4), kind=kOutput, calls=%fused_computation.103 | convolution fusion | flops 1260650496 | bytes 11010048 | tf_op jit(solution)/shard_map/dot_general | solution.py:51
  206.8 32.6 %collective-permute-done.18 = bf16[8,48,1536]{2,1,0:T(8,128)(2,1)S(1)} collective-permute-done((bf16[8,48,1536]{2,1,0:T(8,128)(2,1)S(1)}, bf16[8,48,1536]{2,1,0:T(8,128)(2,1)S(1)}, u32[]{:S(2)}, u32[]{:S(2)}) %collective-permute-start.18) | collective-permute-done | bytes 1179680 | tf_op jit(solution)/shard_map/ppermute | solution.py:219
  239.4 3.7 collective-permute-done.17
  285.1 26.6 %all_to_all.116 = bf16[16,32,768]{2,1,0:T(8,128)(2,1)} all-to-all(bf16[16,32,768]{2,1,0:T(8,128)(2,1)S(1)} %broadcast_in_dim.142), channel_id=1, replica_groups=mesh['dp'=16,'tensor'=2] {'dp'}, dimensions={0} | all-to-all | bytes 1572864 | tf_op jit(solution)/shard_map/all_to_all | solution.py:45
  314.3 5.4 fusion.314
  328.4 8.1 %all-to-all-done.7 = f32[32,2,1024]{2,1,0:T(2,128)S(1)} async-done(((f32[32,2,1024]{2,1,0:T(2,128)}), f32[32,2,1024]{2,1,0:T(2,128)S(1)}, u32[]{:S(2)}, u32[]{:S(2)}) %all-to-all-start.7) | async-done | bytes 262176 | tf_op jit(solution)/shard_map/all_to_all | solution.py:45
  336.9 6.5 fusion.277
  348.4 4.4 all-to-all-start.8
  355.2 17.8 %all-to-all-done.8 = bf16[16,32,768]{2,1,0:T(8,128)(2,1)} async-done(((bf16[16,32,768]{2,1,0:T(8,128)(2,1)}), bf16[16,32,768]{2,1,0:T(8,128)(2,1)}, u32[]{:S(2)}, u32[]{:S(2)}) %all-to-all-start.8) | async-done | bytes 786464 | tf_op jit(solution)/shard_map/all_to_all | solution.py:608
  377.7 3.1 add_convert_fusion.3
  391.8 3.2 shard_map.463
  427.5 3.2 shard_map.465
  451.9 7.1 %shard_map.464 = (bf16[512,768]{1,0:T(8,128)(2,1)S(1)}, bf16[512,384]{1,0:T(8,128)(2,1)S(1)}) custom-call(bf16[512,768]{1,0:T(8,128)(2,1)S(1)} %copy-done.3, bf16[512,384]{1,0:T(8,128)(2,1)S(1)} %convolution_convert_fusion.20.refs_1_, bf16[512,384]{1,0:T(8,128)(2,1)S(1)} %convolution_convert_fusion.19.refs_2_, f32[512,1]{1,0:T(8,128)S(1)} %convert_element_type.641.refs_3_), custom_call_target="tpu_custom_call" | custom-call | flops 4026531840 | bytes 3149824 | tf_op jit(solution)/shard_map/pallas_call | solution.py:104
  470.4 3.1 fusion.54
  476.7 3.4 fusion.92
  480.1 4.1 all-to-all-start.9
  502.9 16.0 %collective-permute-done.40 = bf16[4,1,48,2304]{3,2,0,1:T(8,128)(2,1)} collective-permute-done((bf16[4,1,48,2304]{3,2,0,1:T(8,128)(2,1)}, bf16[4,1,48,2304]{3,2,0,1:T(8,128)(2,1)}, u32[]{:S(2)}, u32[]{:S(2)}) %collective-permute-start.40) | collective-permute-done | bytes 884768 | tf_op jit(solution)/shard_map/ppermute | solution.py:219
  520.7 5.1 collective-permute-done.41
  529.4 5.4 all-to-all-done.9
  534.8 11.2 %collective-permute-done.46 = bf16[8,1,48,384]{3,2,0,1:T(8,128)(2,1)} collective-permute-done((bf16[8,1,48,384]{3,2,0,1:T(8,128)(2,1)S(1)}, bf16[8,1,48,384]{3,2,0,1:T(8,128)(2,1)}, u32[]{:S(2)}, u32[]{:S(2)}) %collective-permute-start.46) | collective-permute-done | bytes 294944 | tf_op jit(solution)/shard_map/ppermute | solution.py:219
  568.3 7.1 %fusion.34 = f32[1572,768]{1,0:T(8,128)} fusion(bf16[1024,768]{1,0:T(8,128)(2,1)} %bitcast.116, s32[1024]{0:T(1024)S(1)} %copy-done.198), kind=kOutput, calls=%fused_computation.66 | convolution fusion | flops 2474151936 | bytes 6406144 | tf_op jit(solution)/shard_map/dot_general | solution.py:55
  576.2 11.5 %convolution_add_fusion = f32[1572,768]{1,0:T(8,128)} fusion(f32[1572,768]{1,0:T(8,128)} %fusion.34, bf16[512,768]{1,0:T(8,128)(2,1)} %collective-permute-done.25, bf16[512,768]{1,0:T(8,128)(2,1)} %bitcast.95, pred[]{:T(512)S(6)} %eq.398, f32[1024,1572]{0,1:T(8,128)} %copy-done.37, f32[1024]{0:T(1024)S(1)} %copy-done.200, f32[1024]{0:T(1024)S(1)} %copy-done.202, ...), kind=kOutput, calls=%fused_computation.86 | convolution fusion | flops 2490485760 | bytes 17682432 | tf_op jit(solution)/shard_map/dot_general | solution.py:55
  588.7 3.2 all-to-all-start.10
  591.9 4.4 multiply_reduce_fusion
  596.3 2.9 all-to-all-done.10
  610.9 3.3 collective-permute-done.52
  614.2 9.4 %collective-permute-done.53 = bf16[1,1,48,2304]{3,2,1,0:T(8,128)(2,1)S(1)} collective-permute-done((bf16[1,1,48,2304]{3,2,1,0:T(8,128)(2,1)S(1)}, bf16[1,1,48,2304]{3,2,1,0:T(8,128)(2,1)S(1)}, u32[]{:S(2)}, u32[]{:S(2)}) %collective-permute-start.53) | collective-permute-done | bytes 221216 | tf_op jit(solution)/shard_map/ppermute | solution.py:219
  623.5 5.9 collective-permute-done.54
  636.4 4.0 collective-permute-done.57
  648.6 3.9 all-to-all-start.11
  654.3 5.5 all-to-all-done.11
  661.3 3.1 multiply_subtract_fusion.1
  672.0 9.0 %multiply_subtract_fusion = (f32[1572,768]{1,0:T(8,128)}, f32[1572,768]{1,0:T(8,128)}, f32[1572,768]{1,0:T(8,128)}) fusion(f32[1572,768]{1,0:T(8,128)S(1)} %bitcast.592, f32[]{:T(128)} %bitcast.210, f32[]{:T(128)} %bitcast.209, f32[1572,768]{1,0:T(8,128)S(1)} %bitcast.594, f32[]{:T(128)S(6)} %min.3, f32[1572,768]{1,0:T(8,128)} %param.58, f32[1572,768]{1,0:T(8,128)} %param.57), kind=kLoop, calls=%fused_computation.73 | loop fusion | flops 19316736 | bytes 33804300 | tf_op jit(solution)/shard_map/sub | solution.py:201
  (957 shorter events, 285.4 us)
Async XLA Ops:
  7.2 134.4 %all-gather.3.cloned.1.call-start = ((), (), s32[]{:S(2)}) async-start(), calls=%async_computation.13 | async-start | bytes 5013504 | tf_op jit(solution)/shard_map/all_gather | solution.py:416
  11.8 23.4 %collective-permute-start = (bf16[1,48,768]{2,1,0:T(8,128)(2,1)}, bf16[1,48,768]{2,1,0:T(8,128)(2,1)}, u32[]{:S(2)}, u32[]{:S(2)}) collective-permute-start(bf16[1,48,768]{2,1,0:T(8,128)(2,1)} %get-tuple-element.907), channel_id=1, source_target_pairs={{0,16},{2,18},{4,20},{6,22},{8,24},{10,26},{12,28},{14,30},{16,0},... | collective-permute-start | bytes 221192 | tf_op jit(solution)/shard_map/ppermute | solution.py:219
  17.2 18.0 %collective-permute-start.1 = (bf16[1,48,1024]{2,1,0:T(8,128)(2,1)}, bf16[1,48,1024]{2,1,0:T(8,128)(2,1)S(1)}, u32[]{:S(2)}, u32[]{:S(2)}) collective-permute-start(bf16[1,48,1024]{2,1,0:T(8,128)(2,1)} %get-tuple-element.905), channel_id=1, source_target_pairs={{0,8},{2,10},{4,12},{6,14},{8,0},{10,2},{12,4},{14,6},{16,24},{18,... | collective-permute-start | bytes 294920 | tf_op jit(solution)/shard_map/ppermute | solution.py:219
  25.1 10.2 %all-to-all-start.4 = ((s32[32,1,129]{2,1,0:T(1,128)}), s32[32,1,129]{2,1,0:T(1,128)S(1)}, u32[]{:S(2)}, u32[]{:S(2)}) async-start(s32[32,1,129]{2,1,0:T(1,128)} %all_to_all.73), calls=%async_computation.4 | async-start | bytes 65536 | tf_op jit(solution)/shard_map/all_to_all | solution.py:456
  38.5 20.9 %collective-permute-start.3 = (bf16[2,48,1024]{2,1,0:T(8,128)(2,1)S(1)}, bf16[2,48,1024]{2,1,0:T(8,128)(2,1)}, u32[]{:S(2)}, u32[]{:S(2)}) collective-permute-start(bf16[2,48,1024]{2,1,0:T(8,128)(2,1)S(1)} %get-tuple-element.899), channel_id=1, source_target_pairs={{0,16},{2,18},{4,20},{6,22},{8,24},{10,26},{12,28},{14,30},{16,0},... | collective-permute-start | bytes 589832 | tf_op jit(solution)/shard_map/ppermute | solution.py:219
  59.5 73.6 %all-to-all-start.5 = ((bf16[32,32,768]{2,1,0:T(8,128)(2,1)}), bf16[32,32,768]{2,1,0:T(8,128)(2,1)}, u32[]{:S(2)}, u32[]{:S(2)}) async-start(bf16[32,32,768]{2,1,0:T(8,128)(2,1)} %bitcast.661), calls=%async_computation.5 | async-start | bytes 3145728 | tf_op jit(solution)/shard_map/all_to_all | solution.py:470
  63.0 206.1 %all-gather.5.cloned.1.call-start = ((), (), s32[]{:S(2)}) async-start(), calls=%async_computation.14 | async-start | bytes 5013504 | tf_op jit(solution)/shard_map/all_gather | solution.py:416
  68.7 29.5 %collective-permute-start.5 = (bf16[4,48,1024]{2,1,0:T(8,128)(2,1)S(1)}, bf16[4,48,1024]{2,1,0:T(8,128)(2,1)S(1)}, u32[]{:S(2)}, u32[]{:S(2)}) collective-permute-start(bf16[4,48,1024]{2,1,0:T(8,128)(2,1)S(1)} %bitcast.665), channel_id=1, source_target_pairs={{0,2},{2,0},{4,6},{6,4},{8,10},{10,8},{12,14},{14,12},{16,18},{18,... | collective-permute-start | bytes 1179656 | tf_op jit(solution)/shard_map/ppermute | solution.py:219
  70.4 21.0 %collective-permute-start.4 = (bf16[4,48,768]{2,1,0:T(8,128)(2,1)S(1)}, bf16[4,48,768]{2,1,0:T(8,128)(2,1)S(1)}, u32[]{:S(2)}, u32[]{:S(2)}) collective-permute-start(bf16[4,48,768]{2,1,0:T(8,128)(2,1)S(1)} %bitcast.679), channel_id=1, source_target_pairs={{0,4},{2,6},{4,0},{6,2},{8,12},{10,14},{12,8},{14,10},{16,20},{18,... | collective-permute-start | bytes 884744 | tf_op jit(solution)/shard_map/ppermute | solution.py:219
  98.4 34.6 %collective-permute-start.7 = (bf16[8,48,1024]{2,1,0:T(8,128)(2,1)S(1)}, bf16[8,48,1024]{2,1,0:T(8,128)(2,1)}, u32[]{:S(2)}, u32[]{:S(2)}) collective-permute-start(bf16[8,48,1024]{2,1,0:T(8,128)(2,1)S(1)} %bitcast.689), channel_id=1, source_target_pairs={{0,4},{2,6},{4,0},{6,2},{8,12},{10,14},{12,8},{14,10},{16,20},{18,... | collective-permute-start | bytes 2359304 | tf_op jit(solution)/shard_map/ppermute | solution.py:219
  100.1 32.9 %collective-permute-start.6 = (bf16[8,48,768]{2,1,0:T(8,128)(2,1)S(1)}, bf16[8,48,768]{2,1,0:T(8,128)(2,1)S(1)}, u32[]{:S(2)}, u32[]{:S(2)}) collective-permute-start(bf16[8,48,768]{2,1,0:T(8,128)(2,1)S(1)} %bitcast.644), channel_id=1, source_target_pairs={{0,2},{2,0},{4,6},{6,4},{8,10},{10,8},{12,14},{14,12},{16,18},{18,... | collective-permute-start | bytes 1769480 | tf_op jit(solution)/shard_map/ppermute | solution.py:219
  102.9 30.2 %collective-permute-start.8 = (bf16[1,48,1792]{2,1,0:T(8,128)(2,1)}, bf16[1,48,1792]{2,1,0:T(8,128)(2,1)S(1)}, u32[]{:S(2)}, u32[]{:S(2)}) collective-permute-start(bf16[1,48,1792]{2,1,0:T(8,128)(2,1)} %bitcast.34), channel_id=1, source_target_pairs={{0,16},{2,18},{4,20},{6,22},{8,24},{10,26},{12,28},{14,30},{16,0},... | collective-permute-start | bytes 516104 | tf_op jit(solution)/shard_map/ppermute | solution.py:219
  103.1 12.0 %collective-permute-start.9 = (bf16[1,48,1536]{2,1,0:T(8,128)(2,1)S(1)}, bf16[1,48,1536]{2,1,0:T(8,128)(2,1)S(1)}, u32[]{:S(2)}, u32[]{:S(2)}) collective-permute-start(bf16[1,48,1536]{2,1,0:T(8,128)(2,1)S(1)} %maximum_bitcast_fusion.3), channel_id=1, source_target_pairs={{0,8},{2,10},{4,12},{6,14},{8,0},{10,2},{12,4},{14,6},{16,24},{18,... | collective-permute-start | bytes 442376 | tf_op jit(solution)/shard_map/ppermute | solution.py:219
  137.9 22.5 %collective-permute-start.10 = (bf16[2,48,1792]{2,1,0:T(8,128)(2,1)}, bf16[2,48,1792]{2,1,0:T(8,128)(2,1)}, u32[]{:S(2)}, u32[]{:S(2)}) collective-permute-start(bf16[2,48,1792]{2,1,0:T(8,128)(2,1)} %get-tuple-element.884), channel_id=1, source_target_pairs={{0,8},{2,10},{4,12},{6,14},{8,0},{10,2},{12,4},{14,6},{16,24},{18,... | collective-permute-start | bytes 1032200 | tf_op jit(solution)/shard_map/ppermute | solution.py:219
  138.7 21.7 %collective-permute-start.11 = (bf16[2,48,1536]{2,1,0:T(8,128)(2,1)}, bf16[2,48,1536]{2,1,0:T(8,128)(2,1)}, u32[]{:S(2)}, u32[]{:S(2)}) collective-permute-start(bf16[2,48,1536]{2,1,0:T(8,128)(2,1)} %get-tuple-element.896), channel_id=1, source_target_pairs={{0,16},{2,18},{4,20},{6,22},{8,24},{10,26},{12,28},{14,30},{16,0},... | collective-permute-start | bytes 884744 | tf_op jit(solution)/shard_map/ppermute | solution.py:219
  161.5 25.8 %collective-permute-start.13 = (bf16[4,48,1792]{2,1,0:T(8,128)(2,1)S(1)}, bf16[4,48,1792]{2,1,0:T(8,128)(2,1)S(1)}, u32[]{:S(2)}, u32[]{:S(2)}) collective-permute-start(bf16[4,48,1792]{2,1,0:T(8,128)(2,1)S(1)} %bitcast.636), channel_id=1, source_target_pairs={{0,4},{2,6},{4,0},{6,2},{8,12},{10,14},{12,8},{14,10},{16,20},{18,... | collective-permute-start | bytes 2064392 | tf_op jit(solution)/shard_map/ppermute | solution.py:219
  164.2 23.1 %collective-permute-start.14 = (bf16[4,48,1536]{2,1,0:T(8,128)(2,1)S(1)}, bf16[4,48,1536]{2,1,0:T(8,128)(2,1)S(1)}, u32[]{:S(2)}, u32[]{:S(2)}) collective-permute-start(bf16[4,48,1536]{2,1,0:T(8,128)(2,1)S(1)} %bitcast.638), channel_id=1, source_target_pairs={{0,2},{2,0},{4,6},{6,4},{8,10},{10,8},{12,14},{14,12},{16,18},{18,... | collective-permute-start | bytes 1769480 | tf_op jit(solution)/shard_map/ppermute | solution.py:219
  193.9 49.2 %collective-permute-start.17 = (bf16[8,48,1792]{2,1,0:T(8,128)(2,1)S(1)}, bf16[8,48,1792]{2,1,0:T(8,128)(2,1)S(1)}, u32[]{:S(2)}, u32[]{:S(2)}) collective-permute-start(bf16[8,48,1792]{2,1,0:T(8,128)(2,1)S(1)} %bitcast.615), channel_id=1, source_target_pairs={{0,2},{2,0},{4,6},{6,4},{8,10},{10,8},{12,14},{14,12},{16,18},{18,... | collective-permute-start | bytes 4128776 | tf_op jit(solution)/shard_map/ppermute | solution.py:219
  195.6 43.9 %collective-permute-start.18 = (bf16[8,48,1536]{2,1,0:T(8,128)(2,1)S(1)}, bf16[8,48,1536]{2,1,0:T(8,128)(2,1)S(1)}, u32[]{:S(2)}, u32[]{:S(2)}) collective-permute-start(bf16[8,48,1536]{2,1,0:T(8,128)(2,1)S(1)} %bitcast.670), channel_id=1, source_target_pairs={{0,4},{2,6},{4,0},{6,2},{8,12},{10,14},{12,8},{14,10},{16,20},{18,... | collective-permute-start | bytes 3538952 | tf_op jit(solution)/shard_map/ppermute | solution.py:219
  323.3 13.2 %all-to-all-start.7 = ((f32[32,2,1024]{2,1,0:T(2,128)}), f32[32,2,1024]{2,1,0:T(2,128)S(1)}, u32[]{:S(2)}, u32[]{:S(2)}) async-start(f32[32,2,1024]{2,1,0:T(2,128)} %broadcast_in_dim.144), calls=%async_computation.7 | async-start | bytes 524288 | tf_op jit(solution)/shard_map/all_to_all | solution.py:45
  348.4 24.5 %all-to-all-start.8 = ((bf16[16,32,768]{2,1,0:T(8,128)(2,1)}), bf16[16,32,768]{2,1,0:T(8,128)(2,1)}, u32[]{:S(2)}, u32[]{:S(2)}) async-start(bf16[16,32,768]{2,1,0:T(8,128)(2,1)} %bitcast.635), calls=%async_computation.8 | async-start | bytes 1572864 | tf_op jit(solution)/shard_map/all_to_all | solution.py:608
  352.9 213.6 %reduce-scatter.2.cloned.1.call-start = ((), (), s32[]{:S(2)}) async-start(), calls=%async_computation.15 | async-start | bytes 5013504 | tf_op jit(solution)/shard_map/reduce_scatter | solution.py:622
  405.2 54.4 %collective-permute-start.33 = (bf16[8,1,48,768]{3,2,0,1:T(8,128)(2,1)}, bf16[8,1,48,768]{3,2,0,1:T(8,128)(2,1)}, u32[]{:S(2)}, u32[]{:S(2)}) collective-permute-start(bf16[8,1,48,768]{3,2,0,1:T(8,128)(2,1)} %slice_bitcast_fusion.16), channel_id=1, source_target_pairs={{0,2},{2,0},{4,6},{6,4},{8,10},{10,8},{12,14},{14,12},{16,18},{18,... | collective-permute-start | bytes 1769480 | tf_op jit(solution)/shard_map/ppermute | solution.py:219
  409.7 51.2 %collective-permute-start.34 = (bf16[4,2,48,768]{3,2,1,0:T(8,128)(2,1)}, bf16[4,2,48,768]{3,2,1,0:T(8,128)(2,1)}, u32[]{:S(2)}, u32[]{:S(2)}) collective-permute-start(bf16[4,2,48,768]{3,2,1,0:T(8,128)(2,1)} %slice_bitcast_fusion.15), channel_id=1, source_target_pairs={{0,4},{2,6},{4,0},{6,2},{8,12},{10,14},{12,8},{14,10},{16,20},{18,... | collective-permute-start | bytes 1769480 | tf_op jit(solution)/shard_map/ppermute | solution.py:219
  417.9 25.7 %collective-permute-start.31 = (f32[256,768]{1,0:T(8,128)}, f32[256,768]{1,0:T(8,128)}, u32[]{:S(2)}, u32[]{:S(2)}) collective-permute-start(f32[256,768]{1,0:T(8,128)} %slice.519), channel_id=1, source_target_pairs={{0,1},{1,0},{2,3},{3,2},{4,5},{5,4},{6,7},{7,6},{8,9},{9,8},{10,11... | collective-permute-start | bytes 2359304 | tf_op jit(solution)/shard_map/ppermute | solution.py:31
  420.7 40.2 %collective-permute-start.35 = (bf16[8,1,48,1536]{3,2,0,1:T(8,128)(2,1)}, bf16[8,1,48,1536]{3,2,0,1:T(8,128)(2,1)}, u32[]{:S(2)}, u32[]{:S(2)}) collective-permute-start(bf16[8,1,48,1536]{3,2,0,1:T(8,128)(2,1)} %slice_bitcast_fusion.4), channel_id=1, source_target_pairs={{0,2},{2,0},{4,6},{6,4},{8,10},{10,8},{12,14},{14,12},{16,18},{18,... | collective-permute-start | bytes 3538952 | tf_op jit(solution)/shard_map/ppermute | solution.py:219
  424.9 36.1 %collective-permute-start.36 = (bf16[4,2,48,1536]{3,2,1,0:T(8,128)(2,1)}, bf16[4,2,48,1536]{3,2,1,0:T(8,128)(2,1)}, u32[]{:S(2)}, u32[]{:S(2)}) collective-permute-start(bf16[4,2,48,1536]{3,2,1,0:T(8,128)(2,1)} %slice_bitcast_fusion.3), channel_id=1, source_target_pairs={{0,4},{2,6},{4,0},{6,2},{8,12},{10,14},{12,8},{14,10},{16,20},{18,... | collective-permute-start | bytes 3538952 | tf_op jit(solution)/shard_map/ppermute | solution.py:219
  450.6 51.0 %collective-permute-start.42 = (bf16[8,1,48,768]{3,2,0,1:T(8,128)(2,1)}, bf16[8,1,48,768]{3,2,0,1:T(8,128)(2,1)}, u32[]{:S(2)}, u32[]{:S(2)}) collective-permute-start(bf16[8,1,48,768]{3,2,0,1:T(8,128)(2,1)} %slice_bitcast_fusion.12), channel_id=1, source_target_pairs={{0,2},{2,0},{4,6},{6,4},{8,10},{10,8},{12,14},{14,12},{16,18},{18,... | collective-permute-start | bytes 1769480 | tf_op jit(solution)/shard_map/ppermute | solution.py:219
  459.6 75.2 %collective-permute-start.43 = (bf16[4,2,48,768]{3,2,1,0:T(8,128)(2,1)}, bf16[4,2,48,768]{3,2,1,0:T(8,128)(2,1)}, u32[]{:S(2)}, u32[]{:S(2)}) collective-permute-start(bf16[4,2,48,768]{3,2,1,0:T(8,128)(2,1)} %slice_bitcast_fusion.11), channel_id=1, source_target_pairs={{0,4},{2,6},{4,0},{6,2},{8,12},{10,14},{12,8},{14,10},{16,20},{18,... | collective-permute-start | bytes 1769480 | tf_op jit(solution)/shard_map/ppermute | solution.py:219
  461.8 11.7 %collective-permute-start.37 = (f32[256,768]{1,0:T(8,128)S(1)}, f32[256,768]{1,0:T(8,128)S(1)}, u32[]{:S(2)}, u32[]{:S(2)}) collective-permute-start(f32[256,768]{1,0:T(8,128)S(1)} %slice.652), channel_id=1, source_target_pairs={{0,1},{1,0},{2,3},{3,2},{4,5},{5,4},{6,7},{7,6},{8,9},{9,8},{10,11... | collective-permute-start | bytes 2359304 | tf_op jit(solution)/shard_map/ppermute | solution.py:31
  466.9 51.9 %collective-permute-start.40 = (bf16[4,1,48,2304]{3,2,0,1:T(8,128)(2,1)}, bf16[4,1,48,2304]{3,2,0,1:T(8,128)(2,1)}, u32[]{:S(2)}, u32[]{:S(2)}) collective-permute-start(bf16[4,1,48,2304]{3,2,0,1:T(8,128)(2,1)} %fusion.121), channel_id=1, source_target_pairs={{0,4},{2,6},{4,0},{6,2},{8,12},{10,14},{12,8},{14,10},{16,20},{18,... | collective-permute-start | bytes 2654216 | tf_op jit(solution)/shard_map/ppermute | solution.py:219
  480.1 54.7 %all-to-all-start.9 = ((bf16[32,32,768]{2,1,0:T(8,128)(2,1)}), bf16[32,32,768]{2,1,0:T(8,128)(2,1)}, u32[]{:S(2)}, u32[]{:S(2)}) async-start(bf16[32,32,768]{2,1,0:T(8,128)(2,1)} %bitcast.662), calls=%async_computation.9 | async-start | bytes 3145728 | tf_op jit(solution)/shard_map/all_to_all | solution.py:470
  487.6 38.3 %collective-permute-start.41 = (bf16[4,1,48,2304]{3,2,0,1:T(8,128)(2,1)}, bf16[4,1,48,2304]{3,2,0,1:T(8,128)(2,1)}, u32[]{:S(2)}, u32[]{:S(2)}) collective-permute-start(bf16[4,1,48,2304]{3,2,0,1:T(8,128)(2,1)} %fusion.122), channel_id=1, source_target_pairs={{0,2},{2,0},{4,6},{6,4},{8,10},{10,8},{12,14},{14,12},{16,18},{18,... | collective-permute-start | bytes 2654216 | tf_op jit(solution)/shard_map/ppermute | solution.py:219
  497.1 49.0 %collective-permute-start.45 = (bf16[4,2,48,768]{3,2,1,0:T(8,128)(2,1)}, bf16[4,2,48,768]{3,2,1,0:T(8,128)(2,1)}, u32[]{:S(2)}, u32[]{:S(2)}) collective-permute-start(bf16[4,2,48,768]{3,2,1,0:T(8,128)(2,1)} %slice_bitcast_fusion.10), channel_id=1, source_target_pairs={{0,4},{2,6},{4,0},{6,2},{8,12},{10,14},{12,8},{14,10},{16,20},{18,... | collective-permute-start | bytes 1769480 | tf_op jit(solution)/shard_map/ppermute | solution.py:219
  501.5 44.6 %collective-permute-start.44 = (bf16[8,1,48,640]{3,2,0,1:T(8,128)(2,1)}, bf16[8,1,48,640]{3,2,0,1:T(8,128)(2,1)S(1)}, u32[]{:S(2)}, u32[]{:S(2)}) collective-permute-start(bf16[8,1,48,640]{3,2,0,1:T(8,128)(2,1)} %slice_bitcast_fusion.18), channel_id=1, source_target_pairs={{0,2},{2,0},{4,6},{6,4},{8,10},{10,8},{12,14},{14,12},{16,18},{18,... | collective-permute-start | bytes 1474568 | tf_op jit(solution)/shard_map/ppermute | solution.py:219
  518.9 27.2 %collective-permute-start.46 = (bf16[8,1,48,384]{3,2,0,1:T(8,128)(2,1)S(1)}, bf16[8,1,48,384]{3,2,0,1:T(8,128)(2,1)}, u32[]{:S(2)}, u32[]{:S(2)}) collective-permute-start(bf16[8,1,48,384]{3,2,0,1:T(8,128)(2,1)S(1)} %slice_bitcast_fusion.26), channel_id=1, source_target_pairs={{0,2},{2,0},{4,6},{6,4},{8,10},{10,8},{12,14},{14,12},{16,18},{18,... | collective-permute-start | bytes 884744 | tf_op jit(solution)/shard_map/ppermute | solution.py:219
  525.9 20.2 %collective-permute-start.47 = (bf16[4,2,48,256]{3,2,1,0:T(8,128)(2,1)}, bf16[4,2,48,256]{3,2,1,0:T(8,128)(2,1)}, u32[]{:S(2)}, u32[]{:S(2)}) collective-permute-start(bf16[4,2,48,256]{3,2,1,0:T(8,128)(2,1)} %slice_bitcast_fusion.28), channel_id=1, source_target_pairs={{0,4},{2,6},{4,0},{6,2},{8,12},{10,14},{12,8},{14,10},{16,20},{18,... | collective-permute-start | bytes 589832 | tf_op jit(solution)/shard_map/ppermute | solution.py:219
  548.7 51.3 %collective-permute-start.48 = (bf16[2,1,48,2304]{3,2,0,1:T(8,128)(2,1)}, bf16[2,1,48,2304]{3,2,0,1:T(8,128)(2,1)}, u32[]{:S(2)}, u32[]{:S(2)}) collective-permute-start(bf16[2,1,48,2304]{3,2,0,1:T(8,128)(2,1)} %fusion.164), channel_id=1, source_target_pairs={{0,8},{2,10},{4,12},{6,14},{8,0},{10,2},{12,4},{14,6},{16,24},{18,... | collective-permute-start | bytes 1327112 | tf_op jit(solution)/shard_map/ppermute | solution.py:219
  552.4 47.5 %collective-permute-start.49 = (bf16[1,2,48,2304]{3,2,1,0:T(8,128)(2,1)}, bf16[1,2,48,2304]{3,2,1,0:T(8,128)(2,1)}, u32[]{:S(2)}, u32[]{:S(2)}) collective-permute-start(bf16[1,2,48,2304]{3,2,1,0:T(8,128)(2,1)} %fusion.163), channel_id=1, source_target_pairs={{0,16},{2,18},{4,20},{6,22},{8,24},{10,26},{12,28},{14,30},{16,0},... | collective-permute-start | bytes 1327112 | tf_op jit(solution)/shard_map/ppermute | solution.py:219
  558.4 41.6 %collective-permute-start.50 = (bf16[4,1,48,1792]{3,2,0,1:T(8,128)(2,1)}, bf16[4,1,48,1792]{3,2,0,1:T(8,128)(2,1)}, u32[]{:S(2)}, u32[]{:S(2)}) collective-permute-start(bf16[4,1,48,1792]{3,2,0,1:T(8,128)(2,1)} %fusion.134), channel_id=1, source_target_pairs={{0,4},{2,6},{4,0},{6,2},{8,12},{10,14},{12,8},{14,10},{16,20},{18,... | collective-permute-start | bytes 2064392 | tf_op jit(solution)/shard_map/ppermute | solution.py:219
  565.9 34.1 %collective-permute-start.51 = (bf16[4,1,48,1792]{3,2,0,1:T(8,128)(2,1)}, bf16[4,1,48,1792]{3,2,0,1:T(8,128)(2,1)}, u32[]{:S(2)}, u32[]{:S(2)}) collective-permute-start(bf16[4,1,48,1792]{3,2,0,1:T(8,128)(2,1)} %fusion.135), channel_id=1, source_target_pairs={{0,2},{2,0},{4,6},{6,4},{8,10},{10,8},{12,14},{14,12},{16,18},{18,... | collective-permute-start | bytes 2064392 | tf_op jit(solution)/shard_map/ppermute | solution.py:219
  588.7 10.5 %all-to-all-start.10 = ((f32[32,1,168]{2,1,0:T(1,128)}), f32[32,1,168]{2,1,0:T(1,128)}, u32[]{:S(2)}, u32[]{:S(2)}) async-start(f32[32,1,168]{2,1,0:T(1,128)} %all_to_all.91), calls=%async_computation.11 | async-start | bytes 65536 | tf_op jit(solution)/shard_map/all_to_all | solution.py:725
  601.3 12.9 %collective-permute-start.52 = (bf16[1,1,48,2304]{3,2,1,0:T(8,128)(2,1)S(1)}, bf16[1,1,48,2304]{3,2,1,0:T(8,128)(2,1)S(1)}, u32[]{:S(2)}, u32[]{:S(2)}) collective-permute-start(bf16[1,1,48,2304]{3,2,1,0:T(8,128)(2,1)S(1)} %fusion.188), channel_id=1, source_target_pairs={{0,16},{2,18},{4,20},{6,22},{8,24},{10,26},{12,28},{14,30},{16,0},... | collective-permute-start | bytes 663560 | tf_op jit(solution)/shard_map/ppermute | solution.py:219
  603.1 20.4 %collective-permute-start.53 = (bf16[1,1,48,2304]{3,2,1,0:T(8,128)(2,1)S(1)}, bf16[1,1,48,2304]{3,2,1,0:T(8,128)(2,1)S(1)}, u32[]{:S(2)}, u32[]{:S(2)}) collective-permute-start(bf16[1,1,48,2304]{3,2,1,0:T(8,128)(2,1)S(1)} %fusion.189), channel_id=1, source_target_pairs={{0,8},{2,10},{4,12},{6,14},{8,0},{10,2},{12,4},{14,6},{16,24},{18,... | collective-permute-start | bytes 663560 | tf_op jit(solution)/shard_map/ppermute | solution.py:219
  605.2 24.3 %collective-permute-start.54 = (bf16[2,1,48,1792]{3,2,0,1:T(8,128)(2,1)S(1)}, bf16[2,1,48,1792]{3,2,0,1:T(8,128)(2,1)S(1)}, u32[]{:S(2)}, u32[]{:S(2)}) collective-permute-start(bf16[2,1,48,1792]{3,2,0,1:T(8,128)(2,1)S(1)} %fusion.179), channel_id=1, source_target_pairs={{0,8},{2,10},{4,12},{6,14},{8,0},{10,2},{12,4},{14,6},{16,24},{18,... | collective-permute-start | bytes 1032200 | tf_op jit(solution)/shard_map/ppermute | solution.py:219
  607.8 21.6 %collective-permute-start.55 = (bf16[1,2,48,1792]{3,2,1,0:T(8,128)(2,1)S(1)}, bf16[1,2,48,1792]{3,2,1,0:T(8,128)(2,1)S(1)}, u32[]{:S(2)}, u32[]{:S(2)}) collective-permute-start(bf16[1,2,48,1792]{3,2,1,0:T(8,128)(2,1)S(1)} %fusion.178), channel_id=1, source_target_pairs={{0,16},{2,18},{4,20},{6,22},{8,24},{10,26},{12,28},{14,30},{16,0},... | collective-permute-start | bytes 1032200 | tf_op jit(solution)/shard_map/ppermute | solution.py:219
  631.2 10.2 %collective-permute-start.56 = (bf16[1,1,48,1792]{3,2,1,0:T(8,128)(2,1)}, bf16[1,1,48,1792]{3,2,1,0:T(8,128)(2,1)}, u32[]{:S(2)}, u32[]{:S(2)}) collective-permute-start(bf16[1,1,48,1792]{3,2,1,0:T(8,128)(2,1)} %fusion.198), channel_id=1, source_target_pairs={{0,8},{2,10},{4,12},{6,14},{8,0},{10,2},{12,4},{14,6},{16,24},{18,... | collective-permute-start | bytes 516104 | tf_op jit(solution)/shard_map/ppermute | solution.py:219
  648.6 11.2 %all-to-all-start.11 = ((f32[32,1,169]{2,1,0:T(1,128)}), f32[32,1,169]{2,1,0:T(1,128)S(1)}, u32[]{:S(2)}, u32[]{:S(2)}) async-start(f32[32,1,169]{2,1,0:T(1,128)} %broadcast_in_dim.274), calls=%async_computation.12 | async-start | bytes 65536 | tf_op jit(solution)/shard_map/all_to_all | solution.py:45
  (271 other events, 2054.3 us)
Sparse Core Ops, SparseCore 0:
  11.3 116.5 all-gather.2
  131.2 112.3 all-gather.4
  388.2 161.7 reduce-scatter.1

commit v5 on v4

--- a/solution.py
+++ b/solution.py
@@ -714,16 +714,6 @@
     ]
     advance(early)
     advance(late)
-    gain_partial = jnp.concatenate(
-        [
-            reordered_exact(jnp.stack([gain_zero, gain_one, gain_two, gain_three, gain_four])),
-            jnp.stack([gain_five, gain_six]),
-        ]
-    )
-    gain_partial, got = tie(gain_partial, got)
-    gain_own = jnp.sum(
-        lax.all_to_all(gain_partial.reshape(devices, -1), EVERY, 0, 0, tiled=True), axis=0
-    )
     table_grad = grad_table + placed(asked_first, got)
     table_grad = lax.while_loop(
         lambda state: state[0] < rounds_all,
@@ -733,11 +723,21 @@
         ),
         (jnp.int32(1), table_grad),
     )[1]
+    table_grad = meet(table_grad, early + late)
+    advance(early)
+    advance(late)
+    gain_partial = jnp.concatenate(
+        [
+            reordered_exact(jnp.stack([gain_zero, gain_one, gain_two, gain_three, gain_four])),
+            jnp.stack([gain_five, gain_six]),
+        ]
+    )
+    gain_partial, table_grad = tie(gain_partial, table_grad)
+    gain_own = jnp.sum(
+        lax.all_to_all(gain_partial.reshape(devices, -1), EVERY, 0, 0, tiled=True), axis=0
+    )
     squares = jnp.sum(table_grad * table_grad)
     squares, gain_own = tie(squares, gain_own)
-    squares = meet(squares, early + late)
-    advance(early)
-    advance(late)
     squares = meet(squares, early + late)
     advance(late)
     early_rows = [scatter.rows() for scatter in early]

time: 701 us -> 694 us (0.990)
  waiting for transfers between devices: 236 us -> 223 us
    ppermute x38, waiting for transfers between devices: 184 us -> 175 us  [swap_bit(): return lax.ppermute(values, 'dp', pairs)]
    dot_general x21, matrix products: 45.5 us -> 54.2 us  [product(): return jnp.dot(left, right, preferred_element_type=jnp.float32)]
    unnamed x512 -> x540, local copies, waits for them, and re-layouts: 20 us -> 21 us
  transfers between devices with their start and end apart: 68 -> 68, of which waited for: 30 -> 29; matrix products, arithmetic and copies ran while one was open for 30% -> 30% of each run, Pallas kernels for 3% -> 3%
where the time goes in v5:
time: 694 us; the launch traced here: 685 us
  waiting for transfers between devices  223 us (32%)
  other arithmetic  122 us (18%)
  matrix products  109 us (16%)
  starting transfers between devices  80.9 us (12%)
  local copies, waits for them, and re-layouts  66.7 us (10%)
  between operations  32.3 us (5%)
  blocking collectives  26.5 us (4%)
  Pallas kernels  22.7 us (3%)
    ppermute x38, waiting for transfers between devices, swap_bit(): return lax.ppermute(values, 'dp', pairs)  175 us
    dot_general x21, matrix products, product(): return jnp.dot(left, right, preferred_element_type=jnp.float32)  54.2 us
    ppermute x38, starting transfers between devices, swap_bit(): return lax.ppermute(values, 'dp', pairs)  52.4 us
    dot_general x16, matrix products, product_tn(): lax.dot_general(left, right, (((0,), (0,)), ((), ())), preferred_element_...  28.1 us
    all_to_all x1, blocking collectives, to_all(): lax.all_to_all(jnp.broadcast_to(values[None], (size,) + values.shape), ax...  26.5 us
    pallas_call x6, Pallas kernels, kernel_call(): pl.pallas_call(kernel, out_shape=outputs, in_specs=[pl.BlockSpec(memory_s...  22.7 us
    unnamed x540, local copies, waits for them, and re-layouts  21 us
    sub x7, other arithmetic, adam_step(): master - rate * (first_new / fix_one / (jnp.sqrt(second_new / fix_two) +...  20.5 us
  transfers between devices with their start and end apart: 68, of which 29 were waited for; matrix products, arithmetic and copies ran while one was open for 30% of the time, Pallas kernels for 3%

profile of v5, /device:TPU:0, one launch (start us, length us, event | category | flops | bytes accessed | tf_op | source)
XLA Modules:
  0.0 684.8 jit_solution(10489112157826373083)
XLA Ops:
  11.8 4.0 collective-permute-start
  25.1 2.8 all-to-all-start.4
  27.9 2.6 convert_element_type.599
  30.6 4.7 all-to-all-done.4
  39.2 4.4 fusion.93
  45.5 14.0 %collective-permute-done.3 = bf16[2,48,1024]{2,1,0:T(8,128)(2,1)} collective-permute-done((bf16[2,48,1024]{2,1,0:T(8,128)(2,1)S(1)}, bf16[2,48,1024]{2,1,0:T(8,128)(2,1)}, u32[]{:S(2)}, u32[]{:S(2)}) %collective-permute-start.3) | collective-permute-done | bytes 196640 | tf_op jit(solution)/shard_map/ppermute | solution.py:219
  59.5 3.5 all-to-all-start.5
  72.7 18.7 %collective-permute-done.4 = bf16[4,48,768]{2,1,0:T(8,128)(2,1)S(1)} collective-permute-done((bf16[4,48,768]{2,1,0:T(8,128)(2,1)S(1)}, bf16[4,48,768]{2,1,0:T(8,128)(2,1)S(1)}, u32[]{:S(2)}, u32[]{:S(2)}) %collective-permute-start.4) | collective-permute-done | bytes 294944 | tf_op jit(solution)/shard_map/ppermute | solution.py:219
  91.4 6.8 collective-permute-done.5
  103.1 3.2 collective-permute-start.9
  106.9 8.1 %collective-permute-done.9 = bf16[1,48,1536]{2,1,0:T(8,128)(2,1)S(1)} collective-permute-done((bf16[1,48,1536]{2,1,0:T(8,128)(2,1)S(1)}, bf16[1,48,1536]{2,1,0:T(8,128)(2,1)S(1)}, u32[]{:S(2)}, u32[]{:S(2)}) %collective-permute-start.9) | collective-permute-done | bytes 147488 | tf_op jit(solution)/shard_map/ppermute | solution.py:219
  115.0 18.0 %collective-permute-done.8 = bf16[1,48,1792]{2,1,0:T(8,128)(2,1)S(1)} collective-permute-done((bf16[1,48,1792]{2,1,0:T(8,128)(2,1)}, bf16[1,48,1792]{2,1,0:T(8,128)(2,1)S(1)}, u32[]{:S(2)}, u32[]{:S(2)}) %collective-permute-start.8) | collective-permute-done | bytes 172064 | tf_op jit(solution)/shard_map/ppermute | solution.py:219
  141.6 3.6 fusion.80
  149.8 10.6 %collective-permute-done.11 = bf16[2,48,1536]{2,1,0:T(8,128)(2,1)} collective-permute-done((bf16[2,48,1536]{2,1,0:T(8,128)(2,1)}, bf16[2,48,1536]{2,1,0:T(8,128)(2,1)}, u32[]{:S(2)}, u32[]{:S(2)}) %collective-permute-start.11) | collective-permute-done | bytes 294944 | tf_op jit(solution)/shard_map/ppermute | solution.py:219
  167.5 4.5 shard_map.460
  172.0 15.3 %collective-permute-done.14 = bf16[4,48,1536]{2,1,0:T(8,128)(2,1)S(1)} collective-permute-done((bf16[4,48,1536]{2,1,0:T(8,128)(2,1)S(1)}, bf16[4,48,1536]{2,1,0:T(8,128)(2,1)S(1)}, u32[]{:S(2)}, u32[]{:S(2)}) %collective-permute-start.14) | collective-permute-done | bytes 589856 | tf_op jit(solution)/shard_map/ppermute | solution.py:219
  197.2 19.2 %multiply_convert_fusion.1 = (bf16[512,1536]{1,0:T(8,128)(2,1)S(1)}, f32[512,1536]{1,0:T(8,128)}, f32[512,1536]{1,0:T(8,128)}) fusion(bf16[768,1536]{1,0:T(8,128)(2,1)S(1)} %convolution_convert_fusion.5, bf16[256,768]{1,0:T(8,128)(2,1)S(1)} %collective-permute-done.16, bf16[256,768]{1,0:T(8,128)(2,1)S(1)} %multiply_convert_fusion.4), kind=kOutput, calls=%fused_computation.103 | convolution fusion | flops 1260650496 | bytes 11010048 | tf_op jit(solution)/shard_map/dot_general | solution.py:51
  216.4 23.0 %collective-permute-done.18 = bf16[8,48,1536]{2,1,0:T(8,128)(2,1)S(1)} collective-permute-done((bf16[8,48,1536]{2,1,0:T(8,128)(2,1)S(1)}, bf16[8,48,1536]{2,1,0:T(8,128)(2,1)S(1)}, u32[]{:S(2)}, u32[]{:S(2)}) %collective-permute-start.18) | collective-permute-done | bytes 1179680 | tf_op jit(solution)/shard_map/ppermute | solution.py:219
  239.4 3.7 collective-permute-done.17
  285.1 26.5 %all_to_all.116 = bf16[16,32,768]{2,1,0:T(8,128)(2,1)} all-to-all(bf16[16,32,768]{2,1,0:T(8,128)(2,1)S(1)} %broadcast_in_dim.142), channel_id=1, replica_groups=mesh['dp'=16,'tensor'=2] {'dp'}, dimensions={0} | all-to-all | bytes 1572864 | tf_op jit(solution)/shard_map/all_to_all | solution.py:45
  314.3 5.4 fusion.314
  328.6 7.8 %all-to-all-done.7 = f32[32,2,1024]{2,1,0:T(2,128)S(1)} async-done(((f32[32,2,1024]{2,1,0:T(2,128)}), f32[32,2,1024]{2,1,0:T(2,128)S(1)}, u32[]{:S(2)}, u32[]{:S(2)}) %all-to-all-start.7) | async-done | bytes 262176 | tf_op jit(solution)/shard_map/all_to_all | solution.py:45
  336.8 6.5 fusion.277
  348.4 4.4 all-to-all-start.8
  355.1 17.7 %all-to-all-done.8 = bf16[16,32,768]{2,1,0:T(8,128)(2,1)} async-done(((bf16[16,32,768]{2,1,0:T(8,128)(2,1)}), bf16[16,32,768]{2,1,0:T(8,128)(2,1)}, u32[]{:S(2)}, u32[]{:S(2)}) %all-to-all-start.8) | async-done | bytes 786464 | tf_op jit(solution)/shard_map/all_to_all | solution.py:608
  377.6 3.1 add_convert_fusion.3
  385.4 2.6 pad_maximum_fusion
  391.7 3.2 shard_map.463
  427.3 3.2 shard_map.465
  451.8 7.1 %shard_map.464 = (bf16[512,768]{1,0:T(8,128)(2,1)S(1)}, bf16[512,384]{1,0:T(8,128)(2,1)S(1)}) custom-call(bf16[512,768]{1,0:T(8,128)(2,1)S(1)} %copy-done.3, bf16[512,384]{1,0:T(8,128)(2,1)S(1)} %convolution_convert_fusion.20.refs_1_, bf16[512,384]{1,0:T(8,128)(2,1)S(1)} %convolution_convert_fusion.19.refs_2_, f32[512,1]{1,0:T(8,128)S(1)} %convert_element_type.641.refs_3_), custom_call_target="tpu_custom_call" | custom-call | flops 4026531840 | bytes 3149824 | tf_op jit(solution)/shard_map/pallas_call | solution.py:104
  470.5 3.1 fusion.54
  478.1 4.1 all-to-all-start.9
  500.6 18.7 %collective-permute-done.40 = bf16[4,1,48,2304]{3,2,0,1:T(8,128)(2,1)} collective-permute-done((bf16[4,1,48,2304]{3,2,0,1:T(8,128)(2,1)}, bf16[4,1,48,2304]{3,2,0,1:T(8,128)(2,1)}, u32[]{:S(2)}, u32[]{:S(2)}) %collective-permute-start.40) | collective-permute-done | bytes 884768 | tf_op jit(solution)/shard_map/ppermute | solution.py:219
  521.1 2.7 collective-permute-done.41
  527.4 5.1 all-to-all-done.9
  532.4 11.6 %collective-permute-done.46 = bf16[8,1,48,384]{3,2,0,1:T(8,128)(2,1)} collective-permute-done((bf16[8,1,48,384]{3,2,0,1:T(8,128)(2,1)S(1)}, bf16[8,1,48,384]{3,2,0,1:T(8,128)(2,1)}, u32[]{:S(2)}, u32[]{:S(2)}) %collective-permute-start.46) | collective-permute-done | bytes 294944 | tf_op jit(solution)/shard_map/ppermute | solution.py:219
  566.1 5.2 fusion.34
  571.4 8.2 %convolution_add_fusion = f32[1572,768]{1,0:T(8,128)} fusion(f32[1572,768]{1,0:T(8,128)S(1)} %fusion.34, bf16[512,768]{1,0:T(8,128)(2,1)} %collective-permute-done.25, bf16[512,768]{1,0:T(8,128)(2,1)} %bitcast.95, pred[]{:T(512)S(6)} %eq.398, f32[1024,1572]{0,1:T(8,128)S(1)} %bitcast.613, f32[1024]{0:T(1024)S(1)} %copy-done.209, f32[1024]{0:T(1024)S(1)} %copy-done.211, ...), kind=kOutput, calls=%fused_computation.86 | convolution fusion | flops 2490485760 | bytes 17682432 | tf_op jit(solution)/shard_map/dot_general | solution.py:55
  586.3 2.7 collective-permute-start.52
  600.3 10.9 %collective-permute-done.53 = bf16[1,1,48,2304]{3,2,1,0:T(8,128)(2,1)} collective-permute-done((bf16[1,1,48,2304]{3,2,1,0:T(8,128)(2,1)}, bf16[1,1,48,2304]{3,2,1,0:T(8,128)(2,1)}, u32[]{:S(2)}, u32[]{:S(2)}) %collective-permute-start.53) | collective-permute-done | bytes 221216 | tf_op jit(solution)/shard_map/ppermute | solution.py:219
  611.2 6.3 collective-permute-done.54
  630.1 3.8 collective-permute-done.57
  642.0 4.0 all-to-all-start.11
  648.0 5.3 all-to-all-done.11
  654.9 3.0 multiply_subtract_fusion.1
  658.9 3.4 multiply_subtract_fusion.3
  662.3 2.7 multiply_subtract_fusion.2
  665.2 9.0 %multiply_subtract_fusion = (f32[1572,768]{1,0:T(8,128)}, f32[1572,768]{1,0:T(8,128)}, f32[1572,768]{1,0:T(8,128)}) fusion(f32[1572,768]{1,0:T(8,128)S(1)} %bitcast.592, f32[]{:T(128)} %bitcast.210, f32[]{:T(128)} %bitcast.209, f32[1572,768]{1,0:T(8,128)S(1)} %bitcast.596, f32[]{:T(128)S(6)} %min.3, f32[1572,768]{1,0:T(8,128)} %param.58, f32[1572,768]{1,0:T(8,128)} %param.57), kind=kLoop, calls=%fused_computation.73 | loop fusion | flops 19316736 | bytes 33804300 | tf_op jit(solution)/shard_map/sub | solution.py:201
  (987 shorter events, 284.4 us)
Async XLA Ops:
  7.2 134.4 %all-gather.3.cloned.1.call-start = ((), (), s32[]{:S(2)}) async-start(), calls=%async_computation.13 | async-start | bytes 5013504 | tf_op jit(solution)/shard_map/all_gather | solution.py:416
  11.8 23.4 %collective-permute-start = (bf16[1,48,768]{2,1,0:T(8,128)(2,1)}, bf16[1,48,768]{2,1,0:T(8,128)(2,1)}, u32[]{:S(2)}, u32[]{:S(2)}) collective-permute-start(bf16[1,48,768]{2,1,0:T(8,128)(2,1)} %get-tuple-element.907), channel_id=1, source_target_pairs={{0,16},{2,18},{4,20},{6,22},{8,24},{10,26},{12,28},{14,30},{16,0},... | collective-permute-start | bytes 221192 | tf_op jit(solution)/shard_map/ppermute | solution.py:219
  17.2 18.0 %collective-permute-start.1 = (bf16[1,48,1024]{2,1,0:T(8,128)(2,1)}, bf16[1,48,1024]{2,1,0:T(8,128)(2,1)S(1)}, u32[]{:S(2)}, u32[]{:S(2)}) collective-permute-start(bf16[1,48,1024]{2,1,0:T(8,128)(2,1)} %get-tuple-element.905), channel_id=1, source_target_pairs={{0,8},{2,10},{4,12},{6,14},{8,0},{10,2},{12,4},{14,6},{16,24},{18,... | collective-permute-start | bytes 294920 | tf_op jit(solution)/shard_map/ppermute | solution.py:219
  25.1 10.2 %all-to-all-start.4 = ((s32[32,1,129]{2,1,0:T(1,128)}), s32[32,1,129]{2,1,0:T(1,128)S(1)}, u32[]{:S(2)}, u32[]{:S(2)}) async-start(s32[32,1,129]{2,1,0:T(1,128)} %all_to_all.73), calls=%async_computation.4 | async-start | bytes 65536 | tf_op jit(solution)/shard_map/all_to_all | solution.py:456
  38.5 20.9 %collective-permute-start.3 = (bf16[2,48,1024]{2,1,0:T(8,128)(2,1)S(1)}, bf16[2,48,1024]{2,1,0:T(8,128)(2,1)}, u32[]{:S(2)}, u32[]{:S(2)}) collective-permute-start(bf16[2,48,1024]{2,1,0:T(8,128)(2,1)S(1)} %get-tuple-element.899), channel_id=1, source_target_pairs={{0,16},{2,18},{4,20},{6,22},{8,24},{10,26},{12,28},{14,30},{16,0},... | collective-permute-start | bytes 589832 | tf_op jit(solution)/shard_map/ppermute | solution.py:219
  59.5 73.6 %all-to-all-start.5 = ((bf16[32,32,768]{2,1,0:T(8,128)(2,1)}), bf16[32,32,768]{2,1,0:T(8,128)(2,1)}, u32[]{:S(2)}, u32[]{:S(2)}) async-start(bf16[32,32,768]{2,1,0:T(8,128)(2,1)} %bitcast.665), calls=%async_computation.5 | async-start | bytes 3145728 | tf_op jit(solution)/shard_map/all_to_all | solution.py:470
  63.0 206.1 %all-gather.5.cloned.1.call-start = ((), (), s32[]{:S(2)}) async-start(), calls=%async_computation.14 | async-start | bytes 5013504 | tf_op jit(solution)/shard_map/all_gather | solution.py:416
  68.7 29.5 %collective-permute-start.5 = (bf16[4,48,1024]{2,1,0:T(8,128)(2,1)S(1)}, bf16[4,48,1024]{2,1,0:T(8,128)(2,1)S(1)}, u32[]{:S(2)}, u32[]{:S(2)}) collective-permute-start(bf16[4,48,1024]{2,1,0:T(8,128)(2,1)S(1)} %bitcast.669), channel_id=1, source_target_pairs={{0,2},{2,0},{4,6},{6,4},{8,10},{10,8},{12,14},{14,12},{16,18},{18,... | collective-permute-start | bytes 1179656 | tf_op jit(solution)/shard_map/ppermute | solution.py:219
  70.4 21.0 %collective-permute-start.4 = (bf16[4,48,768]{2,1,0:T(8,128)(2,1)S(1)}, bf16[4,48,768]{2,1,0:T(8,128)(2,1)S(1)}, u32[]{:S(2)}, u32[]{:S(2)}) collective-permute-start(bf16[4,48,768]{2,1,0:T(8,128)(2,1)S(1)} %bitcast.683), channel_id=1, source_target_pairs={{0,4},{2,6},{4,0},{6,2},{8,12},{10,14},{12,8},{14,10},{16,20},{18,... | collective-permute-start | bytes 884744 | tf_op jit(solution)/shard_map/ppermute | solution.py:219
  98.4 34.6 %collective-permute-start.7 = (bf16[8,48,1024]{2,1,0:T(8,128)(2,1)S(1)}, bf16[8,48,1024]{2,1,0:T(8,128)(2,1)}, u32[]{:S(2)}, u32[]{:S(2)}) collective-permute-start(bf16[8,48,1024]{2,1,0:T(8,128)(2,1)S(1)} %bitcast.693), channel_id=1, source_target_pairs={{0,4},{2,6},{4,0},{6,2},{8,12},{10,14},{12,8},{14,10},{16,20},{18,... | collective-permute-start | bytes 2359304 | tf_op jit(solution)/shard_map/ppermute | solution.py:219
  100.1 32.9 %collective-permute-start.6 = (bf16[8,48,768]{2,1,0:T(8,128)(2,1)S(1)}, bf16[8,48,768]{2,1,0:T(8,128)(2,1)S(1)}, u32[]{:S(2)}, u32[]{:S(2)}) collective-permute-start(bf16[8,48,768]{2,1,0:T(8,128)(2,1)S(1)} %bitcast.648), channel_id=1, source_target_pairs={{0,2},{2,0},{4,6},{6,4},{8,10},{10,8},{12,14},{14,12},{16,18},{18,... | collective-permute-start | bytes 1769480 | tf_op jit(solution)/shard_map/ppermute | solution.py:219
  102.8 30.2 %collective-permute-start.8 = (bf16[1,48,1792]{2,1,0:T(8,128)(2,1)}, bf16[1,48,1792]{2,1,0:T(8,128)(2,1)S(1)}, u32[]{:S(2)}, u32[]{:S(2)}) collective-permute-start(bf16[1,48,1792]{2,1,0:T(8,128)(2,1)} %bitcast.34), channel_id=1, source_target_pairs={{0,16},{2,18},{4,20},{6,22},{8,24},{10,26},{12,28},{14,30},{16,0},... | collective-permute-start | bytes 516104 | tf_op jit(solution)/shard_map/ppermute | solution.py:219
  103.1 12.0 %collective-permute-start.9 = (bf16[1,48,1536]{2,1,0:T(8,128)(2,1)S(1)}, bf16[1,48,1536]{2,1,0:T(8,128)(2,1)S(1)}, u32[]{:S(2)}, u32[]{:S(2)}) collective-permute-start(bf16[1,48,1536]{2,1,0:T(8,128)(2,1)S(1)} %maximum_bitcast_fusion.3), channel_id=1, source_target_pairs={{0,8},{2,10},{4,12},{6,14},{8,0},{10,2},{12,4},{14,6},{16,24},{18,... | collective-permute-start | bytes 442376 | tf_op jit(solution)/shard_map/ppermute | solution.py:219
  137.9 22.5 %collective-permute-start.10 = (bf16[2,48,1792]{2,1,0:T(8,128)(2,1)}, bf16[2,48,1792]{2,1,0:T(8,128)(2,1)}, u32[]{:S(2)}, u32[]{:S(2)}) collective-permute-start(bf16[2,48,1792]{2,1,0:T(8,128)(2,1)} %get-tuple-element.884), channel_id=1, source_target_pairs={{0,8},{2,10},{4,12},{6,14},{8,0},{10,2},{12,4},{14,6},{16,24},{18,... | collective-permute-start | bytes 1032200 | tf_op jit(solution)/shard_map/ppermute | solution.py:219
  138.7 21.7 %collective-permute-start.11 = (bf16[2,48,1536]{2,1,0:T(8,128)(2,1)}, bf16[2,48,1536]{2,1,0:T(8,128)(2,1)}, u32[]{:S(2)}, u32[]{:S(2)}) collective-permute-start(bf16[2,48,1536]{2,1,0:T(8,128)(2,1)} %get-tuple-element.896), channel_id=1, source_target_pairs={{0,16},{2,18},{4,20},{6,22},{8,24},{10,26},{12,28},{14,30},{16,0},... | collective-permute-start | bytes 884744 | tf_op jit(solution)/shard_map/ppermute | solution.py:219
  161.5 25.7 %collective-permute-start.13 = (bf16[4,48,1792]{2,1,0:T(8,128)(2,1)S(1)}, bf16[4,48,1792]{2,1,0:T(8,128)(2,1)S(1)}, u32[]{:S(2)}, u32[]{:S(2)}) collective-permute-start(bf16[4,48,1792]{2,1,0:T(8,128)(2,1)S(1)} %bitcast.640), channel_id=1, source_target_pairs={{0,4},{2,6},{4,0},{6,2},{8,12},{10,14},{12,8},{14,10},{16,20},{18,... | collective-permute-start | bytes 2064392 | tf_op jit(solution)/shard_map/ppermute | solution.py:219
  164.2 23.1 %collective-permute-start.14 = (bf16[4,48,1536]{2,1,0:T(8,128)(2,1)S(1)}, bf16[4,48,1536]{2,1,0:T(8,128)(2,1)S(1)}, u32[]{:S(2)}, u32[]{:S(2)}) collective-permute-start(bf16[4,48,1536]{2,1,0:T(8,128)(2,1)S(1)} %bitcast.642), channel_id=1, source_target_pairs={{0,2},{2,0},{4,6},{6,4},{8,10},{10,8},{12,14},{14,12},{16,18},{18,... | collective-permute-start | bytes 1769480 | tf_op jit(solution)/shard_map/ppermute | solution.py:219
  193.9 49.2 %collective-permute-start.17 = (bf16[8,48,1792]{2,1,0:T(8,128)(2,1)S(1)}, bf16[8,48,1792]{2,1,0:T(8,128)(2,1)S(1)}, u32[]{:S(2)}, u32[]{:S(2)}) collective-permute-start(bf16[8,48,1792]{2,1,0:T(8,128)(2,1)S(1)} %bitcast.619), channel_id=1, source_target_pairs={{0,2},{2,0},{4,6},{6,4},{8,10},{10,8},{12,14},{14,12},{16,18},{18,... | collective-permute-start | bytes 4128776 | tf_op jit(solution)/shard_map/ppermute | solution.py:219
  195.5 44.0 %collective-permute-start.18 = (bf16[8,48,1536]{2,1,0:T(8,128)(2,1)S(1)}, bf16[8,48,1536]{2,1,0:T(8,128)(2,1)S(1)}, u32[]{:S(2)}, u32[]{:S(2)}) collective-permute-start(bf16[8,48,1536]{2,1,0:T(8,128)(2,1)S(1)} %bitcast.674), channel_id=1, source_target_pairs={{0,4},{2,6},{4,0},{6,2},{8,12},{10,14},{12,8},{14,10},{16,20},{18,... | collective-permute-start | bytes 3538952 | tf_op jit(solution)/shard_map/ppermute | solution.py:219
  323.3 13.2 %all-to-all-start.7 = ((f32[32,2,1024]{2,1,0:T(2,128)}), f32[32,2,1024]{2,1,0:T(2,128)S(1)}, u32[]{:S(2)}, u32[]{:S(2)}) async-start(f32[32,2,1024]{2,1,0:T(2,128)} %broadcast_in_dim.144), calls=%async_computation.7 | async-start | bytes 524288 | tf_op jit(solution)/shard_map/all_to_all | solution.py:45
  348.4 24.5 %all-to-all-start.8 = ((bf16[16,32,768]{2,1,0:T(8,128)(2,1)}), bf16[16,32,768]{2,1,0:T(8,128)(2,1)}, u32[]{:S(2)}, u32[]{:S(2)}) async-start(bf16[16,32,768]{2,1,0:T(8,128)(2,1)} %bitcast.639), calls=%async_computation.8 | async-start | bytes 1572864 | tf_op jit(solution)/shard_map/all_to_all | solution.py:608
  352.8 211.4 %reduce-scatter.2.cloned.1.call-start = ((), (), s32[]{:S(2)}) async-start(), calls=%async_computation.15 | async-start | bytes 5013504 | tf_op jit(solution)/shard_map/reduce_scatter | solution.py:622
  405.1 54.4 %collective-permute-start.33 = (bf16[8,1,48,768]{3,2,0,1:T(8,128)(2,1)}, bf16[8,1,48,768]{3,2,0,1:T(8,128)(2,1)}, u32[]{:S(2)}, u32[]{:S(2)}) collective-permute-start(bf16[8,1,48,768]{3,2,0,1:T(8,128)(2,1)} %slice_bitcast_fusion.16), channel_id=1, source_target_pairs={{0,2},{2,0},{4,6},{6,4},{8,10},{10,8},{12,14},{14,12},{16,18},{18,... | collective-permute-start | bytes 1769480 | tf_op jit(solution)/shard_map/ppermute | solution.py:219
  409.6 51.1 %collective-permute-start.34 = (bf16[4,2,48,768]{3,2,1,0:T(8,128)(2,1)}, bf16[4,2,48,768]{3,2,1,0:T(8,128)(2,1)}, u32[]{:S(2)}, u32[]{:S(2)}) collective-permute-start(bf16[4,2,48,768]{3,2,1,0:T(8,128)(2,1)} %slice_bitcast_fusion.15), channel_id=1, source_target_pairs={{0,4},{2,6},{4,0},{6,2},{8,12},{10,14},{12,8},{14,10},{16,20},{18,... | collective-permute-start | bytes 1769480 | tf_op jit(solution)/shard_map/ppermute | solution.py:219
  417.8 25.7 %collective-permute-start.31 = (f32[256,768]{1,0:T(8,128)}, f32[256,768]{1,0:T(8,128)}, u32[]{:S(2)}, u32[]{:S(2)}) collective-permute-start(f32[256,768]{1,0:T(8,128)} %slice.519), channel_id=1, source_target_pairs={{0,1},{1,0},{2,3},{3,2},{4,5},{5,4},{6,7},{7,6},{8,9},{9,8},{10,11... | collective-permute-start | bytes 2359304 | tf_op jit(solution)/shard_map/ppermute | solution.py:31
  420.6 40.2 %collective-permute-start.35 = (bf16[8,1,48,1536]{3,2,0,1:T(8,128)(2,1)}, bf16[8,1,48,1536]{3,2,0,1:T(8,128)(2,1)}, u32[]{:S(2)}, u32[]{:S(2)}) collective-permute-start(bf16[8,1,48,1536]{3,2,0,1:T(8,128)(2,1)} %slice_bitcast_fusion.4), channel_id=1, source_target_pairs={{0,2},{2,0},{4,6},{6,4},{8,10},{10,8},{12,14},{14,12},{16,18},{18,... | collective-permute-start | bytes 3538952 | tf_op jit(solution)/shard_map/ppermute | solution.py:219
  424.7 36.0 %collective-permute-start.36 = (bf16[4,2,48,1536]{3,2,1,0:T(8,128)(2,1)}, bf16[4,2,48,1536]{3,2,1,0:T(8,128)(2,1)}, u32[]{:S(2)}, u32[]{:S(2)}) collective-permute-start(bf16[4,2,48,1536]{3,2,1,0:T(8,128)(2,1)} %slice_bitcast_fusion.3), channel_id=1, source_target_pairs={{0,4},{2,6},{4,0},{6,2},{8,12},{10,14},{12,8},{14,10},{16,20},{18,... | collective-permute-start | bytes 3538952 | tf_op jit(solution)/shard_map/ppermute | solution.py:219
  450.4 48.9 %collective-permute-start.42 = (bf16[8,1,48,768]{3,2,0,1:T(8,128)(2,1)}, bf16[8,1,48,768]{3,2,0,1:T(8,128)(2,1)}, u32[]{:S(2)}, u32[]{:S(2)}) collective-permute-start(bf16[8,1,48,768]{3,2,0,1:T(8,128)(2,1)} %slice_bitcast_fusion.12), channel_id=1, source_target_pairs={{0,2},{2,0},{4,6},{6,4},{8,10},{10,8},{12,14},{14,12},{16,18},{18,... | collective-permute-start | bytes 1769480 | tf_op jit(solution)/shard_map/ppermute | solution.py:219
  459.5 73.0 %collective-permute-start.43 = (bf16[4,2,48,768]{3,2,1,0:T(8,128)(2,1)}, bf16[4,2,48,768]{3,2,1,0:T(8,128)(2,1)}, u32[]{:S(2)}, u32[]{:S(2)}) collective-permute-start(bf16[4,2,48,768]{3,2,1,0:T(8,128)(2,1)} %slice_bitcast_fusion.11), channel_id=1, source_target_pairs={{0,4},{2,6},{4,0},{6,2},{8,12},{10,14},{12,8},{14,10},{16,20},{18,... | collective-permute-start | bytes 1769480 | tf_op jit(solution)/shard_map/ppermute | solution.py:219
  461.6 11.9 %collective-permute-start.37 = (f32[256,768]{1,0:T(8,128)S(1)}, f32[256,768]{1,0:T(8,128)S(1)}, u32[]{:S(2)}, u32[]{:S(2)}) collective-permute-start(f32[256,768]{1,0:T(8,128)S(1)} %slice.652), channel_id=1, source_target_pairs={{0,1},{1,0},{2,3},{3,2},{4,5},{5,4},{6,7},{7,6},{8,9},{9,8},{10,11... | collective-permute-start | bytes 2359304 | tf_op jit(solution)/shard_map/ppermute | solution.py:31
  466.9 52.3 %collective-permute-start.40 = (bf16[4,1,48,2304]{3,2,0,1:T(8,128)(2,1)}, bf16[4,1,48,2304]{3,2,0,1:T(8,128)(2,1)}, u32[]{:S(2)}, u32[]{:S(2)}) collective-permute-start(bf16[4,1,48,2304]{3,2,0,1:T(8,128)(2,1)} %fusion.121), channel_id=1, source_target_pairs={{0,4},{2,6},{4,0},{6,2},{8,12},{10,14},{12,8},{14,10},{16,20},{18,... | collective-permute-start | bytes 2654216 | tf_op jit(solution)/shard_map/ppermute | solution.py:219
  478.1 54.4 %all-to-all-start.9 = ((bf16[32,32,768]{2,1,0:T(8,128)(2,1)}), bf16[32,32,768]{2,1,0:T(8,128)(2,1)}, u32[]{:S(2)}, u32[]{:S(2)}) async-start(bf16[32,32,768]{2,1,0:T(8,128)(2,1)} %bitcast.666), calls=%async_computation.9 | async-start | bytes 3145728 | tf_op jit(solution)/shard_map/all_to_all | solution.py:470
  485.5 38.3 %collective-permute-start.41 = (bf16[4,1,48,2304]{3,2,0,1:T(8,128)(2,1)}, bf16[4,1,48,2304]{3,2,0,1:T(8,128)(2,1)}, u32[]{:S(2)}, u32[]{:S(2)}) collective-permute-start(bf16[4,1,48,2304]{3,2,0,1:T(8,128)(2,1)} %fusion.122), channel_id=1, source_target_pairs={{0,2},{2,0},{4,6},{6,4},{8,10},{10,8},{12,14},{14,12},{16,18},{18,... | collective-permute-start | bytes 2654216 | tf_op jit(solution)/shard_map/ppermute | solution.py:219
  495.1 49.0 %collective-permute-start.45 = (bf16[4,2,48,768]{3,2,1,0:T(8,128)(2,1)}, bf16[4,2,48,768]{3,2,1,0:T(8,128)(2,1)}, u32[]{:S(2)}, u32[]{:S(2)}) collective-permute-start(bf16[4,2,48,768]{3,2,1,0:T(8,128)(2,1)} %slice_bitcast_fusion.10), channel_id=1, source_target_pairs={{0,4},{2,6},{4,0},{6,2},{8,12},{10,14},{12,8},{14,10},{16,20},{18,... | collective-permute-start | bytes 1769480 | tf_op jit(solution)/shard_map/ppermute | solution.py:219
  499.3 44.7 %collective-permute-start.44 = (bf16[8,1,48,640]{3,2,0,1:T(8,128)(2,1)}, bf16[8,1,48,640]{3,2,0,1:T(8,128)(2,1)S(1)}, u32[]{:S(2)}, u32[]{:S(2)}) collective-permute-start(bf16[8,1,48,640]{3,2,0,1:T(8,128)(2,1)} %slice_bitcast_fusion.18), channel_id=1, source_target_pairs={{0,2},{2,0},{4,6},{6,4},{8,10},{10,8},{12,14},{14,12},{16,18},{18,... | collective-permute-start | bytes 1474568 | tf_op jit(solution)/shard_map/ppermute | solution.py:219
  519.2 24.8 %collective-permute-start.46 = (bf16[8,1,48,384]{3,2,0,1:T(8,128)(2,1)S(1)}, bf16[8,1,48,384]{3,2,0,1:T(8,128)(2,1)}, u32[]{:S(2)}, u32[]{:S(2)}) collective-permute-start(bf16[8,1,48,384]{3,2,0,1:T(8,128)(2,1)S(1)} %slice_bitcast_fusion.26), channel_id=1, source_target_pairs={{0,2},{2,0},{4,6},{6,4},{8,10},{10,8},{12,14},{14,12},{16,18},{18,... | collective-permute-start | bytes 884744 | tf_op jit(solution)/shard_map/ppermute | solution.py:219
  523.8 20.2 %collective-permute-start.47 = (bf16[4,2,48,256]{3,2,1,0:T(8,128)(2,1)}, bf16[4,2,48,256]{3,2,1,0:T(8,128)(2,1)}, u32[]{:S(2)}, u32[]{:S(2)}) collective-permute-start(bf16[4,2,48,256]{3,2,1,0:T(8,128)(2,1)} %slice_bitcast_fusion.28), channel_id=1, source_target_pairs={{0,4},{2,6},{4,0},{6,2},{8,12},{10,14},{12,8},{14,10},{16,20},{18,... | collective-permute-start | bytes 589832 | tf_op jit(solution)/shard_map/ppermute | solution.py:219
  546.4 33.1 %collective-permute-start.48 = (bf16[2,1,48,2304]{3,2,0,1:T(8,128)(2,1)}, bf16[2,1,48,2304]{3,2,0,1:T(8,128)(2,1)}, u32[]{:S(2)}, u32[]{:S(2)}) collective-permute-start(bf16[2,1,48,2304]{3,2,0,1:T(8,128)(2,1)} %fusion.164), channel_id=1, source_target_pairs={{0,8},{2,10},{4,12},{6,14},{8,0},{10,2},{12,4},{14,6},{16,24},{18,... | collective-permute-start | bytes 1327112 | tf_op jit(solution)/shard_map/ppermute | solution.py:219
  550.2 29.4 %collective-permute-start.49 = (bf16[1,2,48,2304]{3,2,1,0:T(8,128)(2,1)}, bf16[1,2,48,2304]{3,2,1,0:T(8,128)(2,1)}, u32[]{:S(2)}, u32[]{:S(2)}) collective-permute-start(bf16[1,2,48,2304]{3,2,1,0:T(8,128)(2,1)} %fusion.163), channel_id=1, source_target_pairs={{0,16},{2,18},{4,20},{6,22},{8,24},{10,26},{12,28},{14,30},{16,0},... | collective-permute-start | bytes 1327112 | tf_op jit(solution)/shard_map/ppermute | solution.py:219
  556.1 23.4 %collective-permute-start.50 = (bf16[4,1,48,1792]{3,2,0,1:T(8,128)(2,1)}, bf16[4,1,48,1792]{3,2,0,1:T(8,128)(2,1)S(1)}, u32[]{:S(2)}, u32[]{:S(2)}) collective-permute-start(bf16[4,1,48,1792]{3,2,0,1:T(8,128)(2,1)} %fusion.134), channel_id=1, source_target_pairs={{0,4},{2,6},{4,0},{6,2},{8,12},{10,14},{12,8},{14,10},{16,20},{18,... | collective-permute-start | bytes 2064392 | tf_op jit(solution)/shard_map/ppermute | solution.py:219
  563.7 16.9 %collective-permute-start.51 = (bf16[4,1,48,1792]{3,2,0,1:T(8,128)(2,1)}, bf16[4,1,48,1792]{3,2,0,1:T(8,128)(2,1)}, u32[]{:S(2)}, u32[]{:S(2)}) collective-permute-start(bf16[4,1,48,1792]{3,2,0,1:T(8,128)(2,1)} %fusion.135), channel_id=1, source_target_pairs={{0,2},{2,0},{4,6},{6,4},{8,10},{10,8},{12,14},{14,12},{16,18},{18,... | collective-permute-start | bytes 2064392 | tf_op jit(solution)/shard_map/ppermute | solution.py:219
  582.4 17.3 %all-to-all-start.10 = ((f32[32,1,168]{2,1,0:T(1,128)}), f32[32,1,168]{2,1,0:T(1,128)S(1)}, u32[]{:S(2)}, u32[]{:S(2)}) async-start(f32[32,1,168]{2,1,0:T(1,128)} %all_to_all.91), calls=%async_computation.11 | async-start | bytes 65536 | tf_op jit(solution)/shard_map/all_to_all | solution.py:737
  586.3 14.0 %collective-permute-start.52 = (bf16[1,1,48,2304]{3,2,1,0:T(8,128)(2,1)S(1)}, bf16[1,1,48,2304]{3,2,1,0:T(8,128)(2,1)}, u32[]{:S(2)}, u32[]{:S(2)}) collective-permute-start(bf16[1,1,48,2304]{3,2,1,0:T(8,128)(2,1)S(1)} %fusion.188), channel_id=1, source_target_pairs={{0,16},{2,18},{4,20},{6,22},{8,24},{10,26},{12,28},{14,30},{16,0},... | collective-permute-start | bytes 663560 | tf_op jit(solution)/shard_map/ppermute | solution.py:219
  591.5 19.7 %collective-permute-start.53 = (bf16[1,1,48,2304]{3,2,1,0:T(8,128)(2,1)}, bf16[1,1,48,2304]{3,2,1,0:T(8,128)(2,1)}, u32[]{:S(2)}, u32[]{:S(2)}) collective-permute-start(bf16[1,1,48,2304]{3,2,1,0:T(8,128)(2,1)} %fusion.189), channel_id=1, source_target_pairs={{0,8},{2,10},{4,12},{6,14},{8,0},{10,2},{12,4},{14,6},{16,24},{18,... | collective-permute-start | bytes 663560 | tf_op jit(solution)/shard_map/ppermute | solution.py:219
  593.9 23.5 %collective-permute-start.54 = (bf16[2,1,48,1792]{3,2,0,1:T(8,128)(2,1)}, bf16[2,1,48,1792]{3,2,0,1:T(8,128)(2,1)}, u32[]{:S(2)}, u32[]{:S(2)}) collective-permute-start(bf16[2,1,48,1792]{3,2,0,1:T(8,128)(2,1)} %fusion.179), channel_id=1, source_target_pairs={{0,8},{2,10},{4,12},{6,14},{8,0},{10,2},{12,4},{14,6},{16,24},{18,... | collective-permute-start | bytes 1032200 | tf_op jit(solution)/shard_map/ppermute | solution.py:219
  596.4 21.0 %collective-permute-start.55 = (bf16[1,2,48,1792]{3,2,1,0:T(8,128)(2,1)}, bf16[1,2,48,1792]{3,2,1,0:T(8,128)(2,1)}, u32[]{:S(2)}, u32[]{:S(2)}) collective-permute-start(bf16[1,2,48,1792]{3,2,1,0:T(8,128)(2,1)} %fusion.178), channel_id=1, source_target_pairs={{0,16},{2,18},{4,20},{6,22},{8,24},{10,26},{12,28},{14,30},{16,0},... | collective-permute-start | bytes 1032200 | tf_op jit(solution)/shard_map/ppermute | solution.py:219
  624.7 10.2 %collective-permute-start.56 = (bf16[1,1,48,1792]{3,2,1,0:T(8,128)(2,1)}, bf16[1,1,48,1792]{3,2,1,0:T(8,128)(2,1)}, u32[]{:S(2)}, u32[]{:S(2)}) collective-permute-start(bf16[1,1,48,1792]{3,2,1,0:T(8,128)(2,1)} %fusion.198), channel_id=1, source_target_pairs={{0,8},{2,10},{4,12},{6,14},{8,0},{10,2},{12,4},{14,6},{16,24},{18,... | collective-permute-start | bytes 516104 | tf_op jit(solution)/shard_map/ppermute | solution.py:219
  642.0 11.3 %all-to-all-start.11 = ((f32[32,1,169]{2,1,0:T(1,128)}), f32[32,1,169]{2,1,0:T(1,128)S(1)}, u32[]{:S(2)}, u32[]{:S(2)}) async-start(f32[32,1,169]{2,1,0:T(1,128)} %broadcast_in_dim.274), calls=%async_computation.12 | async-start | bytes 65536 | tf_op jit(solution)/shard_map/all_to_all | solution.py:45
  (285 other events, 2092.5 us)
Sparse Core Ops, SparseCore 0:
  11.3 116.5 all-gather.2
  131.2 112.3 all-gather.4
  388.1 160.7 reduce-scatter.1
